TPU v7x, 512 devices: a whole 4x4x16 slice. The times are simulated.
512 devices in a mesh: video: 8 (over y, core), tm: 64 (over x, z).
Axes of the slice: x: 4, y: 4, z: 16, core: 2. Of those that a mesh axis runs over, the one named last changes fastest.
Arguments:
- tokens: bfloat16 [131072, 1152], P(('video', 'tm')), parts along dimension 0, may hold values from -1000 to 1000
- gain: bfloat16 [1152], replicated, may hold values from 0.099609375 to 1.8984375
- w_query: bfloat16 [1152, 640], P('tm'), may hold values from -0.5 to 0.5
- w_key: bfloat16 [1152, 640], P('tm'), may hold values from -0.5 to 0.5
- w_value: bfloat16 [1152, 640], P('tm'), may hold values from -0.1875 to 0.1875
- conv_weight: bfloat16 [27, 640], replicated, may hold values from -1.25 to 1.25
Outputs:
- mixed: float32 [131072, 640], P(('video', 'tm')), parts along dimension 0
There are 8 independent parts, one for each index of `video`. A program takes and returns all parts, laid end to end along the dimension named above; an argument that names none is the same for every part. Nothing has to cross between parts.
All inputs are finite; a program needn't handle non-finite values.
Results may differ from a plain program's by a relative error of at most 0.004.
Values may be sent and summed in bfloat16 or wider, within the bound.
No kernel may reach another device: no remote copies, remote signals or barrier semaphores. Data moves between devices by JAX's collectives and lax.ppermute only.
A program may use at most 64 MiB of HBM per device.

v0:
```python
import jax
import jax.numpy as jnp
from jax import lax
from jax.sharding import PartitionSpec as P

HEAD_WIDTH = 32
FH = 8
FW = 32


def extended(cells, sides, width):
    for axis, dim in sides:
        count = lax.axis_size(axis)
        ends = count - 1
        head = lax.slice_in_dim(cells, 0, width, axis=dim)
        tail = lax.slice_in_dim(cells, cells.shape[dim] - width, cells.shape[dim], axis=dim)
        cells = jnp.concatenate(
            [
                lax.ppermute(tail, axis, [(i, (i + 1) % count) for i in range(ends)]),
                cells,
                lax.ppermute(head, axis, [((i + 1) % count, i) for i in range(ends)]),
            ],
            axis=dim,
        )
    return cells


def body(tokens, gain, w_query, w_key, w_value, conv_weight):
    rows = tokens.shape[0]
    width = w_query.shape[1]
    head_split = width // HEAD_WIDTH
    xfloat = tokens.astype(jnp.float32)
    scale = lax.rsqrt(jnp.mean(xfloat * xfloat, axis=1, keepdims=True) + 1e-06)
    normed = (xfloat * scale * gain.astype(jnp.float32)).astype(jnp.bfloat16)
    query = jnp.dot(
        normed,
        lax.all_gather(w_query, "tm", axis=0, tiled=True),
        preferred_element_type=jnp.float32,
    )
    keys = jnp.dot(
        normed, lax.all_gather(w_key, "tm", axis=0, tiled=True), preferred_element_type=jnp.float32
    )
    values = jnp.dot(
        normed,
        lax.all_gather(w_value, "tm", axis=0, tiled=True),
        preferred_element_type=jnp.float32,
    )
    values = values.astype(jnp.bfloat16)
    framed = extended(values.reshape(1, FH, FW, width), (("tm", 0),), 1)
    qfeat = (jax.nn.elu(query) + 1.0).astype(jnp.bfloat16)
    kfeat = (jax.nn.elu(keys) + 1.0).astype(jnp.bfloat16)
    key_value_state = jnp.einsum(
        "gin,gil->inl",
        kfeat.reshape(rows, head_split, HEAD_WIDTH),
        values.reshape(rows, head_split, HEAD_WIDTH),
        preferred_element_type=jnp.float32,
    ).reshape(width, HEAD_WIDTH)
    ksum = jnp.sum(kfeat, axis=0, dtype=jnp.float32)
    padded = jnp.pad(framed, ((0, 0), (1, 1), (1, 1), (0, 0)))
    kernel = conv_weight.astype(jnp.float32)
    local = jnp.zeros((FH, FW, width), jnp.float32)
    for shift_t in range(3):
        for shift_y in range(3):
            for shift_x in range(3):
                window = padded[shift_t, shift_y : shift_y + FH, shift_x : shift_x + FW, :]
                local = (
                    local + window.astype(jnp.float32) * kernel[9 * shift_t + 3 * shift_y + shift_x]
                )
    key_value_state, ksum = lax.psum((key_value_state, ksum), "tm")
    query_heads = qfeat.astype(jnp.float32).reshape(rows, head_split, HEAD_WIDTH)
    numerator = jnp.einsum(
        "dnb,nbt->dnt",
        query_heads,
        key_value_state.reshape(head_split, HEAD_WIDTH, HEAD_WIDTH),
        precision=lax.Precision.HIGHEST,
    )
    denom = jnp.einsum(
        "rhk,hk->rh",
        query_heads,
        ksum.reshape(head_split, HEAD_WIDTH),
        precision=lax.Precision.HIGHEST,
    )
    attended = (numerator / denom[:, :, None]).reshape(rows, width)
    return attended + local.reshape(rows, width)


def solution(mesh):
    in_specs = (P(("video", "tm"), None), P(), P("tm", None), P("tm", None), P("tm", None), P())
    out_specs = P(("video", "tm"), None)
    return jax.shard_map(body, mesh=mesh, in_specs=in_specs, out_specs=out_specs, check_vma=False)
```

profile of v0, /device:TPU:8, one launch (start us, length us, event | category | flops | bytes accessed | tf_op | source)
XLA Modules:
  0.0 729.6 jit_solution(11153499234140848705)
XLA Ops:
  6.5 0.7 all-gather.9.cloned.1.call-update
  7.3 0.7 all-gather.7.cloned.1.call-update
  8.1 0.7 all-gather.11.cloned.1.call-update
  8.8 0.7 convert_element_type.214
  9.5 0.8 convert_element_type.222
  10.3 0.1 slice_reduce_fusion.25
  10.3 0.1 slice_reduce_fusion.26
  10.5 1.3 fusion.7
  11.7 143.9 %all-gather.9.cloned.1.call-done = bf16[64,18,640]{2,1,0:T(8,128)(2,1)} async-done(((bf16[1,18,640]{2,1,0:T(8,128)(2,1)}), bf16[64,18,640]{2,1,0:T(8,128)(2,1)}) %all-gather.9.cloned.1.call-update) | async-done | bytes 1474576 | tf_op jit(solution)/shard_map/all_gather | solution.py:45
  155.7 2.5 reshape.180
  158.2 0.7 convolution_convert_fusion
  158.9 0.2 copy.14
  159.1 1.3 collective-permute-start.1
  160.4 4.6 collective-permute-start
  165.0 130.3 %all-gather.7.cloned.1.call-done = bf16[64,18,640]{2,1,0:T(8,128)(2,1)} async-done(((bf16[1,18,640]{2,1,0:T(8,128)(2,1)}), bf16[64,18,640]{2,1,0:T(8,128)(2,1)}) %all-gather.7.cloned.1.call-update) | async-done | bytes 1474576 | tf_op jit(solution)/shard_map/all_gather | solution.py:41
  295.3 2.5 reshape.178
  297.8 1.6 convert_reduce_fusion
  299.4 1.1 copy.13
  300.5 0.9 fusion.56
  301.5 133.4 %all-gather.11.cloned.1.call-done = bf16[64,18,640]{2,1,0:T(8,128)(2,1)} async-done(((bf16[1,18,640]{2,1,0:T(8,128)(2,1)}), bf16[64,18,640]{2,1,0:T(8,128)(2,1)}) %all-gather.11.cloned.1.call-update) | async-done | bytes 1474576 | tf_op jit(solution)/shard_map/all_gather | solution.py:37
  434.9 2.5 reshape.182
  437.5 0.8 fusion.15
  438.3 0.2 copy.15
  438.5 0.1 reshape.147
  438.5 277.3 %psum.15 = f32[20,32]{1,0:T(8,128)S(1)} all-reduce(f32[20,32]{1,0:T(8,128)S(1)} %reshape.147), channel_id=1, replica_groups=mesh['video'=8,'tm'=64] {'tm'}, use_global_device_ids=true, to_apply=%region_3.4 | all-reduce | flops 640 | bytes 5120 | tf_op jit(solution)/shard_map/psum | solution.py:69
  715.8 0.3 fusion.43
  716.1 1.4 fusion.6
  717.6 0.2 copy.17
  717.8 0.5 select_maximum_fusion
  718.4 0.3 fusion.55
  718.7 0.9 fusion.54
  719.6 3.5 fusion.17
  (12 shorter events, 0.2 us)
Async XLA Ops:
  6.5 149.1 %all-gather.9.cloned.1.call-start = ((), (), s32[]{:S(2)}) async-start(), calls=%async_computation.2 | async-start | bytes 1996800 | tf_op jit(solution)/shard_map/all_gather | solution.py:45
  7.3 288.0 %all-gather.7.cloned.1.call-start = ((), (), s32[]{:S(2)}) async-start(), calls=%async_computation.1 | async-start | bytes 1996800 | tf_op jit(solution)/shard_map/all_gather | solution.py:41
  8.0 426.9 %all-gather.11.cloned.1.call-start = ((), (), s32[]{:S(2)}) async-start(), calls=%async_computation.3 | async-start | bytes 1996800 | tf_op jit(solution)/shard_map/all_gather | solution.py:37
  8.7 707.4 %all-reduce.3.cloned.1.call-start = ((), (), s32[]{:S(2)}) async-start(), calls=%async_computation | async-start | bytes 655360 | tf_op jit(solution)/shard_map/psum | solution.py:69
  11.7 146.5 %copy-start = (bf16[256,1152]{1,0:T(8,128)(2,1)S(1)}, bf16[256,1152]{1,0:T(8,128)(2,1)}, u32[]{:S(2)}) copy-start(bf16[256,1152]{1,0:T(8,128)(2,1)} %param.6) | copy-start | bytes 1769476
  159.1 558.7 %collective-permute-start.1 = (bf16[1,8,32,640]{3,2,1,0:T(8,128)(2,1)S(1)}, bf16[1,8,32,640]{3,2,1,0:T(8,128)(2,1)S(1)}, u32[]{:S(2)}, u32[]{:S(2)}) collective-permute-start(bf16[1,8,32,640]{3,2,1,0:T(8,128)(2,1)S(1)} %bitcast.104), channel_id=1, source_target_pairs={{1,0},{2,1},{3,2},{4,3},{5,4},{6,5},{7,6},{8,7},{9,8},{10,9},{11,1... | collective-permute-start | bytes 983048 | tf_op jit(solution)/shard_map/ppermute | solution.py:21
  160.4 557.4 %collective-permute-start = (bf16[1,8,32,640]{3,2,1,0:T(8,128)(2,1)S(1)}, bf16[1,8,32,640]{3,2,1,0:T(8,128)(2,1)S(1)}, u32[]{:S(2)}, u32[]{:S(2)}) collective-permute-start(bf16[1,8,32,640]{3,2,1,0:T(8,128)(2,1)S(1)} %bitcast.105), channel_id=1, source_target_pairs={{0,1},{1,2},{2,3},{3,4},{4,5},{5,6},{6,7},{7,8},{8,9},{9,10},{10,1... | collective-permute-start | bytes 983048 | tf_op jit(solution)/shard_map/ppermute | solution.py:19
Sparse Core Ops, SparseCore 0:
  10.3 145.3 all-gather.8
  158.6 136.6 all-gather.6
  298.3 136.6 all-gather.10
  438.2 258.3 all-reduce.2
where the time goes:
time: 730 us
  waiting for transfers between devices  410 us (56%)
  blocking collectives  277 us (38%)
  between operations  13.3 us (2%)
  local copies, waits for them, and re-layouts  10.8 us (1%)
    psum x1, blocking collectives, body(): key_value_state, ksum = lax.psum((key_value_state, ksum), 'tm')  277 us
    all_gather x1, waiting for transfers between devices, body(): lax.all_gather(w_value, 'tm', axis=0, tiled=True)  144 us
    all_gather x1, waiting for transfers between devices, body(): lax.all_gather(w_query, 'tm', axis=0, tiled=True)  133 us
    all_gather x1, waiting for transfers between devices, body(): lax.all_gather(w_key, 'tm', axis=0, tiled=True)  130 us
  transfers between devices with their start and end apart: 6, of which 3 were waited for; matrix products, arithmetic and copies ran while one was open for 2% of the time, Pallas kernels for 0%

commit v1 on v0

v1 whole, which is shorter than its diff:
```python
import jax
import jax.numpy as jnp
from jax import lax
from jax.sharding import Mesh
from jax.sharding import PartitionSpec as P

HEAD_WIDTH = 32
FH = 8
FW = 32
LANES = 128

AXES = ("y", "core", "x", "zh", "zl")
ZAX = ("zh", "zl")
TM = ("x", "zh", "zl")
NEAR = ("x", "zl")


def exchange(blocks, axes):
    return lax.all_to_all(blocks, axes, 0, 0, tiled=True)


def spread(block, axes):
    count = lax.axis_size(axes)
    return exchange(jnp.broadcast_to(block[None], (count,) + block.shape), axes)


def swap(block):
    return lax.ppermute(block, "core", [(0, 1), (1, 0)])


def gather_weights(w_query, w_key, w_value):
    rows = w_query.shape[0]
    pad = jnp.zeros((rows, LANES), w_query.dtype)
    first = jnp.concatenate([w_value, w_query[:, : 3 * LANES]], axis=1)
    second = jnp.concatenate([w_key, w_query[:, 3 * LANES :], pad], axis=1)
    core = lax.axis_index("core")
    mine = jnp.where(core == 0, first, second)
    mine = lax.dynamic_slice_in_dim(mine, lax.axis_index("y") * 2 * LANES, 2 * LANES, axis=1)
    column = spread(mine, ZAX)
    column = column.reshape(column.shape[0] * rows, 2 * LANES)
    full = spread(column, ("y", "x"))
    return full.reshape(lax.axis_size("y"), -1, 2 * LANES)


def body(tokens, gain, w_query, w_key, w_value, conv_weight):
    rows = tokens.shape[0]
    width = w_query.shape[1]
    heads = width // HEAD_WIDTH
    groups = width // LANES
    core = lax.axis_index("core")
    xfloat = tokens.astype(jnp.float32)
    scale = lax.rsqrt(jnp.mean(xfloat * xfloat, axis=1, keepdims=True) + 1e-06)
    normed = (xfloat * scale * gain.astype(jnp.float32)).astype(jnp.bfloat16)
    other = swap(normed)
    weights = gather_weights(w_query, w_key, w_value)
    both = jnp.concatenate([normed, other], axis=0)
    proj = jnp.concatenate(
        [jnp.dot(both, weights[i], preferred_element_type=jnp.float32) for i in range(weights.shape[0])],
        axis=1,
    )
    feat = jax.nn.elu(proj) + 1.0
    plain = jnp.logical_and(core == 0, lax.broadcasted_iota(jnp.int32, proj.shape, 1) < width)
    proj = jnp.where(plain, proj, feat).astype(jnp.bfloat16)
    mine, theirs = proj[:rows], swap(proj[rows:])
    first = jnp.where(core == 0, mine, theirs)
    second = jnp.where(core == 0, theirs, mine)
    values = first[:, :width]
    kfeat = second[:, :width]
    qfeat = jnp.concatenate([first[:, width:], second[:, width : 2 * width - 3 * LANES]], axis=1)

    count = lax.axis_size(TM)
    before = lax.ppermute(values, TM, [(i, i + 1) for i in range(count - 1)])
    after = lax.ppermute(values, TM, [(i + 1, i) for i in range(count - 1)])

    state = jnp.einsum(
        "gni,gnl->inl",
        kfeat.reshape(rows, heads, HEAD_WIDTH),
        values.reshape(rows, heads, HEAD_WIDTH),
        preferred_element_type=jnp.float32,
    ).reshape(HEAD_WIDTH, width)
    ksum = jnp.sum(kfeat, axis=0, dtype=jnp.float32)
    near = lax.axis_size(NEAR)
    chunks = jnp.concatenate([state.reshape(near, -1), ksum.reshape(near, -1)], axis=1)
    part = jnp.sum(exchange(chunks, NEAR), axis=0)
    part = jnp.sum(spread(part, "zh"), axis=0)
    chunks = spread(part, NEAR)
    state = chunks[:, : HEAD_WIDTH * width // near].reshape(HEAD_WIDTH, heads, HEAD_WIDTH)
    ksum = chunks[:, HEAD_WIDTH * width // near :].reshape(heads, HEAD_WIDTH)

    framed = jnp.stack([before, values, after]).reshape(3, FH, FW, width)
    padded = jnp.pad(framed, ((0, 0), (1, 1), (1, 1), (0, 0)))
    kernel = conv_weight.astype(jnp.float32)
    local = jnp.zeros((FH, FW, width), jnp.float32)
    for shift_t in range(3):
        for shift_y in range(3):
            for shift_x in range(3):
                window = padded[shift_t, shift_y : shift_y + FH, shift_x : shift_x + FW, :]
                local = (
                    local + window.astype(jnp.float32) * kernel[9 * shift_t + 3 * shift_y + shift_x]
                )
    query_heads = qfeat.astype(jnp.float32).reshape(rows, heads, HEAD_WIDTH)
    numerator = jnp.einsum("dnb,bnt->dnt", query_heads, state, precision=lax.Precision.HIGHEST)
    denom = jnp.einsum("rhk,hk->rh", query_heads, ksum, precision=lax.Precision.HIGHEST)
    attended = (numerator / denom[:, :, None]).reshape(rows, width)
    return attended + local.reshape(rows, width)


def solution(mesh):
    fine = Mesh(mesh.devices.reshape(4, 2, 4, 4, 4), AXES)
    rows = P(AXES, None)
    split = P(TM, None)
    return jax.shard_map(
        body, mesh=fine, in_specs=(rows, P(), split, split, split, P()), out_specs=rows, check_vma=False
    )
```

time: 730 us -> 200 us (0.27)
  the two profiles are of different devices: /device:TPU:8 before, /device:TPU:2 now
where the time goes in v1:
time: 200 us; the launch traced here: 198 us
  local copies, waits for them, and re-layouts  61.3 us (31%)
  starting transfers between devices  39.7 us (20%)
  blocking collectives  31.4 us (16%)
  waiting for transfers between devices  31.4 us (16%)
  other arithmetic  25.1 us (13%)
  matrix products  8.63 us (4%)
    convert_element_type x24, local copies, waits for them, and re-layouts, body(): window.astype(jnp.float32) * kernel[9 * shift_t + 3 * shift_y + shift_x]  45.5 us
    all_to_all x1, blocking collectives, exchange(): return lax.all_to_all(blocks, axes, 0, 0, tiled=True)  31.4 us
    all_to_all x4, waiting for transfers between devices, exchange(): return lax.all_to_all(blocks, axes, 0, 0, tiled=True)  29.5 us
    all_to_all x4, starting transfers between devices, exchange(): return lax.all_to_all(blocks, axes, 0, 0, tiled=True)  26.4 us
    convert_element_type x13, other arithmetic, body(): window.astype(jnp.float32) * kernel[9 * shift_t + 3 * shift_y + shift_x]  13.9 us
    ppermute x1, starting transfers between devices, body(): after = lax.ppermute(values, TM, [(i + 1, i) for i in range(count - 1)])  7.62 us
    add x1, other arithmetic, body(): return attended + local.reshape(rows, width)  7.42 us
    dot_general x4, matrix products, body(): jnp.dot(both, weights[i], preferred_element_type=jnp.float32)  6.48 us
  transfers between devices with their start and end apart: 8, of which 3 were waited for; matrix products, arithmetic and copies ran while one was open for 34% of the time, Pallas kernels for 0%

profile of v1, /device:TPU:2, one launch (start us, length us, event | category | flops | bytes accessed | tf_op | source)
XLA Modules:
  0.0 198.4 jit_solution(10248900603882944880)
XLA Ops:
  2.3 31.4 %all_to_all.34 = bf16[16,18,256]{2,1,0:T(8,128)(2,1)S(1)} all-to-all(bf16[16,18,256]{2,1,0:T(8,128)(2,1)S(1)} %broadcast_in_dim.16), channel_id=1, replica_groups=mesh['y'=4,'core'=2,'x'=4,'zh'=4,'zl'=4] {'zh','zl'}, dimensions={0} | all-to-all | bytes 294912 | tf_op jit(solution)/shard_map/all_to_all | solution.py:19
  35.4 7.6 %all-to-all-start.1 = ((bf16[16,288,256]{2,1,0:T(8,128)(2,1)}), bf16[16,288,256]{2,1,0:T(8,128)(2,1)S(1)}, u32[]{:S(2)}, u32[]{:S(2)}) async-start(bf16[16,288,256]{2,1,0:T(8,128)(2,1)} %broadcast_in_dim.18), calls=%async_computation.1 | async-start | bytes 4718592 | tf_op jit(solution)/shard_map/all_to_all | solution.py:19
  43.5 1.9 collective-permute-start
  45.4 25.0 %all-to-all-done.1 = bf16[16,288,256]{2,1,0:T(8,128)(2,1)S(1)} async-done(((bf16[16,288,256]{2,1,0:T(8,128)(2,1)}), bf16[16,288,256]{2,1,0:T(8,128)(2,1)S(1)}, u32[]{:S(2)}, u32[]{:S(2)}) %all-to-all-start.1) | async-done | bytes 2359328 | tf_op jit(solution)/shard_map/all_to_all | solution.py:19
  78.1 1.9 collective-permute-start.1
  82.2 7.6 %collective-permute-start.3 = (bf16[256,640]{0,1:T(8,128)(2,1)S(1)}, bf16[256,640]{0,1:T(8,128)(2,1)S(1)}, u32[]{:S(2)}, u32[]{:S(2)}) collective-permute-start(bf16[256,640]{0,1:T(8,128)(2,1)S(1)} %slice.276), channel_id=1, source_target_pairs={{1,0},{2,1},{3,2},{4,3},{5,4},{6,5},{7,6},{8,7},{9,8},{10,9},{11,1... | collective-permute-start | bytes 983048 | tf_op jit(solution)/shard_map/ppermute | solution.py:73
  93.2 6.8 %all-to-all-start.2 = ((f32[16,1,1320]{2,1,0:T(1,128)}), f32[16,1,1320]{2,1,0:T(1,128)S(1)}, u32[]{:S(2)}, u32[]{:S(2)}) async-start(f32[16,1,1320]{2,1,0:T(1,128)} %copy.101), calls=%async_computation.2 | async-start | bytes 180224 | tf_op jit(solution)/shard_map/all_to_all | solution.py:19
  102.4 4.5 %all-to-all-done.2 = f32[16,1,1320]{2,1,0:T(1,128)S(1)} async-done(((f32[16,1,1320]{2,1,0:T(1,128)}), f32[16,1,1320]{2,1,0:T(1,128)S(1)}, u32[]{:S(2)}, u32[]{:S(2)}) %all-to-all-start.2) | async-done | bytes 84512 | tf_op jit(solution)/shard_map/all_to_all | solution.py:19
  107.6 6.6 %all-to-all-start.3 = ((f32[4,1,1320]{2,1,0:T(1,128)}), f32[4,1,1320]{2,1,0:T(1,128)S(1)}, u32[]{:S(2)}, u32[]{:S(2)}) async-start(f32[4,1,1320]{2,1,0:T(1,128)} %broadcast_in_dim.19), calls=%async_computation.3 | async-start | bytes 45056 | tf_op jit(solution)/shard_map/all_to_all | solution.py:19
  130.4 5.3 %all-to-all-start.4 = ((f32[16,1,1320]{2,1,0:T(1,128)}), f32[16,1,1320]{2,1,0:T(1,128)}, u32[]{:S(2)}, u32[]{:S(2)}) async-start(f32[16,1,1320]{2,1,0:T(1,128)} %broadcast_in_dim.20), calls=%async_computation.4 | async-start | bytes 180224 | tf_op jit(solution)/shard_map/all_to_all | solution.py:19
  138.7 2.2 %copy.126 = f32[256,640]{0,1:T(8,128)} copy(f32[256,640]{1,0:T(8,128)} %get-tuple-element.69) | data formatting | bytes 1310720 | tf_op jit(solution)/shard_map/convert_element_type | solution.py:99
  140.9 2.2 %copy.125 = f32[256,640]{0,1:T(8,128)} copy(f32[256,640]{1,0:T(8,128)} %get-tuple-element.70) | data formatting | bytes 1310720 | tf_op jit(solution)/shard_map/convert_element_type | solution.py:99
  143.0 2.2 %copy.124 = f32[256,640]{0,1:T(8,128)} copy(f32[256,640]{1,0:T(8,128)} %get-tuple-element.71) | data formatting | bytes 1310720 | tf_op jit(solution)/shard_map/convert_element_type | solution.py:99
  145.2 2.2 %copy.123 = f32[256,640]{0,1:T(8,128)} copy(f32[256,640]{1,0:T(8,128)} %get-tuple-element.72) | data formatting | bytes 1310720 | tf_op jit(solution)/shard_map/convert_element_type | solution.py:99
  147.4 2.2 %copy.122 = f32[256,640]{0,1:T(8,128)} copy(f32[256,640]{1,0:T(8,128)} %get-tuple-element.73) | data formatting | bytes 1310720 | tf_op jit(solution)/shard_map/convert_element_type | solution.py:99
  149.6 2.2 %copy.121 = f32[256,640]{0,1:T(8,128)} copy(f32[256,640]{1,0:T(8,128)} %get-tuple-element.74) | data formatting | bytes 1310720 | tf_op jit(solution)/shard_map/convert_element_type | solution.py:99
  151.7 2.2 %copy.120 = f32[256,640]{0,1:T(8,128)} copy(f32[256,640]{1,0:T(8,128)} %get-tuple-element.75) | data formatting | bytes 1310720 | tf_op jit(solution)/shard_map/convert_element_type | solution.py:99
  153.9 2.2 %copy.119 = f32[256,640]{0,1:T(8,128)} copy(f32[256,640]{1,0:T(8,128)} %get-tuple-element.76) | data formatting | bytes 1310720 | tf_op jit(solution)/shard_map/convert_element_type | solution.py:99
  156.1 2.2 %copy.118 = f32[256,640]{0,1:T(8,128)} copy(f32[256,640]{1,0:T(8,128)} %get-tuple-element.77) | data formatting | bytes 1310720 | tf_op jit(solution)/shard_map/convert_element_type | solution.py:99
  158.3 2.2 %copy.117 = f32[256,640]{0,1:T(8,128)} copy(f32[256,640]{1,0:T(8,128)} %get-tuple-element.78) | data formatting | bytes 1310720 | tf_op jit(solution)/shard_map/convert_element_type | solution.py:99
  160.4 2.2 %copy.116 = f32[256,640]{0,1:T(8,128)} copy(f32[256,640]{1,0:T(8,128)} %get-tuple-element.79) | data formatting | bytes 1310720 | tf_op jit(solution)/shard_map/convert_element_type | solution.py:99
  162.6 2.2 %copy.115 = f32[256,640]{0,1:T(8,128)} copy(f32[256,640]{1,0:T(8,128)} %get-tuple-element.80) | data formatting | bytes 1310720 | tf_op jit(solution)/shard_map/convert_element_type | solution.py:99
  164.8 2.2 %copy.114 = f32[256,640]{0,1:T(8,128)} copy(f32[256,640]{1,0:T(8,128)} %get-tuple-element.81) | data formatting | bytes 1310720 | tf_op jit(solution)/shard_map/convert_element_type | solution.py:99
  166.9 2.2 %copy.113 = f32[256,640]{0,1:T(8,128)} copy(f32[256,640]{1,0:T(8,128)} %get-tuple-element.82) | data formatting | bytes 1310720 | tf_op jit(solution)/shard_map/convert_element_type | solution.py:99
  169.1 2.2 %copy.112 = f32[256,640]{0,1:T(8,128)} copy(f32[256,640]{1,0:T(8,128)} %get-tuple-element.83) | data formatting | bytes 1310720 | tf_op jit(solution)/shard_map/convert_element_type | solution.py:99
  171.3 2.2 %copy.111 = f32[256,640]{0,1:T(8,128)} copy(f32[256,640]{1,0:T(8,128)} %get-tuple-element.63) | data formatting | bytes 1310720 | tf_op jit(solution)/shard_map/convert_element_type | solution.py:99
  173.5 2.2 %copy.110 = f32[256,640]{0,1:T(8,128)} copy(f32[256,640]{1,0:T(8,128)} %get-tuple-element.64) | data formatting | bytes 1310720 | tf_op jit(solution)/shard_map/convert_element_type | solution.py:99
  175.6 2.2 %copy.109 = f32[256,640]{0,1:T(8,128)} copy(f32[256,640]{1,0:T(8,128)} %get-tuple-element.65) | data formatting | bytes 1310720 | tf_op jit(solution)/shard_map/convert_element_type | solution.py:99
  177.8 2.2 %copy.108 = f32[256,640]{0,1:T(8,128)} copy(f32[256,640]{1,0:T(8,128)} %bitcast_convert_fusion.22) | data formatting | bytes 1310720 | tf_op jit(solution)/shard_map/convert_element_type | solution.py:99
  180.9 2.2 %copy.107 = f32[256,640]{0,1:T(8,128)} copy(f32[256,640]{1,0:T(8,128)} %bitcast_convert_fusion.23) | data formatting | bytes 1310720 | tf_op jit(solution)/shard_map/convert_element_type | solution.py:99
  188.8 7.4 %bitcast_add_fusion = f32[256,640]{0,1:T(8,128)} fusion(f32[256,20,32]{0,2,1:T(8,128)S(1)} %fusion.10, f32[256,640]{0,1:T(8,128)S(1)} %copy.130, f32[256,640]{0,1:T(8,128)S(1)} %copy.129, f32[256,640]{0,1:T(8,128)S(1)} %copy.128, f32[256,640]{0,1:T(8,128)S(1)} %copy.127, bf16[256,640]{0,1:T(8,128)(2,1)} %copy-done.7, f32[256,640]{0,1:T(8,128)S(1)} %copy-done, ...), kind=kLoop, calls=%fused_computation.27 | loop fusion | flops 9338880 | bytes 18091520 | tf_op jit(solution)/shard_map/add | solution.py:105
  196.3 2.2 %copy.131 = f32[256,640]{1,0:T(8,128)} copy(f32[256,640]{0,1:T(8,128)} %bitcast_add_fusion) | data formatting | bytes 1310720 | tf_op jit(solution)/shard_map/add | solution.py:105
  (154 shorter events, 45.8 us)
Async XLA Ops:
  35.4 7.6 %copy-start.37 = (bf16[1152]{0:T(1024)(128)(2,1)S(1)}, bf16[1152]{0:T(1024)(128)(2,1)}, u32[]{:S(2)}) copy-start(bf16[1152]{0:T(1024)(128)(2,1)} %param.7) | copy-start | bytes 6916
  35.4 7.6 %copy-start.4 = (bf16[256,1152]{1,0:T(8,128)(2,1)S(1)}, bf16[256,1152]{1,0:T(8,128)(2,1)}, u32[]{:S(2)}) copy-start(bf16[256,1152]{1,0:T(8,128)(2,1)} %param.6) | copy-start | bytes 1769476
  35.4 35.0 %all-to-all-start.1 = ((bf16[16,288,256]{2,1,0:T(8,128)(2,1)}), bf16[16,288,256]{2,1,0:T(8,128)(2,1)S(1)}, u32[]{:S(2)}, u32[]{:S(2)}) async-start(bf16[16,288,256]{2,1,0:T(8,128)(2,1)} %broadcast_in_dim.18), calls=%async_computation.1 | async-start | bytes 4718592 | tf_op jit(solution)/shard_map/all_to_all | solution.py:19
  43.5 27.1 %collective-permute-start = (bf16[256,1152]{1,0:T(8,128)(2,1)S(1)}, bf16[256,1152]{1,0:T(8,128)(2,1)}, u32[]{:S(2)}, u32[]{:S(2)}) collective-permute-start(bf16[256,1152]{1,0:T(8,128)(2,1)S(1)} %fusion.13), channel_id=1, source_target_pairs={{0,64},{64,0},{1,65},{65,1},{2,66},{66,2},{3,67},{67,3},{4,68},{68... | collective-permute-start | bytes 1769480 | tf_op jit(solution)/shard_map/ppermute | solution.py:28
  77.1 2.9 %copy-start.9 = (bf16[27,640]{1,0:T(8,128)(2,1)S(1)}, bf16[27,640]{1,0:T(8,128)(2,1)}, u32[]{:S(2)}) copy-start(bf16[27,640]{1,0:T(8,128)(2,1)} %param.11) | copy-start | bytes 103684
  78.1 3.8 %collective-permute-start.1 = (bf16[256,1024]{0,1:T(8,128)(2,1)S(1)}, bf16[256,1024]{0,1:T(8,128)(2,1)S(1)}, u32[]{:S(2)}, u32[]{:S(2)}) collective-permute-start(bf16[256,1024]{0,1:T(8,128)(2,1)S(1)} %slice.275), channel_id=1, source_target_pairs={{0,64},{64,0},{1,65},{65,1},{2,66},{66,2},{3,67},{67,3},{4,68},{68... | collective-permute-start | bytes 1572872 | tf_op jit(solution)/shard_map/ppermute | solution.py:28
  82.2 31.9 %collective-permute-start.3 = (bf16[256,640]{0,1:T(8,128)(2,1)S(1)}, bf16[256,640]{0,1:T(8,128)(2,1)S(1)}, u32[]{:S(2)}, u32[]{:S(2)}) collective-permute-start(bf16[256,640]{0,1:T(8,128)(2,1)S(1)} %slice.276), channel_id=1, source_target_pairs={{1,0},{2,1},{3,2},{4,3},{5,4},{6,5},{7,6},{8,7},{9,8},{10,9},{11,1... | collective-permute-start | bytes 983048 | tf_op jit(solution)/shard_map/ppermute | solution.py:73
  89.9 24.5 %collective-permute-start.2 = (bf16[256,640]{0,1:T(8,128)(2,1)S(1)}, bf16[256,640]{0,1:T(8,128)(2,1)S(1)}, u32[]{:S(2)}, u32[]{:S(2)}) collective-permute-start(bf16[256,640]{0,1:T(8,128)(2,1)S(1)} %slice.276), channel_id=1, source_target_pairs={{0,1},{1,2},{2,3},{3,4},{4,5},{5,6},{6,7},{7,8},{8,9},{9,10},{10,1... | collective-permute-start | bytes 983048 | tf_op jit(solution)/shard_map/ppermute | solution.py:72
  93.2 13.7 %all-to-all-start.2 = ((f32[16,1,1320]{2,1,0:T(1,128)}), f32[16,1,1320]{2,1,0:T(1,128)S(1)}, u32[]{:S(2)}, u32[]{:S(2)}) async-start(f32[16,1,1320]{2,1,0:T(1,128)} %copy.101), calls=%async_computation.2 | async-start | bytes 180224 | tf_op jit(solution)/shard_map/all_to_all | solution.py:19
  107.6 22.1 %all-to-all-start.3 = ((f32[4,1,1320]{2,1,0:T(1,128)}), f32[4,1,1320]{2,1,0:T(1,128)S(1)}, u32[]{:S(2)}, u32[]{:S(2)}) async-start(f32[4,1,1320]{2,1,0:T(1,128)} %broadcast_in_dim.19), calls=%async_computation.3 | async-start | bytes 45056 | tf_op jit(solution)/shard_map/all_to_all | solution.py:19
  128.5 7.3 %copy-start.6 = (bf16[1,8,32,640]{3,2,1,0:T(8,128)(2,1)S(1)}, bf16[1,8,32,640]{3,2,1,0:T(8,128)(2,1)}, u32[]{:S(2)}) copy-start(bf16[1,8,32,640]{3,2,1,0:T(8,128)(2,1)} %get-tuple-element.57) | copy-start | bytes 983044
  130.4 52.7 %all-to-all-start.4 = ((f32[16,1,1320]{2,1,0:T(1,128)}), f32[16,1,1320]{2,1,0:T(1,128)}, u32[]{:S(2)}, u32[]{:S(2)}) async-start(f32[16,1,1320]{2,1,0:T(1,128)} %broadcast_in_dim.20), calls=%async_computation.4 | async-start | bytes 180224 | tf_op jit(solution)/shard_map/all_to_all | solution.py:19
  180.9 5.7 %copy-start.5 = (bf16[256,640]{0,1:T(8,128)(2,1)S(1)}, bf16[256,640]{0,1:T(8,128)(2,1)}, u32[]{:S(2)}) copy-start(bf16[256,640]{0,1:T(8,128)(2,1)} %pad_maximum_fusion.1) | copy-start | bytes 983044
  185.5 3.0 %copy-start.10 = (f32[640]{0:T(1024)S(1)}, f32[640]{0:T(1024)}, u32[]{:S(2)}) copy-start(f32[640]{0:T(1024)} %get-tuple-element.5) | copy-start | bytes 7684
  185.5 3.0 %copy-start.11 = (f32[640]{0:T(1024)S(1)}, f32[640]{0:T(1024)}, u32[]{:S(2)}) copy-start(f32[640]{0:T(1024)} %get-tuple-element.6) | copy-start | bytes 7684
  185.5 3.1 %copy-start.12 = (f32[640]{0:T(1024)S(1)}, f32[640]{0:T(1024)}, u32[]{:S(2)}) copy-start(f32[640]{0:T(1024)} %get-tuple-element.7) | copy-start | bytes 7684
  185.5 3.1 %copy-start.13 = (f32[640]{0:T(1024)S(1)}, f32[640]{0:T(1024)}, u32[]{:S(2)}) copy-start(f32[640]{0:T(1024)} %get-tuple-element.8) | copy-start | bytes 7684
  185.5 3.1 %copy-start.14 = (f32[640]{0:T(1024)S(1)}, f32[640]{0:T(1024)}, u32[]{:S(2)}) copy-start(f32[640]{0:T(1024)} %get-tuple-element.9) | copy-start | bytes 7684
  185.5 3.1 %copy-start.15 = (f32[640]{0:T(1024)S(1)}, f32[640]{0:T(1024)}, u32[]{:S(2)}) copy-start(f32[640]{0:T(1024)} %get-tuple-element.10) | copy-start | bytes 7684
  185.5 3.1 %copy-start.16 = (f32[640]{0:T(1024)S(1)}, f32[640]{0:T(1024)}, u32[]{:S(2)}) copy-start(f32[640]{0:T(1024)} %get-tuple-element.11) | copy-start | bytes 7684
  185.5 3.1 %copy-start.17 = (f32[640]{0:T(1024)S(1)}, f32[640]{0:T(1024)}, u32[]{:S(2)}) copy-start(f32[640]{0:T(1024)} %get-tuple-element.12) | copy-start | bytes 7684
  185.6 3.1 %copy-start.18 = (f32[640]{0:T(1024)S(1)}, f32[640]{0:T(1024)}, u32[]{:S(2)}) copy-start(f32[640]{0:T(1024)} %get-tuple-element.13) | copy-start | bytes 7684
  185.6 3.1 %copy-start.19 = (f32[640]{0:T(1024)S(1)}, f32[640]{0:T(1024)}, u32[]{:S(2)}) copy-start(f32[640]{0:T(1024)} %get-tuple-element.14) | copy-start | bytes 7684
  185.6 3.1 %copy-start.20 = (f32[640]{0:T(1024)S(1)}, f32[640]{0:T(1024)}, u32[]{:S(2)}) copy-start(f32[640]{0:T(1024)} %get-tuple-element.15) | copy-start | bytes 7684
  185.6 3.1 %copy-start.21 = (f32[640]{0:T(1024)S(1)}, f32[640]{0:T(1024)}, u32[]{:S(2)}) copy-start(f32[640]{0:T(1024)} %get-tuple-element.16) | copy-start | bytes 7684
  185.6 3.1 %copy-start.22 = (f32[640]{0:T(1024)S(1)}, f32[640]{0:T(1024)}, u32[]{:S(2)}) copy-start(f32[640]{0:T(1024)} %get-tuple-element.17) | copy-start | bytes 7684
  185.6 3.1 %copy-start.23 = (f32[640]{0:T(1024)S(1)}, f32[640]{0:T(1024)}, u32[]{:S(2)}) copy-start(f32[640]{0:T(1024)} %get-tuple-element.18) | copy-start | bytes 7684
  185.6 3.1 %copy-start.24 = (f32[640]{0:T(1024)S(1)}, f32[640]{0:T(1024)}, u32[]{:S(2)}) copy-start(f32[640]{0:T(1024)} %get-tuple-element.19) | copy-start | bytes 7684
  185.6 3.1 %copy-start.25 = (f32[640]{0:T(1024)S(1)}, f32[640]{0:T(1024)}, u32[]{:S(2)}) copy-start(f32[640]{0:T(1024)} %get-tuple-element.20) | copy-start | bytes 7684
  185.6 3.1 %copy-start.26 = (f32[640]{0:T(1024)S(1)}, f32[640]{0:T(1024)}, u32[]{:S(2)}) copy-start(f32[640]{0:T(1024)} %get-tuple-element.21) | copy-start | bytes 7684
  186.4 2.3 %copy-start.1 = (f32[256,640]{0,1:T(8,128)S(1)}, f32[256,640]{0,1:T(8,128)}, u32[]{:S(2)}) copy-start(f32[256,640]{0,1:T(8,128)} %copy.125) | copy-start | bytes 1966084
  186.4 2.3 %copy-start.2 = (f32[256,640]{0,1:T(8,128)S(1)}, f32[256,640]{0,1:T(8,128)}, u32[]{:S(2)}) copy-start(f32[256,640]{0,1:T(8,128)} %copy.124) | copy-start | bytes 1966084
  (14 other events, 28.9 us)

commit v2 on v1

v2 whole, which is shorter than its diff:
```python
import jax
import jax.numpy as jnp
from jax import lax
from jax.experimental import pallas as pl
from jax.experimental.pallas import tpu as pltpu
from jax.sharding import Mesh
from jax.sharding import PartitionSpec as P

HEAD_WIDTH = 32
FH = 8
FW = 32
LANES = 128
BLOCK = 2 * LANES
GROUPS = 5
TILES = 32

AXES = ("y", "core", "x", "zh", "zl")
ZAX = ("zh", "zl")
TM = ("x", "zh", "zl")
NEAR = ("x", "zl")
PARAMS = pltpu.CompilerParams(vmem_limit_bytes=40 * 1024 * 1024)


def cost(flops, nbytes):
    return pl.CostEstimate(flops=flops, bytes_accessed=nbytes, transcendentals=0)


def exchange(blocks, axes):
    return lax.all_to_all(blocks, axes, 0, 0, tiled=True)


def spread(block, axes):
    count = lax.axis_size(axes)
    return exchange(jnp.broadcast_to(block[None], (count,) + block.shape), axes)


def norm_kernel(tokens_ref, gain_ref, out_ref):
    x = tokens_ref[...].astype(jnp.float32)
    scale = lax.rsqrt(jnp.mean(x * x, axis=1, keepdims=True) + 1e-06)
    normed = (x * scale * gain_ref[...].astype(jnp.float32)).astype(jnp.bfloat16)
    for i in range(out_ref.shape[0]):
        out_ref[i] = normed


def norm(tokens, gain, copies):
    return pl.pallas_call(
        norm_kernel,
        out_shape=jax.ShapeDtypeStruct((copies,) + tokens.shape, jnp.bfloat16),
        compiler_params=PARAMS,
        cost_estimate=cost(10 * tokens.size, 10 * tokens.size),
        name="norm",
    )(tokens, gain.reshape(1, -1))


def project_kernel(tokens_ref, mine_ref, theirs_ref, out_ref):
    core = lax.axis_index("core")
    first = lax.axis_index("y") * 4
    tokens = tokens_ref[0]
    for half, ref in enumerate((mine_ref, theirs_ref)):
        place = core if half == 0 else 1 - core
        proj = jnp.dot(tokens, ref[...], preferred_element_type=jnp.float32)
        feat = jnp.where(proj > 0, proj, jnp.exp(jnp.minimum(proj, 0.0)) - 1.0) + 1.0
        lane = lax.broadcasted_iota(jnp.int32, proj.shape, 1)
        unit = first + 2 * place + lane // LANES
        proj = jnp.where(unit < GROUPS, proj, feat).astype(jnp.bfloat16)
        out_ref[0, :, pl.ds(pl.multiple_of(place * BLOCK, BLOCK), BLOCK)] = proj


def project(tokens, mine, theirs):
    videos, rows, depth = tokens.shape
    whole = pl.BlockSpec((depth, BLOCK), lambda i: (0, 0))
    return pl.pallas_call(
        project_kernel,
        grid=(videos,),
        in_specs=[pl.BlockSpec((1, rows, depth), lambda i: (i, 0, 0)), whole, whole],
        out_specs=pl.BlockSpec((1, rows, 2 * BLOCK), lambda i: (i, 0, 0)),
        out_shape=jax.ShapeDtypeStruct((videos, rows, 2 * BLOCK), jnp.bfloat16),
        compiler_params=PARAMS,
        cost_estimate=cost(2 * videos * rows * depth * 2 * BLOCK, 4 * 1024 * 1024),
        name="project",
    )(tokens, mine, theirs)


def unit_of(ref, unit):
    at = unit % 4
    return ref[unit // 4, :, at * LANES : (at + 1) * LANES]


def state_kernel(proj_ref, values_ref, tiles_ref):
    lane = lax.broadcasted_iota(jnp.int32, (HEAD_WIDTH, LANES), 1) // HEAD_WIDTH
    tiles_ref[...] = jnp.zeros_like(tiles_ref)
    for g in range(GROUPS):
        values = unit_of(proj_ref, g)
        kfeat = unit_of(proj_ref, GROUPS + g)
        values_ref[:, g * LANES : (g + 1) * LANES] = values
        square = lax.dot_general(
            kfeat, values, (((0,), (0,)), ((), ())), preferred_element_type=jnp.float32
        )
        packed = jnp.zeros((HEAD_WIDTH, LANES), jnp.float32)
        for h in range(LANES // HEAD_WIDTH):
            packed = jnp.where(lane == h, square[h * HEAD_WIDTH : (h + 1) * HEAD_WIDTH], packed)
        for t in range(4):
            tiles_ref[4 * g + t] = packed[8 * t : 8 * t + 8]
        tiles_ref[4 * GROUPS, g : g + 1, :] = jnp.sum(
            kfeat.astype(jnp.float32), axis=0, keepdims=True
        )


def states(proj):
    rows = proj.shape[1]
    return pl.pallas_call(
        state_kernel,
        out_shape=(
            jax.ShapeDtypeStruct((rows, GROUPS * LANES), jnp.bfloat16),
            jax.ShapeDtypeStruct((TILES, 8, LANES), jnp.float32),
        ),
        compiler_params=PARAMS,
        cost_estimate=cost(2 * rows * GROUPS * LANES * LANES, 2 * 1024 * 1024),
        name="states",
    )(proj)


def conv_kernel(before_ref, values_ref, after_ref, weight_ref, out_ref):
    zeros = jnp.zeros((FW, LANES), jnp.float32)
    rows = FH * FW
    x = lax.broadcasted_iota(jnp.int32, (rows, LANES), 0) % FW
    weight = weight_ref[...].astype(jnp.float32)
    frames = [
        jnp.concatenate([zeros, ref[...].astype(jnp.float32), zeros], axis=0)
        for ref in (before_ref, values_ref, after_ref)
    ]
    sums = []
    for c in range(3):
        total = None
        for a in range(3):
            for b in range(3):
                tap = 9 * a + 3 * b + c
                term = frames[a][b * FW : b * FW + rows] * weight[tap : tap + 1]
                total = term if total is None else total + term
        sums.append(total)
    left = jnp.where(x == 0, 0.0, pltpu.roll(sums[0], 1, 0))
    right = jnp.where(x == FW - 1, 0.0, pltpu.roll(sums[2], rows - 1, 0))
    out_ref[...] = left + sums[1] + right


def convolve(before, values, after, weight):
    rows, width = values.shape
    block = pl.BlockSpec((rows, LANES), lambda i: (0, i))
    return pl.pallas_call(
        conv_kernel,
        grid=(width // LANES,),
        in_specs=[block, block, block, pl.BlockSpec((27, LANES), lambda i: (0, i))],
        out_specs=block,
        out_shape=jax.ShapeDtypeStruct((rows, width), jnp.float32),
        compiler_params=PARAMS,
        cost_estimate=cost(54 * rows * width, 2 * 1024 * 1024),
        name="convolve",
    )(before, values, after, weight)


def split_dot(a, b):
    high = b.astype(jnp.bfloat16)
    low = (b - high.astype(jnp.float32)).astype(jnp.bfloat16)
    return jnp.dot(a, high, preferred_element_type=jnp.float32) + jnp.dot(
        a, low, preferred_element_type=jnp.float32
    )


def attend_kernel(proj_ref, tiles_ref, local_ref, out_ref):
    row = lax.broadcasted_iota(jnp.int32, (LANES, LANES), 0) // HEAD_WIDTH
    lane = lax.broadcasted_iota(jnp.int32, (LANES, LANES), 1) // HEAD_WIDTH
    same = row == lane
    for g in range(GROUPS):
        qfeat = unit_of(proj_ref, 2 * GROUPS + g)
        packed = tiles_ref[4 * g : 4 * g + 4].reshape(HEAD_WIDTH, LANES)
        state = jnp.where(same, jnp.concatenate([packed] * 4, axis=0), 0.0)
        ksum = jnp.broadcast_to(tiles_ref[4 * GROUPS, g : g + 1, :], (LANES, LANES)).T
        ksum = jnp.where(same, ksum, 0.0)
        both = split_dot(qfeat, jnp.concatenate([state, ksum], axis=1))
        cols = slice(g * LANES, (g + 1) * LANES)
        out_ref[:, cols] = both[:, :LANES] / both[:, LANES:] + local_ref[:, cols]


def attend(proj, tiles, local):
    rows, width = local.shape
    return pl.pallas_call(
        attend_kernel,
        out_shape=jax.ShapeDtypeStruct((rows, width), jnp.float32),
        compiler_params=PARAMS,
        cost_estimate=cost(8 * rows * width * LANES, 3 * 1024 * 1024),
        name="attend",
    )(proj, tiles, local)


def gather_weights(w_query, w_key, w_value):
    rows = w_query.shape[0]
    pad = jnp.zeros((rows, LANES), w_query.dtype)
    cat = jnp.concatenate([w_value, w_key, w_query, pad], axis=1)
    place = 2 * lax.axis_index("y") + lax.axis_index("core")
    mine = lax.dynamic_slice_in_dim(cat, place * BLOCK, BLOCK, axis=1)
    column = spread(mine, ZAX)
    column = column.reshape(column.shape[0] * rows, BLOCK)
    return spread(column, "x").reshape(-1, BLOCK)


def total_state(tiles):
    near = lax.axis_size(NEAR)
    shape = (near, TILES // near) + tiles.shape[1:]
    part = jnp.sum(exchange(tiles, NEAR).reshape(shape), axis=0)
    part = jnp.sum(spread(part, "zh"), axis=0)
    return spread(part, NEAR).reshape(tiles.shape)


def body(tokens, gain, w_query, w_key, w_value, conv_weight):
    mine = gather_weights(w_query, w_key, w_value)
    theirs = lax.ppermute(mine, "core", [(0, 1), (1, 0)])
    normed = exchange(norm(tokens, gain, lax.axis_size("y")), "y")
    proj = exchange(project(normed, mine, theirs), "y")
    values, tiles = states(proj)
    count = lax.axis_size(TM)
    before = lax.ppermute(values, TM, [(i, i + 1) for i in range(count - 1)])
    after = lax.ppermute(values, TM, [(i + 1, i) for i in range(count - 1)])
    tiles = total_state(tiles)
    local = convolve(before, values, after, conv_weight)
    return attend(proj, tiles, local)


def solution(mesh):
    fine = Mesh(mesh.devices.reshape(4, 2, 4, 4, 4), AXES)
    rows = P(AXES, None)
    split = P(TM, None)
    return jax.shard_map(
        body, mesh=fine, in_specs=(rows, P(), split, split, split, P()), out_specs=rows, check_vma=False
    )
```

time: 200 us -> 148 us (0.74)
  local copies, waits for them, and re-layouts: 61.3 us -> 1.7 us
  blocking collectives: 31.4 us -> 81.1 us
  other arithmetic: 25.1 us -> 0.82 us
  starting transfers between devices: 39.7 us -> 24.3 us
  matrix products: 8.63 us -> 0 us
  Pallas kernels: 0 us -> 7.58 us
    all_to_all x1 -> x4, blocking collectives: 31.4 us -> 81.1 us  [exchange(): return lax.all_to_all(blocks, axes, 0, 0, tiled=True)]
    convert_element_type x24 -> x0, local copies, waits for them, and re-layouts: 45.5 us -> none  [body(): window.astype(jnp.float32) * kernel[9 * shift_t + 3 * shift_y + shift_x]]
    convert_element_type x17 -> x0, other arithmetic: 15.1 us -> none  [the longest x13 13.9 us: body(): window.astype(jnp.float32) * kernel[9 * shift_t + 3 * shift_y + shift_x]]
    all_to_all x4 -> x3, starting transfers between devices: 26.4 us -> 14.4 us  [exchange(): return lax.all_to_all(blocks, axes, 0, 0, tiled=True)]
    dot_general x7 -> x0, matrix products: 8.63 us -> none  [the longest x4 6.48 us: body(): jnp.dot(both, weights[i], preferred_element_type=jnp.float32)]
    pallas_call x0 -> x5, Pallas kernels: none -> 7.58 us  [the longest x1 2.41 us: project(): pl.pallas_call(project_kernel, grid=(videos,), in_specs=[pl.BlockSpec((1,...]
    add x1 -> x0, other arithmetic: 7.42 us -> none  [body(): return attended + local.reshape(rows, width)]
    slice x15 -> x0, local copies, waits for them, and re-layouts: 5.76 us -> none  [the longest x2 1.89 us: body(): window = padded[shift_t, shift_y:shift_y + FH, shift_x:shift_x + FW, :]]
  transfers between devices with their start and end apart: 8 -> 6, of which waited for: 3 -> 5; matrix products, arithmetic and copies ran while one was open for 34% -> 0% of each run, Pallas kernels for 0% -> 2%
where the time goes in v2:
time: 148 us; the launch traced here: 147 us
  blocking collectives  81.1 us (55%)
  waiting for transfers between devices  31.5 us (21%)
  starting transfers between devices  24.3 us (16%)
  Pallas kernels  7.58 us (5%)
  local copies, waits for them, and re-layouts  1.7 us (1%)
    all_to_all x4, blocking collectives, exchange(): return lax.all_to_all(blocks, axes, 0, 0, tiled=True)  81.1 us
    all_to_all x3, waiting for transfers between devices, exchange(): return lax.all_to_all(blocks, axes, 0, 0, tiled=True)  24.9 us
    all_to_all x3, starting transfers between devices, exchange(): return lax.all_to_all(blocks, axes, 0, 0, tiled=True)  14.4 us
    ppermute x1, starting transfers between devices, body(): after = lax.ppermute(values, TM, [(i + 1, i) for i in range(count - 1)])  4.57 us
    ppermute x1, starting transfers between devices, body(): before = lax.ppermute(values, TM, [(i, i + 1) for i in range(count - 1)])  3.37 us
    ppermute x1, waiting for transfers between devices, body(): before = lax.ppermute(values, TM, [(i, i + 1) for i in range(count - 1)])  3.11 us
  transfers between devices with their start and end apart: 6, of which 5 were waited for; matrix products, arithmetic and copies ran while one was open for 0% of the time, Pallas kernels for 2%

profile of v2, /device:TPU:2, one launch (start us, length us, event | category | flops | bytes accessed | tf_op | source)
XLA Modules:
  0.0 147.0 jit_solution(9663841203189170727)
XLA Ops:
  0.0 0.0 copy-start.2
  0.0 0.0 copy-start
  0.0 0.1 pad_dynamic-slice_fusion.3
  0.1 0.8 fusion.2
  0.9 31.4 %all_to_all.35 = bf16[16,18,256]{2,1,0:T(8,128)(2,1)S(1)} all-to-all(bf16[16,18,256]{2,1,0:T(8,128)(2,1)S(1)} %broadcast_in_dim.13), channel_id=1, replica_groups=mesh['y'=4,'core'=2,'x'=4,'zh'=4,'zl'=4] {'zh','zl'}, dimensions={0} | all-to-all | bytes 294912 | tf_op jit(solution)/shard_map/all_to_all | solution.py:29
  32.3 0.1 broadcast_in_dim.14
  32.4 0.9 broadcast_in_dim.15
  33.3 4.8 %all-to-all-start.2 = ((bf16[4,288,256]{2,1,0:T(8,128)(2,1)}), bf16[4,288,256]{2,1,0:T(8,128)(2,1)S(1)}, u32[]{:S(2)}, u32[]{:S(2)}) async-start(bf16[4,288,256]{2,1,0:T(8,128)(2,1)} %broadcast_in_dim.15), calls=%async_computation.2 | async-start | bytes 1179648 | tf_op jit(solution)/shard_map/all_to_all | solution.py:29
  38.1 0.0 copy-done.2
  38.1 0.0 copy-done
  38.1 1.7 %norm.1 = bf16[4,256,1152]{2,1,0:T(8,128)(2,1)} custom-call(bf16[256,1152]{1,0:T(8,128)(2,1)S(1)} %copy-done, bf16[1,1152]{1,0:T(2,128)(2,1)S(1)} %reshape.16.gain_ref), custom_call_target="tpu_custom_call" | custom-call | flops 2949120 | bytes 2949120 | tf_op jit(solution)/shard_map/norm/pallas_call | solution.py:46
  39.8 5.3 %all-to-all-done.2 = bf16[4,288,256]{2,1,0:T(8,128)(2,1)S(1)} async-done(((bf16[4,288,256]{2,1,0:T(8,128)(2,1)}), bf16[4,288,256]{2,1,0:T(8,128)(2,1)S(1)}, u32[]{:S(2)}, u32[]{:S(2)}) %all-to-all-start.2) | async-done | bytes 589856 | tf_op jit(solution)/shard_map/all_to_all | solution.py:29
  45.1 4.5 %all-to-all-start = ((bf16[4,256,1152]{2,1,0:T(8,128)(2,1)}), bf16[4,256,1152]{2,1,0:T(8,128)(2,1)S(1)}, u32[]{:S(2)}, u32[]{:S(2)}) async-start(bf16[4,256,1152]{2,1,0:T(8,128)(2,1)} %norm.1), calls=%async_computation | async-start | bytes 4718592 | tf_op jit(solution)/shard_map/all_to_all | solution.py:29
  49.5 1.9 %collective-permute-start = (bf16[1152,256]{1,0:T(8,128)(2,1)S(1)}, bf16[1152,256]{1,0:T(8,128)(2,1)S(1)}, u32[]{:S(2)}, u32[]{:S(2)}) collective-permute-start(bf16[1152,256]{1,0:T(8,128)(2,1)S(1)} %bitcast.3), channel_id=1, source_target_pairs={{0,64},{64,0},{1,65},{65,1},{2,66},{66,2},{3,67},{67,3},{4,68},{68... | collective-permute-start | bytes 1769480 | tf_op jit(solution)/shard_map/ppermute | solution.py:216
  51.4 2.0 %collective-permute-done.theirs_ref = bf16[1152,256]{1,0:T(8,128)(2,1)S(1)} collective-permute-done((bf16[1152,256]{1,0:T(8,128)(2,1)S(1)}, bf16[1152,256]{1,0:T(8,128)(2,1)S(1)}, u32[]{:S(2)}, u32[]{:S(2)}) %collective-permute-start) | collective-permute-done | bytes 589856 | tf_op jit(solution)/shard_map/ppermute | solution.py:216
  53.4 19.7 %all-to-all-done.tokens_ref = bf16[4,256,1152]{2,1,0:T(8,128)(2,1)S(1)} async-done(((bf16[4,256,1152]{2,1,0:T(8,128)(2,1)}), bf16[4,256,1152]{2,1,0:T(8,128)(2,1)S(1)}, u32[]{:S(2)}, u32[]{:S(2)}) %all-to-all-start) | async-done | bytes 2359328 | tf_op jit(solution)/shard_map/all_to_all | solution.py:29
  73.1 2.4 %project.1 = bf16[4,256,512]{2,1,0:T(8,128)(2,1)S(1)} custom-call(bf16[4,256,1152]{2,1,0:T(8,128)(2,1)S(1)} %all-to-all-done.tokens_ref, bf16[1152,256]{1,0:T(8,128)(2,1)S(1)} %bitcast.4, bf16[1152,256]{1,0:T(8,128)(2,1)S(1)} %collective-permute-done.theirs_ref), custom_call_target="tpu_custom_call" | custom-call | flops 1207959552 | bytes 4194304 | tf_op jit(solution)/shard_map/project/pallas_call | solution.py:72
  75.5 0.0 copy-start.1
  75.5 13.3 %all_to_all.36.proj_ref = bf16[4,256,512]{2,1,0:T(8,128)(2,1)S(1)} all-to-all(bf16[4,256,512]{2,1,0:T(8,128)(2,1)S(1)} %project.1), channel_id=1, replica_groups=mesh['y'=4,'core'=2,'x'=4,'zh'=4,'zl'=4] {'y'}, dimensions={0} | all-to-all | bytes 2097152 | tf_op jit(solution)/shard_map/all_to_all | solution.py:29
  88.8 0.3 states.1
  89.2 17.8 %all_to_all.37 = f32[32,8,128]{2,1,0:T(8,128)S(1)} all-to-all(f32[32,8,128]{2,1,0:T(8,128)S(1)} %get-tuple-element.7), channel_id=1, replica_groups=mesh['y'=4,'core'=2,'x'=4,'zh'=4,'zl'=4] {'x','zl'}, dimensions={0} | all-to-all | bytes 262144 | tf_op jit(solution)/shard_map/all_to_all | solution.py:29
  107.0 18.6 %all_to_all.38 = f32[4,2,8,128]{3,2,1,0:T(8,128)S(1)} all-to-all(f32[4,2,8,128]{3,2,1,0:T(8,128)S(1)} %broadcast_in_dim.32), channel_id=1, replica_groups=mesh['y'=4,'core'=2,'x'=4,'zh'=4,'zl'=4] {'zh'}, dimensions={0} | all-to-all | bytes 65536 | tf_op jit(solution)/shard_map/all_to_all | solution.py:29
  125.5 0.7 broadcast_in_dim.33
  126.2 5.2 %all-to-all-start.6 = ((f32[16,2,8,128]{3,2,1,0:T(8,128)}), f32[16,2,8,128]{3,2,1,0:T(8,128)S(1)}, u32[]{:S(2)}, u32[]{:S(2)}) async-start(f32[16,2,8,128]{3,2,1,0:T(8,128)} %broadcast_in_dim.33), calls=%async_computation.6 | async-start | bytes 262144 | tf_op jit(solution)/shard_map/all_to_all | solution.py:29
  131.3 3.4 %collective-permute-start.1 = (bf16[256,640]{1,0:T(8,128)(2,1)S(1)}, bf16[256,640]{1,0:T(8,128)(2,1)S(1)}, u32[]{:S(2)}, u32[]{:S(2)}) collective-permute-start(bf16[256,640]{1,0:T(8,128)(2,1)S(1)} %get-tuple-element.8.values_ref), channel_id=1, source_target_pairs={{0,1},{1,2},{2,3},{3,4},{4,5},{5,6},{6,7},{7,8},{8,9},{9,10},{10,1... | collective-permute-start | bytes 983048 | tf_op jit(solution)/shard_map/ppermute | solution.py:221
  134.7 4.6 %collective-permute-start.2 = (bf16[256,640]{1,0:T(8,128)(2,1)S(1)}, bf16[256,640]{1,0:T(8,128)(2,1)S(1)}, u32[]{:S(2)}, u32[]{:S(2)}) collective-permute-start(bf16[256,640]{1,0:T(8,128)(2,1)S(1)} %get-tuple-element.8.values_ref), channel_id=1, source_target_pairs={{1,0},{2,1},{3,2},{4,3},{5,4},{6,5},{7,6},{8,7},{9,8},{10,9},{11,1... | collective-permute-start | bytes 983048 | tf_op jit(solution)/shard_map/ppermute | solution.py:222
  139.3 3.1 %collective-permute-done.1.before_ref = bf16[256,640]{1,0:T(8,128)(2,1)S(1)} collective-permute-done((bf16[256,640]{1,0:T(8,128)(2,1)S(1)}, bf16[256,640]{1,0:T(8,128)(2,1)S(1)}, u32[]{:S(2)}, u32[]{:S(2)}) %collective-permute-start.1) | collective-permute-done | bytes 327712 | tf_op jit(solution)/shard_map/ppermute | solution.py:221
  142.4 1.5 collective-permute-done.2.after_ref
  143.9 0.0 copy-done.1
  143.9 1.7 %convolve.1.local_ref = f32[256,640]{1,0:T(8,128)S(1)} custom-call(bf16[256,640]{1,0:T(8,128)(2,1)S(1)} %collective-permute-done.1.before_ref, bf16[256,640]{1,0:T(8,128)(2,1)S(1)} %get-tuple-element.8.values_ref, bf16[256,640]{1,0:T(8,128)(2,1)S(1)} %collective-permute-done.2.after_ref, bf16[27,640]{1,0:T(8,128)(2,1)S(1)} %copy-done.1), custom_call_target="tpu_custom_call" | custom-call | flops 8847360 | bytes 2097152 | tf_op jit(solution)/shard_map/convolve/pallas_call | solution.py:149
  145.6 0.0 all-to-all-done.6
  145.6 1.4 attend.1
  (6 shorter events, 0.1 us)
Async XLA Ops:
  0.0 38.1 %copy-start.2 = (bf16[1152]{0:T(1024)(128)(2,1)S(1)}, bf16[1152]{0:T(1024)(128)(2,1)}, u32[]{:S(2)}) copy-start(bf16[1152]{0:T(1024)(128)(2,1)} %param.7) | copy-start | bytes 6916
  0.0 38.1 %copy-start = (bf16[256,1152]{1,0:T(8,128)(2,1)S(1)}, bf16[256,1152]{1,0:T(8,128)(2,1)}, u32[]{:S(2)}) copy-start(bf16[256,1152]{1,0:T(8,128)(2,1)} %tokens_ref.1) | copy-start | bytes 1769476
  33.3 11.8 %all-to-all-start.2 = ((bf16[4,288,256]{2,1,0:T(8,128)(2,1)}), bf16[4,288,256]{2,1,0:T(8,128)(2,1)S(1)}, u32[]{:S(2)}, u32[]{:S(2)}) async-start(bf16[4,288,256]{2,1,0:T(8,128)(2,1)} %broadcast_in_dim.15), calls=%async_computation.2 | async-start | bytes 1179648 | tf_op jit(solution)/shard_map/all_to_all | solution.py:29
  45.1 28.0 %all-to-all-start = ((bf16[4,256,1152]{2,1,0:T(8,128)(2,1)}), bf16[4,256,1152]{2,1,0:T(8,128)(2,1)S(1)}, u32[]{:S(2)}, u32[]{:S(2)}) async-start(bf16[4,256,1152]{2,1,0:T(8,128)(2,1)} %norm.1), calls=%async_computation | async-start | bytes 4718592 | tf_op jit(solution)/shard_map/all_to_all | solution.py:29
  49.5 3.9 %collective-permute-start = (bf16[1152,256]{1,0:T(8,128)(2,1)S(1)}, bf16[1152,256]{1,0:T(8,128)(2,1)S(1)}, u32[]{:S(2)}, u32[]{:S(2)}) collective-permute-start(bf16[1152,256]{1,0:T(8,128)(2,1)S(1)} %bitcast.3), channel_id=1, source_target_pairs={{0,64},{64,0},{1,65},{65,1},{2,66},{66,2},{3,67},{67,3},{4,68},{68... | collective-permute-start | bytes 1769480 | tf_op jit(solution)/shard_map/ppermute | solution.py:216
  75.5 68.4 %copy-start.1 = (bf16[27,640]{1,0:T(8,128)(2,1)S(1)}, bf16[27,640]{1,0:T(8,128)(2,1)}, u32[]{:S(2)}) copy-start(bf16[27,640]{1,0:T(8,128)(2,1)} %weight_ref.1) | copy-start | bytes 103684
  126.2 19.4 %all-to-all-start.6 = ((f32[16,2,8,128]{3,2,1,0:T(8,128)}), f32[16,2,8,128]{3,2,1,0:T(8,128)S(1)}, u32[]{:S(2)}, u32[]{:S(2)}) async-start(f32[16,2,8,128]{3,2,1,0:T(8,128)} %broadcast_in_dim.33), calls=%async_computation.6 | async-start | bytes 262144 | tf_op jit(solution)/shard_map/all_to_all | solution.py:29
  131.3 11.1 %collective-permute-start.1 = (bf16[256,640]{1,0:T(8,128)(2,1)S(1)}, bf16[256,640]{1,0:T(8,128)(2,1)S(1)}, u32[]{:S(2)}, u32[]{:S(2)}) collective-permute-start(bf16[256,640]{1,0:T(8,128)(2,1)S(1)} %get-tuple-element.8.values_ref), channel_id=1, source_target_pairs={{0,1},{1,2},{2,3},{3,4},{4,5},{5,6},{6,7},{7,8},{8,9},{9,10},{10,1... | collective-permute-start | bytes 983048 | tf_op jit(solution)/shard_map/ppermute | solution.py:221
  134.7 9.2 %collective-permute-start.2 = (bf16[256,640]{1,0:T(8,128)(2,1)S(1)}, bf16[256,640]{1,0:T(8,128)(2,1)S(1)}, u32[]{:S(2)}, u32[]{:S(2)}) collective-permute-start(bf16[256,640]{1,0:T(8,128)(2,1)S(1)} %get-tuple-element.8.values_ref), channel_id=1, source_target_pairs={{1,0},{2,1},{3,2},{4,3},{5,4},{6,5},{7,6},{8,7},{9,8},{10,9},{11,1... | collective-permute-start | bytes 983048 | tf_op jit(solution)/shard_map/ppermute | solution.py:222

commit v3 on v2

--- a/solution.py
+++ b/solution.py
@@ -37,62 +37,69 @@
 def norm_kernel(tokens_ref, gain_ref, out_ref):
     x = tokens_ref[...].astype(jnp.float32)
     scale = lax.rsqrt(jnp.mean(x * x, axis=1, keepdims=True) + 1e-06)
-    normed = (x * scale * gain_ref[...].astype(jnp.float32)).astype(jnp.bfloat16)
-    for i in range(out_ref.shape[0]):
-        out_ref[i] = normed
-
-
-def norm(tokens, gain, copies):
+    out_ref[...] = (x * scale * gain_ref[...].astype(jnp.float32)).astype(jnp.bfloat16)
+
+
+def norm(tokens, gain):
     return pl.pallas_call(
         norm_kernel,
-        out_shape=jax.ShapeDtypeStruct((copies,) + tokens.shape, jnp.bfloat16),
-        compiler_params=PARAMS,
-        cost_estimate=cost(10 * tokens.size, 10 * tokens.size),
+        out_shape=jax.ShapeDtypeStruct(tokens.shape, jnp.bfloat16),
+        compiler_params=PARAMS,
+        cost_estimate=cost(10 * tokens.size, 4 * tokens.size),
         name="norm",
     )(tokens, gain.reshape(1, -1))
 
 
-def project_kernel(tokens_ref, mine_ref, theirs_ref, out_ref):
+def project_kernel(mine_ref, theirs_ref, weight_ref, *out_refs):
     core = lax.axis_index("core")
-    first = lax.axis_index("y") * 4
-    tokens = tokens_ref[0]
-    for half, ref in enumerate((mine_ref, theirs_ref)):
-        place = core if half == 0 else 1 - core
-        proj = jnp.dot(tokens, ref[...], preferred_element_type=jnp.float32)
+    weight = weight_ref[0]
+    split = GROUPS * LANES
+    for tokens_ref, main_ref, rest_ref in (
+        (mine_ref, out_refs[0], out_refs[1]),
+        (theirs_ref, out_refs[2], out_refs[3]),
+    ):
+        proj = jnp.dot(tokens_ref[...], weight, preferred_element_type=jnp.float32)
         feat = jnp.where(proj > 0, proj, jnp.exp(jnp.minimum(proj, 0.0)) - 1.0) + 1.0
-        lane = lax.broadcasted_iota(jnp.int32, proj.shape, 1)
-        unit = first + 2 * place + lane // LANES
-        proj = jnp.where(unit < GROUPS, proj, feat).astype(jnp.bfloat16)
-        out_ref[0, :, pl.ds(pl.multiple_of(place * BLOCK, BLOCK), BLOCK)] = proj
-
-
-def project(tokens, mine, theirs):
-    videos, rows, depth = tokens.shape
-    whole = pl.BlockSpec((depth, BLOCK), lambda i: (0, 0))
+        unit = 2 * pl.program_id(0) + lax.broadcasted_iota(jnp.int32, proj.shape, 1) // LANES
+        plain = jnp.logical_and(unit < GROUPS, core == 0)
+        proj = jnp.where(plain, proj, feat).astype(jnp.bfloat16)
+        for step in range(4):
+
+            @pl.when(pl.program_id(0) == step)
+            def _():
+                for half in range(2):
+                    at = step * BLOCK + half * LANES
+                    ref = main_ref if at < split else rest_ref
+                    at = at if at < split else at - split
+                    ref[:, at : at + LANES] = proj[:, half * LANES : (half + 1) * LANES]
+
+
+def project(mine, theirs, weights):
+    steps, depth, _ = weights.shape
+    rows = mine.shape[0]
+    widths = (GROUPS * LANES, steps * BLOCK - GROUPS * LANES) * 2
+    tokens = pl.BlockSpec((rows, depth), lambda i: (0, 0))
     return pl.pallas_call(
         project_kernel,
-        grid=(videos,),
-        in_specs=[pl.BlockSpec((1, rows, depth), lambda i: (i, 0, 0)), whole, whole],
-        out_specs=pl.BlockSpec((1, rows, 2 * BLOCK), lambda i: (i, 0, 0)),
-        out_shape=jax.ShapeDtypeStruct((videos, rows, 2 * BLOCK), jnp.bfloat16),
-        compiler_params=PARAMS,
-        cost_estimate=cost(2 * videos * rows * depth * 2 * BLOCK, 4 * 1024 * 1024),
+        grid=(steps,),
+        in_specs=[tokens, tokens, pl.BlockSpec((1, depth, BLOCK), lambda i: (i, 0, 0))],
+        out_specs=[pl.BlockSpec((rows, width), lambda i: (0, 0)) for width in widths],
+        out_shape=[jax.ShapeDtypeStruct((rows, width), jnp.bfloat16) for width in widths],
+        compiler_params=PARAMS,
+        cost_estimate=cost(4 * rows * depth * steps * BLOCK, 5 * 1024 * 1024),
         name="project",
-    )(tokens, mine, theirs)
-
-
-def unit_of(ref, unit):
-    at = unit % 4
-    return ref[unit // 4, :, at * LANES : (at + 1) * LANES]
-
-
-def state_kernel(proj_ref, values_ref, tiles_ref):
+    )(mine, theirs, weights)
+
+
+def state_kernel(mine_ref, theirs_ref, values_ref, tiles_ref):
+    first = lax.axis_index("core") == 0
     lane = lax.broadcasted_iota(jnp.int32, (HEAD_WIDTH, LANES), 1) // HEAD_WIDTH
     tiles_ref[...] = jnp.zeros_like(tiles_ref)
     for g in range(GROUPS):
-        values = unit_of(proj_ref, g)
-        kfeat = unit_of(proj_ref, GROUPS + g)
-        values_ref[:, g * LANES : (g + 1) * LANES] = values
+        cols = slice(g * LANES, (g + 1) * LANES)
+        values = jnp.where(first, mine_ref[:, cols], theirs_ref[:, cols])
+        kfeat = jnp.where(first, theirs_ref[:, cols], mine_ref[:, cols])
+        values_ref[:, cols] = values
         square = lax.dot_general(
             kfeat, values, (((0,), (0,)), ((), ())), preferred_element_type=jnp.float32
         )
@@ -106,8 +113,8 @@
         )
 
 
-def states(proj):
-    rows = proj.shape[1]
+def states(mine, theirs):
+    rows = mine.shape[0]
     return pl.pallas_call(
         state_kernel,
         out_shape=(
@@ -117,7 +124,7 @@
         compiler_params=PARAMS,
         cost_estimate=cost(2 * rows * GROUPS * LANES * LANES, 2 * 1024 * 1024),
         name="states",
-    )(proj)
+    )(mine, theirs)
 
 
 def conv_kernel(before_ref, values_ref, after_ref, weight_ref, out_ref):
@@ -166,12 +173,15 @@
     )
 
 
-def attend_kernel(proj_ref, tiles_ref, local_ref, out_ref):
+def attend_kernel(mine_ref, theirs_ref, tiles_ref, local_ref, out_ref):
+    first = lax.axis_index("core") == 0
     row = lax.broadcasted_iota(jnp.int32, (LANES, LANES), 0) // HEAD_WIDTH
     lane = lax.broadcasted_iota(jnp.int32, (LANES, LANES), 1) // HEAD_WIDTH
     same = row == lane
     for g in range(GROUPS):
-        qfeat = unit_of(proj_ref, 2 * GROUPS + g)
+        early, late = (mine_ref, theirs_ref) if g < 3 else (theirs_ref, mine_ref)
+        at = slice(g % 3 * LANES, (g % 3 + 1) * LANES)
+        qfeat = jnp.where(first, early[:, at], late[:, at])
         packed = tiles_ref[4 * g : 4 * g + 4].reshape(HEAD_WIDTH, LANES)
         state = jnp.where(same, jnp.concatenate([packed] * 4, axis=0), 0.0)
         ksum = jnp.broadcast_to(tiles_ref[4 * GROUPS, g : g + 1, :], (LANES, LANES)).T
@@ -181,7 +191,7 @@
         out_ref[:, cols] = both[:, :LANES] / both[:, LANES:] + local_ref[:, cols]
 
 
-def attend(proj, tiles, local):
+def attend(mine, theirs, tiles, local):
     rows, width = local.shape
     return pl.pallas_call(
         attend_kernel,
@@ -189,40 +199,45 @@
         compiler_params=PARAMS,
         cost_estimate=cost(8 * rows * width * LANES, 3 * 1024 * 1024),
         name="attend",
-    )(proj, tiles, local)
+    )(mine, theirs, tiles, local)
+
+
+def swap(block):
+    return lax.ppermute(block, "core", [(0, 1), (1, 0)])
 
 
 def gather_weights(w_query, w_key, w_value):
     rows = w_query.shape[0]
     pad = jnp.zeros((rows, LANES), w_query.dtype)
-    cat = jnp.concatenate([w_value, w_key, w_query, pad], axis=1)
-    place = 2 * lax.axis_index("y") + lax.axis_index("core")
+    cut = 3 * LANES
+    cat = jnp.concatenate([w_value, w_query[:, :cut], w_key, w_query[:, cut:], pad], axis=1)
+    place = 4 * lax.axis_index("core") + lax.axis_index("y")
     mine = lax.dynamic_slice_in_dim(cat, place * BLOCK, BLOCK, axis=1)
+    mine = jnp.concatenate([mine[:, :LANES], mine[:, LANES:]], axis=0)
     column = spread(mine, ZAX)
+    column = jnp.concatenate([column[:, :rows], column[:, rows:]], axis=2)
     column = column.reshape(column.shape[0] * rows, BLOCK)
-    return spread(column, "x").reshape(-1, BLOCK)
-
-
-def total_state(tiles):
+    return spread(column, ("y", "x")).reshape(lax.axis_size("y"), -1, BLOCK)
+
+
+def body(tokens, gain, w_query, w_key, w_value, conv_weight):
+    normed = norm(tokens, gain)
+    weights = gather_weights(w_query, w_key, w_value)
+    main, rest, their_main, their_rest = project(normed, swap(normed), weights)
+    values, tiles = states(main, swap(their_main))
+    their_rest = swap(their_rest)
+    count = lax.axis_size(TM)
+    before = lax.ppermute(values, TM, [(i, i + 1) for i in range(count - 1)])
+    after = lax.ppermute(values, TM, [(i + 1, i) for i in range(count - 1)])
+    local = convolve(before, values, after, conv_weight)
+
     near = lax.axis_size(NEAR)
     shape = (near, TILES // near) + tiles.shape[1:]
     part = jnp.sum(exchange(tiles, NEAR).reshape(shape), axis=0)
     part = jnp.sum(spread(part, "zh"), axis=0)
-    return spread(part, NEAR).reshape(tiles.shape)
-
-
-def body(tokens, gain, w_query, w_key, w_value, conv_weight):
-    mine = gather_weights(w_query, w_key, w_value)
-    theirs = lax.ppermute(mine, "core", [(0, 1), (1, 0)])
-    normed = exchange(norm(tokens, gain, lax.axis_size("y")), "y")
-    proj = exchange(project(normed, mine, theirs), "y")
-    values, tiles = states(proj)
-    count = lax.axis_size(TM)
-    before = lax.ppermute(values, TM, [(i, i + 1) for i in range(count - 1)])
-    after = lax.ppermute(values, TM, [(i + 1, i) for i in range(count - 1)])
-    tiles = total_state(tiles)
-    local = convolve(before, values, after, conv_weight)
-    return attend(proj, tiles, local)
+    part, local = lax.optimization_barrier((part, local))
+    tiles = spread(part, NEAR).reshape(tiles.shape)
+    return attend(rest, their_rest, tiles, local)
 
 
 def solution(mesh):

time: 148 us -> 133 us (0.90)
  blocking collectives: 81.1 us -> 30.6 us
  starting transfers between devices: 24.3 us -> 42.1 us
  waiting for transfers between devices: 31.5 us -> 42 us
  local copies, waits for them, and re-layouts: 1.7 us -> 8.6 us
    all_to_all x4 -> x1, blocking collectives: 81.1 us -> 30.6 us  [exchange(): return lax.all_to_all(blocks, axes, 0, 0, tiled=True)]
    all_to_all x3 -> x4, starting transfers between devices: 14.4 us -> 28.3 us  [exchange(): return lax.all_to_all(blocks, axes, 0, 0, tiled=True)]
    all_to_all x3 -> x4, waiting for transfers between devices: 24.9 us -> 37 us  [exchange(): return lax.all_to_all(blocks, axes, 0, 0, tiled=True)]
    unnamed x6 -> x18, local copies, waits for them, and re-layouts: 0.01 us -> 5.52 us
    ppermute x1 -> x3, starting transfers between devices: 1.91 us -> 5.88 us  [swap(): return lax.ppermute(block, 'core', [(0, 1), (1, 0)])]
    ppermute x1, waiting for transfers between devices: 3.11 us -> 0.01 us  [body(): before = lax.ppermute(values, TM, [(i, i + 1) for i in range(count - 1)])]
    ppermute x1 -> x3, waiting for transfers between devices: 1.97 us -> 4.97 us  [swap(): return lax.ppermute(block, 'core', [(0, 1), (1, 0)])]
  transfers between devices with their start and end apart: 6 -> 9, of which waited for: 5 -> 6; matrix products, arithmetic and copies ran while one was open for 0% -> 0% of each run, Pallas kernels for 2% -> 1%
where the time goes in v3:
time: 133 us; the launch traced here: 132 us
  starting transfers between devices  42.1 us (32%)
  waiting for transfers between devices  42 us (32%)
  blocking collectives  30.6 us (23%)
  Pallas kernels  8.63 us (6%)
  local copies, waits for them, and re-layouts  8.6 us (6%)
    all_to_all x4, waiting for transfers between devices, exchange(): return lax.all_to_all(blocks, axes, 0, 0, tiled=True)  37 us
    all_to_all x1, blocking collectives, exchange(): return lax.all_to_all(blocks, axes, 0, 0, tiled=True)  30.6 us
    all_to_all x4, starting transfers between devices, exchange(): return lax.all_to_all(blocks, axes, 0, 0, tiled=True)  28.3 us
    ppermute x3, starting transfers between devices, swap(): return lax.ppermute(block, 'core', [(0, 1), (1, 0)])  5.88 us
    unnamed x18, local copies, waits for them, and re-layouts  5.52 us
    ppermute x3, waiting for transfers between devices, swap(): return lax.ppermute(block, 'core', [(0, 1), (1, 0)])  4.97 us
    ppermute x1, starting transfers between devices, body(): after = lax.ppermute(values, TM, [(i + 1, i) for i in range(count - 1)])  4.58 us
    pallas_call x1, Pallas kernels, project(): pl.pallas_call(project_kernel, grid=(steps,), in_specs=[tokens, tokens, p...  4.21 us
  transfers between devices with their start and end apart: 9, of which 6 were waited for; matrix products, arithmetic and copies ran while one was open for 0% of the time, Pallas kernels for 1%

profile of v3, /device:TPU:2, one launch (start us, length us, event | category | flops | bytes accessed | tf_op | source)
XLA Modules:
  0.0 132.2 jit_solution(4215968780477735836)
XLA Ops:
  0.0 0.8 constant_dynamic-update-slice_fusion.2
  0.8 0.7 slice_dynamic-update-slice_fusion
  1.5 0.8 constant_dynamic-update-slice_fusion.1
  2.2 0.7 slice_dynamic-update-slice_fusion.1
  3.0 30.6 %all_to_all.25 = bf16[16,36,128]{2,1,0:T(8,128)(2,1)S(1)} all-to-all(bf16[16,36,128]{2,1,0:T(8,128)(2,1)S(1)} %broadcast_in_dim.13), channel_id=1, replica_groups=mesh['y'=4,'core'=2,'x'=4,'zh'=4,'zl'=4] {'zh','zl'}, dimensions={0} | all-to-all | bytes 294912 | tf_op jit(solution)/shard_map/all_to_all | solution.py:29
  33.7 0.1 broadcast_in_dim.14
  33.8 1.7 %broadcast_in_dim.15 = bf16[16,288,256]{2,1,0:T(8,128)(2,1)} broadcast(bf16[288,256]{1,0:T(8,128)(2,1)S(1)} %broadcast_in_dim.14), dimensions={1,2} | broadcast | bytes 2506752 | tf_op jit(solution)/shard_map/broadcast_in_dim | solution.py:34
  35.4 7.6 %all-to-all-start.1 = ((bf16[16,288,256]{2,1,0:T(8,128)(2,1)}), bf16[16,288,256]{2,1,0:T(8,128)(2,1)S(1)}, u32[]{:S(2)}, u32[]{:S(2)}) async-start(bf16[16,288,256]{2,1,0:T(8,128)(2,1)} %broadcast_in_dim.15), calls=%async_computation.1 | async-start | bytes 4718592 | tf_op jit(solution)/shard_map/all_to_all | solution.py:29
  43.1 0.2 norm.1.mine_ref
  43.3 1.9 %collective-permute-start = (bf16[256,1152]{1,0:T(8,128)(2,1)S(1)}, bf16[256,1152]{1,0:T(8,128)(2,1)S(1)}, u32[]{:S(2)}, u32[]{:S(2)}) collective-permute-start(bf16[256,1152]{1,0:T(8,128)(2,1)S(1)} %norm.1.mine_ref), channel_id=1, source_target_pairs={{0,64},{64,0},{1,65},{65,1},{2,66},{66,2},{3,67},{67,3},{4,68},{68... | collective-permute-start | bytes 1769480 | tf_op jit(solution)/shard_map/ppermute | solution.py:206
  45.3 2.0 %collective-permute-done.theirs_ref = bf16[256,1152]{1,0:T(8,128)(2,1)S(1)} collective-permute-done((bf16[256,1152]{1,0:T(8,128)(2,1)S(1)}, bf16[256,1152]{1,0:T(8,128)(2,1)S(1)}, u32[]{:S(2)}, u32[]{:S(2)}) %collective-permute-start) | collective-permute-done | bytes 589856 | tf_op jit(solution)/shard_map/ppermute | solution.py:206
  47.2 0.8 copy-done.2
  48.0 22.4 %all-to-all-done.1 = bf16[16,288,256]{2,1,0:T(8,128)(2,1)S(1)} async-done(((bf16[16,288,256]{2,1,0:T(8,128)(2,1)}), bf16[16,288,256]{2,1,0:T(8,128)(2,1)S(1)}, u32[]{:S(2)}, u32[]{:S(2)}) %all-to-all-start.1) | async-done | bytes 2359328 | tf_op jit(solution)/shard_map/all_to_all | solution.py:29
  70.4 1.1 copy-done.3
  71.5 4.2 %project.1 = (bf16[256,640]{1,0:T(8,128)(2,1)S(1)}, bf16[256,384]{1,0:T(8,128)(2,1)S(1)}, bf16[256,640]{1,0:T(8,128)(2,1)S(1)}, bf16[256,384]{1,0:T(8,128)(2,1)S(1)}) custom-call(bf16[256,1152]{1,0:T(8,128)(2,1)S(1)} %norm.1.mine_ref, bf16[256,1152]{1,0:T(8,128)(2,1)S(1)} %copy-done.3, bf16[4,1152,256]{2,1,0:T(8,128)(2,1)S(1)} %bitcast.3), custom_call_target="tpu_custom_call" | custom-call | flops 1207959552 | bytes 5242880 | tf_op jit(solution)/shard_map/project/pallas_call | solution.py:82
  75.7 0.7 copy-done.4
  76.4 2.0 %collective-permute-start.2 = (bf16[256,640]{1,0:T(8,128)(2,1)S(1)}, bf16[256,640]{1,0:T(8,128)(2,1)S(1)}, u32[]{:S(2)}, u32[]{:S(2)}) collective-permute-start(bf16[256,640]{1,0:T(8,128)(2,1)S(1)} %get-tuple-element.16), channel_id=1, source_target_pairs={{0,64},{64,0},{1,65},{65,1},{2,66},{66,2},{3,67},{67,3},{4,68},{68... | collective-permute-start | bytes 983048 | tf_op jit(solution)/shard_map/ppermute | solution.py:206
  78.4 1.6 %collective-permute-done.2.theirs_ref = bf16[256,640]{1,0:T(8,128)(2,1)S(1)} collective-permute-done((bf16[256,640]{1,0:T(8,128)(2,1)S(1)}, bf16[256,640]{1,0:T(8,128)(2,1)S(1)}, u32[]{:S(2)}, u32[]{:S(2)}) %collective-permute-start.2) | collective-permute-done | bytes 327712 | tf_op jit(solution)/shard_map/ppermute | solution.py:206
  80.0 1.0 states.1
  81.0 9.3 %all-to-all-start.2 = ((f32[32,8,128]{2,1,0:T(8,128)}), f32[32,8,128]{2,1,0:T(8,128)S(1)}, u32[]{:S(2)}, u32[]{:S(2)}) async-start(f32[32,8,128]{2,1,0:T(8,128)} %get-tuple-element.17), calls=%async_computation.2 | async-start | bytes 262144 | tf_op jit(solution)/shard_map/all_to_all | solution.py:29
  90.3 3.4 %collective-permute-start.3 = (bf16[256,640]{1,0:T(8,128)(2,1)S(1)}, bf16[256,640]{1,0:T(8,128)(2,1)S(1)}, u32[]{:S(2)}, u32[]{:S(2)}) collective-permute-start(bf16[256,640]{1,0:T(8,128)(2,1)S(1)} %get-tuple-element.18.values_ref), channel_id=1, source_target_pairs={{0,1},{1,2},{2,3},{3,4},{4,5},{5,6},{6,7},{7,8},{8,9},{9,10},{10,1... | collective-permute-start | bytes 983048 | tf_op jit(solution)/shard_map/ppermute | solution.py:230
  93.7 4.6 %collective-permute-start.4 = (bf16[256,640]{1,0:T(8,128)(2,1)S(1)}, bf16[256,640]{1,0:T(8,128)(2,1)S(1)}, u32[]{:S(2)}, u32[]{:S(2)}) collective-permute-start(bf16[256,640]{1,0:T(8,128)(2,1)S(1)} %get-tuple-element.18.values_ref), channel_id=1, source_target_pairs={{1,0},{2,1},{3,2},{4,3},{5,4},{6,5},{7,6},{8,7},{9,8},{10,9},{11,1... | collective-permute-start | bytes 983048 | tf_op jit(solution)/shard_map/ppermute | solution.py:231
  98.3 0.6 broadcast_in_dim.32
  98.9 6.3 %all-to-all-start.3 = ((f32[4,2,8,128]{3,2,1,0:T(8,128)}), f32[4,2,8,128]{3,2,1,0:T(8,128)S(1)}, u32[]{:S(2)}, u32[]{:S(2)}) async-start(f32[4,2,8,128]{3,2,1,0:T(8,128)} %broadcast_in_dim.32), calls=%async_computation.3 | async-start | bytes 65536 | tf_op jit(solution)/shard_map/all_to_all | solution.py:29
  105.2 1.7 %convolve.1.local_ref = f32[256,640]{1,0:T(8,128)S(1)} custom-call(bf16[256,640]{1,0:T(8,128)(2,1)S(1)} %collective-permute-done.3.before_ref, bf16[256,640]{1,0:T(8,128)(2,1)S(1)} %get-tuple-element.18.values_ref, bf16[256,640]{1,0:T(8,128)(2,1)S(1)} %collective-permute-done.4.after_ref, bf16[27,640]{1,0:T(8,128)(2,1)S(1)} %copy-done.1), custom_call_target="tpu_custom_call" | custom-call | flops 8847360 | bytes 2097152 | tf_op jit(solution)/shard_map/convolve/pallas_call | solution.py:156
  106.9 10.9 %all-to-all-done.3 = f32[4,2,8,128]{3,2,1,0:T(8,128)S(1)} async-done(((f32[4,2,8,128]{3,2,1,0:T(8,128)}), f32[4,2,8,128]{3,2,1,0:T(8,128)S(1)}, u32[]{:S(2)}, u32[]{:S(2)}) %all-to-all-start.3) | async-done | bytes 32800 | tf_op jit(solution)/shard_map/all_to_all | solution.py:29
  117.9 0.7 broadcast_in_dim.33
  118.6 5.1 %all-to-all-start.4 = ((f32[16,2,8,128]{3,2,1,0:T(8,128)}), f32[16,2,8,128]{3,2,1,0:T(8,128)S(1)}, u32[]{:S(2)}, u32[]{:S(2)}) async-start(f32[16,2,8,128]{3,2,1,0:T(8,128)} %broadcast_in_dim.33), calls=%async_computation.4 | async-start | bytes 262144 | tf_op jit(solution)/shard_map/all_to_all | solution.py:29
  123.7 1.9 %collective-permute-start.1 = (bf16[256,384]{1,0:T(8,128)(2,1)S(1)}, bf16[256,384]{1,0:T(8,128)(2,1)S(1)}, u32[]{:S(2)}, u32[]{:S(2)}) collective-permute-start(bf16[256,384]{1,0:T(8,128)(2,1)S(1)} %copy-done.5), channel_id=1, source_target_pairs={{0,64},{64,0},{1,65},{65,1},{2,66},{66,2},{3,67},{67,3},{4,68},{68... | collective-permute-start | bytes 589832 | tf_op jit(solution)/shard_map/ppermute | solution.py:206
  125.6 1.4 %collective-permute-done.1.theirs_ref = bf16[256,384]{1,0:T(8,128)(2,1)S(1)} collective-permute-done((bf16[256,384]{1,0:T(8,128)(2,1)S(1)}, bf16[256,384]{1,0:T(8,128)(2,1)S(1)}, u32[]{:S(2)}, u32[]{:S(2)}) %collective-permute-start.1) | collective-permute-done | bytes 196640 | tf_op jit(solution)/shard_map/ppermute | solution.py:206
  127.0 3.7 %all-to-all-done.4 = f32[16,2,8,128]{3,2,1,0:T(8,128)S(1)} async-done(((f32[16,2,8,128]{3,2,1,0:T(8,128)}), f32[16,2,8,128]{3,2,1,0:T(8,128)S(1)}, u32[]{:S(2)}, u32[]{:S(2)}) %all-to-all-start.4) | async-done | bytes 131104 | tf_op jit(solution)/shard_map/all_to_all | solution.py:29
  130.7 1.4 %attend.1 = f32[256,640]{1,0:T(8,128)} custom-call(bf16[256,384]{1,0:T(8,128)(2,1)S(1)} %get-tuple-element.13.mine_ref, bf16[256,384]{1,0:T(8,128)(2,1)S(1)} %collective-permute-done.1.theirs_ref, f32[32,8,128]{2,1,0:T(8,128)S(1)} %bitcast.4, f32[256,640]{1,0:T(8,128)S(1)} %convolve.1.local_ref), custom_call_target="tpu_custom_call" | custom-call | flops 167772160 | bytes 3145728 | tf_op jit(solution)/shard_map/attend/pallas_call | solution.py:196
  (23 shorter events, 0.2 us)
Async XLA Ops:
  35.4 7.6 %copy-start.6 = (bf16[1152]{0:T(1024)(128)(2,1)S(1)}, bf16[1152]{0:T(1024)(128)(2,1)}, u32[]{:S(2)}) copy-start(bf16[1152]{0:T(1024)(128)(2,1)} %param.7) | copy-start | bytes 6916
  35.4 7.6 %copy-start = (bf16[256,1152]{1,0:T(8,128)(2,1)S(1)}, bf16[256,1152]{1,0:T(8,128)(2,1)}, u32[]{:S(2)}) copy-start(bf16[256,1152]{1,0:T(8,128)(2,1)} %tokens_ref.1) | copy-start | bytes 1769476
  35.4 35.0 %all-to-all-start.1 = ((bf16[16,288,256]{2,1,0:T(8,128)(2,1)}), bf16[16,288,256]{2,1,0:T(8,128)(2,1)S(1)}, u32[]{:S(2)}, u32[]{:S(2)}) async-start(bf16[16,288,256]{2,1,0:T(8,128)(2,1)} %broadcast_in_dim.15), calls=%async_computation.1 | async-start | bytes 4718592 | tf_op jit(solution)/shard_map/all_to_all | solution.py:29
  43.3 3.9 %collective-permute-start = (bf16[256,1152]{1,0:T(8,128)(2,1)S(1)}, bf16[256,1152]{1,0:T(8,128)(2,1)S(1)}, u32[]{:S(2)}, u32[]{:S(2)}) collective-permute-start(bf16[256,1152]{1,0:T(8,128)(2,1)S(1)} %norm.1.mine_ref), channel_id=1, source_target_pairs={{0,64},{64,0},{1,65},{65,1},{2,66},{66,2},{3,67},{67,3},{4,68},{68... | collective-permute-start | bytes 1769480 | tf_op jit(solution)/shard_map/ppermute | solution.py:206
  47.2 0.8 copy-start.2
  70.4 1.1 copy-start.3
  71.5 33.7 %copy-start.1 = (bf16[27,640]{1,0:T(8,128)(2,1)S(1)}, bf16[27,640]{1,0:T(8,128)(2,1)}, u32[]{:S(2)}) copy-start(bf16[27,640]{1,0:T(8,128)(2,1)} %weight_ref.1) | copy-start | bytes 103684
  75.7 0.7 copy-start.4
  76.4 47.3 %copy-start.5 = (bf16[256,384]{1,0:T(8,128)(2,1)S(1)}, bf16[256,384]{1,0:T(8,128)(2,1)}, u32[]{:S(2)}) copy-start(bf16[256,384]{1,0:T(8,128)(2,1)} %copy-done.4) | copy-start | bytes 589828
  76.4 3.6 %collective-permute-start.2 = (bf16[256,640]{1,0:T(8,128)(2,1)S(1)}, bf16[256,640]{1,0:T(8,128)(2,1)S(1)}, u32[]{:S(2)}, u32[]{:S(2)}) collective-permute-start(bf16[256,640]{1,0:T(8,128)(2,1)S(1)} %get-tuple-element.16), channel_id=1, source_target_pairs={{0,64},{64,0},{1,65},{65,1},{2,66},{66,2},{3,67},{67,3},{4,68},{68... | collective-permute-start | bytes 983048 | tf_op jit(solution)/shard_map/ppermute | solution.py:206
  81.0 17.2 %all-to-all-start.2 = ((f32[32,8,128]{2,1,0:T(8,128)}), f32[32,8,128]{2,1,0:T(8,128)S(1)}, u32[]{:S(2)}, u32[]{:S(2)}) async-start(f32[32,8,128]{2,1,0:T(8,128)} %get-tuple-element.17), calls=%async_computation.2 | async-start | bytes 262144 | tf_op jit(solution)/shard_map/all_to_all | solution.py:29
  90.3 14.9 %collective-permute-start.3 = (bf16[256,640]{1,0:T(8,128)(2,1)S(1)}, bf16[256,640]{1,0:T(8,128)(2,1)S(1)}, u32[]{:S(2)}, u32[]{:S(2)}) collective-permute-start(bf16[256,640]{1,0:T(8,128)(2,1)S(1)} %get-tuple-element.18.values_ref), channel_id=1, source_target_pairs={{0,1},{1,2},{2,3},{3,4},{4,5},{5,6},{6,7},{7,8},{8,9},{9,10},{10,1... | collective-permute-start | bytes 983048 | tf_op jit(solution)/shard_map/ppermute | solution.py:230
  93.7 11.5 %collective-permute-start.4 = (bf16[256,640]{1,0:T(8,128)(2,1)S(1)}, bf16[256,640]{1,0:T(8,128)(2,1)S(1)}, u32[]{:S(2)}, u32[]{:S(2)}) collective-permute-start(bf16[256,640]{1,0:T(8,128)(2,1)S(1)} %get-tuple-element.18.values_ref), channel_id=1, source_target_pairs={{1,0},{2,1},{3,2},{4,3},{5,4},{6,5},{7,6},{8,7},{9,8},{10,9},{11,1... | collective-permute-start | bytes 983048 | tf_op jit(solution)/shard_map/ppermute | solution.py:231
  98.9 18.9 %all-to-all-start.3 = ((f32[4,2,8,128]{3,2,1,0:T(8,128)}), f32[4,2,8,128]{3,2,1,0:T(8,128)S(1)}, u32[]{:S(2)}, u32[]{:S(2)}) async-start(f32[4,2,8,128]{3,2,1,0:T(8,128)} %broadcast_in_dim.32), calls=%async_computation.3 | async-start | bytes 65536 | tf_op jit(solution)/shard_map/all_to_all | solution.py:29
  118.6 12.2 %all-to-all-start.4 = ((f32[16,2,8,128]{3,2,1,0:T(8,128)}), f32[16,2,8,128]{3,2,1,0:T(8,128)S(1)}, u32[]{:S(2)}, u32[]{:S(2)}) async-start(f32[16,2,8,128]{3,2,1,0:T(8,128)} %broadcast_in_dim.33), calls=%async_computation.4 | async-start | bytes 262144 | tf_op jit(solution)/shard_map/all_to_all | solution.py:29
  123.7 3.3 %collective-permute-start.1 = (bf16[256,384]{1,0:T(8,128)(2,1)S(1)}, bf16[256,384]{1,0:T(8,128)(2,1)S(1)}, u32[]{:S(2)}, u32[]{:S(2)}) collective-permute-start(bf16[256,384]{1,0:T(8,128)(2,1)S(1)} %copy-done.5), channel_id=1, source_target_pairs={{0,64},{64,0},{1,65},{65,1},{2,66},{66,2},{3,67},{67,3},{4,68},{68... | collective-permute-start | bytes 589832 | tf_op jit(solution)/shard_map/ppermute | solution.py:206

commit v4 on v3

--- a/solution.py
+++ b/solution.py
@@ -12,13 +12,12 @@
 LANES = 128
 BLOCK = 2 * LANES
 GROUPS = 5
-TILES = 32
+TILES = 24
 
 AXES = ("y", "core", "x", "zh", "zl")
 ZAX = ("zh", "zl")
 TM = ("x", "zh", "zl")
-NEAR = ("x", "zl")
-PARAMS = pltpu.CompilerParams(vmem_limit_bytes=40 * 1024 * 1024)
+PARAMS = pltpu.CompilerParams(vmem_limit_bytes=16 * 1024 * 1024)
 
 
 def cost(flops, nbytes):
@@ -51,39 +50,32 @@
 
 
 def project_kernel(mine_ref, theirs_ref, weight_ref, *out_refs):
-    core = lax.axis_index("core")
-    weight = weight_ref[0]
+    first = lax.axis_index("core") == 0
     split = GROUPS * LANES
-    for tokens_ref, main_ref, rest_ref in (
-        (mine_ref, out_refs[0], out_refs[1]),
-        (theirs_ref, out_refs[2], out_refs[3]),
-    ):
-        proj = jnp.dot(tokens_ref[...], weight, preferred_element_type=jnp.float32)
-        feat = jnp.where(proj > 0, proj, jnp.exp(jnp.minimum(proj, 0.0)) - 1.0) + 1.0
-        unit = 2 * pl.program_id(0) + lax.broadcasted_iota(jnp.int32, proj.shape, 1) // LANES
-        plain = jnp.logical_and(unit < GROUPS, core == 0)
-        proj = jnp.where(plain, proj, feat).astype(jnp.bfloat16)
-        for step in range(4):
-
-            @pl.when(pl.program_id(0) == step)
-            def _():
-                for half in range(2):
-                    at = step * BLOCK + half * LANES
-                    ref = main_ref if at < split else rest_ref
-                    at = at if at < split else at - split
-                    ref[:, at : at + LANES] = proj[:, half * LANES : (half + 1) * LANES]
+    for step in range(weight_ref.shape[0]):
+        weight = weight_ref[step]
+        for tokens_ref, main_ref, rest_ref in (
+            (mine_ref, out_refs[0], out_refs[1]),
+            (theirs_ref, out_refs[2], out_refs[3]),
+        ):
+            both = jnp.dot(tokens_ref[...], weight, preferred_element_type=jnp.float32)
+            for half in range(2):
+                at = step * BLOCK + half * LANES
+                proj = both[:, half * LANES : (half + 1) * LANES]
+                feat = jnp.where(proj > 0, proj, jnp.exp(jnp.minimum(proj, 0.0)) - 1.0) + 1.0
+                if at < split:
+                    feat = jnp.where(first, proj, feat).astype(jnp.bfloat16)
+                    main_ref[:, at : at + LANES] = feat
+                else:
+                    rest_ref[:, at - split : at - split + LANES] = feat.astype(jnp.bfloat16)
 
 
 def project(mine, theirs, weights):
     steps, depth, _ = weights.shape
     rows = mine.shape[0]
     widths = (GROUPS * LANES, steps * BLOCK - GROUPS * LANES) * 2
-    tokens = pl.BlockSpec((rows, depth), lambda i: (0, 0))
     return pl.pallas_call(
         project_kernel,
-        grid=(steps,),
-        in_specs=[tokens, tokens, pl.BlockSpec((1, depth, BLOCK), lambda i: (i, 0, 0))],
-        out_specs=[pl.BlockSpec((rows, width), lambda i: (0, 0)) for width in widths],
         out_shape=[jax.ShapeDtypeStruct((rows, width), jnp.bfloat16) for width in widths],
         compiler_params=PARAMS,
         cost_estimate=cost(4 * rows * depth * steps * BLOCK, 5 * 1024 * 1024),
@@ -206,24 +198,44 @@
     return lax.ppermute(block, "core", [(0, 1), (1, 0)])
 
 
-def gather_weights(w_query, w_key, w_value):
+def pick_kernel(value_ref, key_ref, query_ref, out_ref, held):
+    width = GROUPS * LANES
+    cut = 3 * LANES
+    query = query_ref[...].astype(jnp.float32)
+    held[:, :width] = value_ref[...].astype(jnp.float32)
+    held[:, width : width + cut] = query[:, :cut]
+    held[:, width + cut : 2 * width + cut] = key_ref[...].astype(jnp.float32)
+    held[:, 2 * width + cut : 3 * width] = query[:, cut:]
+    held[:, 3 * width :] = jnp.zeros((held.shape[0], LANES), jnp.float32)
+    place = 4 * lax.axis_index("core") + lax.axis_index("y")
+    mine = held[:, pl.ds(pl.multiple_of(place * BLOCK, BLOCK), BLOCK)]
+    mine = jnp.concatenate([mine[:, :LANES], mine[:, LANES:]], axis=0).astype(jnp.bfloat16)
+    for i in range(out_ref.shape[0]):
+        out_ref[i] = mine
+
+
+def pick(w_value, w_key, w_query, copies):
+    rows, width = w_query.shape
+    return pl.pallas_call(
+        pick_kernel,
+        out_shape=jax.ShapeDtypeStruct((copies, 2 * rows, LANES), jnp.bfloat16),
+        scratch_shapes=[pltpu.VMEM((rows, 3 * width + LANES), jnp.float32)],
+        compiler_params=PARAMS,
+        cost_estimate=cost(0, 4 * 1024 * rows),
+        name="pick",
+    )(w_value, w_key, w_query)
+
+
+def body(tokens, gain, w_query, w_key, w_value, conv_weight):
     rows = w_query.shape[0]
-    pad = jnp.zeros((rows, LANES), w_query.dtype)
-    cut = 3 * LANES
-    cat = jnp.concatenate([w_value, w_query[:, :cut], w_key, w_query[:, cut:], pad], axis=1)
-    place = 4 * lax.axis_index("core") + lax.axis_index("y")
-    mine = lax.dynamic_slice_in_dim(cat, place * BLOCK, BLOCK, axis=1)
-    mine = jnp.concatenate([mine[:, :LANES], mine[:, LANES:]], axis=0)
-    column = spread(mine, ZAX)
-    column = jnp.concatenate([column[:, :rows], column[:, rows:]], axis=2)
-    column = column.reshape(column.shape[0] * rows, BLOCK)
-    return spread(column, ("y", "x")).reshape(lax.axis_size("y"), -1, BLOCK)
-
-
-def body(tokens, gain, w_query, w_key, w_value, conv_weight):
     normed = norm(tokens, gain)
-    weights = gather_weights(w_query, w_key, w_value)
-    main, rest, their_main, their_rest = project(normed, swap(normed), weights)
+    other = swap(normed)
+    column = exchange(pick(w_value, w_key, w_query, lax.axis_size(ZAX)), ZAX)
+    column = jnp.concatenate([column[:, :rows], column[:, rows:]], axis=2).reshape(-1, BLOCK)
+    column, other = lax.optimization_barrier((column, other))
+    weights = spread(column, ("y", "x")).reshape(lax.axis_size("y"), -1, BLOCK)
+
+    main, rest, their_main, their_rest = project(normed, other, weights)
     values, tiles = states(main, swap(their_main))
     their_rest = swap(their_rest)
     count = lax.axis_size(TM)
@@ -231,12 +243,12 @@
     after = lax.ppermute(values, TM, [(i + 1, i) for i in range(count - 1)])
     local = convolve(before, values, after, conv_weight)
 
-    near = lax.axis_size(NEAR)
-    shape = (near, TILES // near) + tiles.shape[1:]
-    part = jnp.sum(exchange(tiles, NEAR).reshape(shape), axis=0)
-    part = jnp.sum(spread(part, "zh"), axis=0)
+    share = TILES // lax.axis_size("x")
+    part = jnp.sum(exchange(tiles, "x").reshape((-1, share) + tiles.shape[1:]), axis=0)
+    part = spread(part.astype(jnp.bfloat16).reshape(-1, LANES), ZAX)
+    part = jnp.sum(part.astype(jnp.float32), axis=0)
     part, local = lax.optimization_barrier((part, local))
-    tiles = spread(part, NEAR).reshape(tiles.shape)
+    tiles = spread(part.reshape((share,) + tiles.shape[1:]), "x").reshape(tiles.shape)
     return attend(rest, their_rest, tiles, local)
 
 

time: 133 us -> 122 us (0.917)
  waiting for transfers between devices: 42 us -> 27.1 us
  blocking collectives: 30.6 us -> 41.8 us
  local copies, waits for them, and re-layouts: 8.6 us -> 5.67 us
  Pallas kernels: 8.63 us -> 6.15 us
  starting transfers between devices: 42.1 us -> 40.6 us
    all_to_all x4 -> x3, waiting for transfers between devices: 37 us -> 16.1 us  [exchange(): return lax.all_to_all(blocks, axes, 0, 0, tiled=True)]
    all_to_all x1 -> x2, blocking collectives: 30.6 us -> 41.8 us  [exchange(): return lax.all_to_all(blocks, axes, 0, 0, tiled=True)]
    ppermute x1, waiting for transfers between devices: 0.01 us -> 7.16 us  [body(): after = lax.ppermute(values, TM, [(i + 1, i) for i in range(count - 1)])]
    ppermute x3, waiting for transfers between devices: 4.97 us -> 1.6 us  [swap(): return lax.ppermute(block, 'core', [(0, 1), (1, 0)])]
    ppermute x1, waiting for transfers between devices: 0.01 us -> 2.33 us  [body(): before = lax.ppermute(values, TM, [(i, i + 1) for i in range(count - 1)])]
    unnamed x18 -> x10, local copies, waits for them, and re-layouts: 5.52 us -> 3.32 us
    pallas_call x1 -> x2, Pallas kernels: 4.21 us -> 2.42 us  [the longest x1 1.73 us: project(): pl.pallas_call(project_kernel, out_shape=[jax.ShapeDtypeStruct((rows, wid...]
    broadcast_in_dim x5 -> x3, local copies, waits for them, and re-layouts: 3.03 us -> 1.57 us  [spread(): return exchange(jnp.broadcast_to(block[None], (count,) + block.shape), axes)]
  transfers between devices with their start and end apart: 9 -> 8, of which waited for: 6 -> 5; matrix products, arithmetic and copies ran while one was open for 0% -> 1% of each run, Pallas kernels for 1% -> 2%
where the time goes in v4:
time: 122 us
  blocking collectives  41.8 us (34%)
  starting transfers between devices  40.6 us (33%)
  waiting for transfers between devices  27.1 us (22%)
  Pallas kernels  6.15 us (5%)
  local copies, waits for them, and re-layouts  5.67 us (5%)
    all_to_all x2, blocking collectives, exchange(): return lax.all_to_all(blocks, axes, 0, 0, tiled=True)  41.8 us
    all_to_all x3, starting transfers between devices, exchange(): return lax.all_to_all(blocks, axes, 0, 0, tiled=True)  27 us
    all_to_all x3, waiting for transfers between devices, exchange(): return lax.all_to_all(blocks, axes, 0, 0, tiled=True)  16.1 us
    ppermute x1, waiting for transfers between devices, body(): after = lax.ppermute(values, TM, [(i + 1, i) for i in range(count - 1)])  7.16 us
    ppermute x1, starting transfers between devices, body(): after = lax.ppermute(values, TM, [(i + 1, i) for i in range(count - 1)])  5.94 us
    ppermute x3, starting transfers between devices, swap(): return lax.ppermute(block, 'core', [(0, 1), (1, 0)])  5.76 us
    unnamed x10, local copies, waits for them, and re-layouts  3.32 us
  transfers between devices with their start and end apart: 8, of which 5 were waited for; matrix products, arithmetic and copies ran while one was open for 1% of the time, Pallas kernels for 2%

profile of v4, /device:TPU:2, one launch (start us, length us, event | category | flops | bytes accessed | tf_op | source)
XLA Modules:
  0.0 121.6 jit_solution(6052757255372905536)
XLA Ops:
  0.0 0.8 copy-done.2
  0.8 0.8 copy-done.3
  1.5 0.8 copy-done.4
  2.3 0.7 pick.1
  3.0 15.2 %all-to-all-start = ((bf16[16,36,128]{2,1,0:T(8,128)(2,1)}), bf16[16,36,128]{2,1,0:T(8,128)(2,1)S(1)}, u32[]{:S(2)}, u32[]{:S(2)}) async-start(bf16[16,36,128]{2,1,0:T(8,128)(2,1)} %pick.1), calls=%async_computation | async-start | bytes 327680 | tf_op jit(solution)/shard_map/all_to_all | solution.py:28
  18.2 0.7 reshape.23.gain_ref
  18.9 1.1 copy-done
  19.9 0.2 norm.1.mine_ref
  20.2 1.9 %collective-permute-start = (bf16[256,1152]{1,0:T(8,128)(2,1)S(1)}, bf16[256,1152]{1,0:T(8,128)(2,1)S(1)}, u32[]{:S(2)}, u32[]{:S(2)}) collective-permute-start(bf16[256,1152]{1,0:T(8,128)(2,1)S(1)} %norm.1.mine_ref), channel_id=1, source_target_pairs={{0,64},{64,0},{1,65},{65,1},{2,66},{66,2},{3,67},{67,3},{4,68},{68... | collective-permute-start | bytes 1769480 | tf_op jit(solution)/shard_map/ppermute | solution.py:198
  22.1 11.7 %all-to-all-done = bf16[16,36,128]{2,1,0:T(8,128)(2,1)S(1)} async-done(((bf16[16,36,128]{2,1,0:T(8,128)(2,1)}), bf16[16,36,128]{2,1,0:T(8,128)(2,1)S(1)}, u32[]{:S(2)}, u32[]{:S(2)}) %all-to-all-start) | async-done | bytes 147488 | tf_op jit(solution)/shard_map/all_to_all | solution.py:28
  33.9 0.1 reshape.24
  33.9 0.0 collective-permute-done.theirs_ref
  33.9 0.2 broadcast_in_dim.8
  34.2 33.6 %all_to_all.25 = bf16[16,288,256]{2,1,0:T(8,128)(2,1)S(1)} all-to-all(bf16[16,288,256]{2,1,0:T(8,128)(2,1)S(1)} %broadcast_in_dim.8), channel_id=1, replica_groups=mesh['y'=4,'core'=2,'x'=4,'zh'=4,'zl'=4] {'y','x'}, dimensions={0} | all-to-all | bytes 4718592 | tf_op jit(solution)/shard_map/all_to_all | solution.py:28
  67.8 1.7 %project.1 = (bf16[256,640]{1,0:T(8,128)(2,1)S(1)}, bf16[256,384]{1,0:T(8,128)(2,1)S(1)}, bf16[256,640]{1,0:T(8,128)(2,1)S(1)}, bf16[256,384]{1,0:T(8,128)(2,1)S(1)}) custom-call(bf16[256,1152]{1,0:T(8,128)(2,1)S(1)} %norm.1.mine_ref, bf16[256,1152]{1,0:T(8,128)(2,1)S(1)} %collective-permute-done.theirs_ref, bf16[4,1152,256]{2,1,0:T(8,128)(2,1)S(1)} %bitcast.7), custom_call_target="tpu_custom_call" | custom-call | flops 1207959552 | bytes 5242880 | tf_op jit(solution)/shard_map/project/pallas_call | solution.py:77
  69.5 1.9 %collective-permute-start.2 = (bf16[256,640]{1,0:T(8,128)(2,1)S(1)}, bf16[256,640]{1,0:T(8,128)(2,1)S(1)}, u32[]{:S(2)}, u32[]{:S(2)}) collective-permute-start(bf16[256,640]{1,0:T(8,128)(2,1)S(1)} %get-tuple-element.20), channel_id=1, source_target_pairs={{0,64},{64,0},{1,65},{65,1},{2,66},{66,2},{3,67},{67,3},{4,68},{68... | collective-permute-start | bytes 983048 | tf_op jit(solution)/shard_map/ppermute | solution.py:198
  71.5 1.6 %collective-permute-done.2.theirs_ref = bf16[256,640]{1,0:T(8,128)(2,1)S(1)} collective-permute-done((bf16[256,640]{1,0:T(8,128)(2,1)S(1)}, bf16[256,640]{1,0:T(8,128)(2,1)S(1)}, u32[]{:S(2)}, u32[]{:S(2)}) %collective-permute-start.2) | collective-permute-done | bytes 327712 | tf_op jit(solution)/shard_map/ppermute | solution.py:198
  73.1 0.3 states.1
  73.4 8.2 %all_to_all.26 = f32[24,8,128]{2,1,0:T(8,128)S(1)} all-to-all(f32[24,8,128]{2,1,0:T(8,128)S(1)} %get-tuple-element.21), channel_id=1, replica_groups=mesh['y'=4,'core'=2,'x'=4,'zh'=4,'zl'=4] {'x'}, dimensions={0} | all-to-all | bytes 196608 | tf_op jit(solution)/shard_map/all_to_all | solution.py:28
  81.6 0.7 broadcast_in_dim.9
  82.3 7.8 %all-to-all-start.3 = ((bf16[16,48,128]{2,1,0:T(8,128)(2,1)}), bf16[16,48,128]{2,1,0:T(8,128)(2,1)S(1)}, u32[]{:S(2)}, u32[]{:S(2)}) async-start(bf16[16,48,128]{2,1,0:T(8,128)(2,1)} %broadcast_in_dim.9), calls=%async_computation.3 | async-start | bytes 393216 | tf_op jit(solution)/shard_map/all_to_all | solution.py:28
  90.1 5.9 %collective-permute-start.4 = (bf16[256,640]{1,0:T(8,128)(2,1)S(1)}, bf16[256,640]{1,0:T(8,128)(2,1)S(1)}, u32[]{:S(2)}, u32[]{:S(2)}) collective-permute-start(bf16[256,640]{1,0:T(8,128)(2,1)S(1)} %get-tuple-element.22.values_ref), channel_id=1, source_target_pairs={{1,0},{2,1},{3,2},{4,3},{5,4},{6,5},{7,6},{8,7},{9,8},{10,9},{11,1... | collective-permute-start | bytes 983048 | tf_op jit(solution)/shard_map/ppermute | solution.py:243
  96.0 1.9 %collective-permute-start.3 = (bf16[256,640]{1,0:T(8,128)(2,1)S(1)}, bf16[256,640]{1,0:T(8,128)(2,1)S(1)}, u32[]{:S(2)}, u32[]{:S(2)}) collective-permute-start(bf16[256,640]{1,0:T(8,128)(2,1)S(1)} %get-tuple-element.22.values_ref), channel_id=1, source_target_pairs={{0,1},{1,2},{2,3},{3,4},{4,5},{5,6},{6,7},{7,8},{8,9},{9,10},{10,1... | collective-permute-start | bytes 983048 | tf_op jit(solution)/shard_map/ppermute | solution.py:242
  98.0 1.9 %collective-permute-start.1 = (bf16[256,384]{1,0:T(8,128)(2,1)S(1)}, bf16[256,384]{1,0:T(8,128)(2,1)S(1)}, u32[]{:S(2)}, u32[]{:S(2)}) collective-permute-start(bf16[256,384]{1,0:T(8,128)(2,1)S(1)} %get-tuple-element.18), channel_id=1, source_target_pairs={{0,64},{64,0},{1,65},{65,1},{2,66},{66,2},{3,67},{67,3},{4,68},{68... | collective-permute-start | bytes 589832 | tf_op jit(solution)/shard_map/ppermute | solution.py:198
  99.9 7.2 %collective-permute-done.4.after_ref = bf16[256,640]{1,0:T(8,128)(2,1)S(1)} collective-permute-done((bf16[256,640]{1,0:T(8,128)(2,1)S(1)}, bf16[256,640]{1,0:T(8,128)(2,1)S(1)}, u32[]{:S(2)}, u32[]{:S(2)}) %collective-permute-start.4) | collective-permute-done | bytes 327712 | tf_op jit(solution)/shard_map/ppermute | solution.py:243
  107.1 2.3 %collective-permute-done.3.before_ref = bf16[256,640]{1,0:T(8,128)(2,1)S(1)} collective-permute-done((bf16[256,640]{1,0:T(8,128)(2,1)S(1)}, bf16[256,640]{1,0:T(8,128)(2,1)S(1)}, u32[]{:S(2)}, u32[]{:S(2)}) %collective-permute-start.3) | collective-permute-done | bytes 327712 | tf_op jit(solution)/shard_map/ppermute | solution.py:242
  109.4 1.7 %convolve.1.local_ref = f32[256,640]{1,0:T(8,128)S(1)} custom-call(bf16[256,640]{1,0:T(8,128)(2,1)S(1)} %collective-permute-done.3.before_ref, bf16[256,640]{1,0:T(8,128)(2,1)S(1)} %get-tuple-element.22.values_ref, bf16[256,640]{1,0:T(8,128)(2,1)S(1)} %collective-permute-done.4.after_ref, bf16[27,640]{1,0:T(8,128)(2,1)S(1)} %copy-done.1), custom_call_target="tpu_custom_call" | custom-call | flops 8847360 | bytes 2097152 | tf_op jit(solution)/shard_map/convolve/pallas_call | solution.py:148
  111.2 0.6 broadcast_in_dim.21
  111.8 4.0 %all-to-all-start.4 = ((f32[4,6,8,128]{3,2,1,0:T(8,128)}), f32[4,6,8,128]{3,2,1,0:T(8,128)S(1)}, u32[]{:S(2)}, u32[]{:S(2)}) async-start(f32[4,6,8,128]{3,2,1,0:T(8,128)} %broadcast_in_dim.21), calls=%async_computation.4 | async-start | bytes 196608 | tf_op jit(solution)/shard_map/all_to_all | solution.py:28
  115.8 0.0 collective-permute-done.1.theirs_ref
  115.8 4.3 %all-to-all-done.4 = f32[4,6,8,128]{3,2,1,0:T(8,128)S(1)} async-done(((f32[4,6,8,128]{3,2,1,0:T(8,128)}), f32[4,6,8,128]{3,2,1,0:T(8,128)S(1)}, u32[]{:S(2)}, u32[]{:S(2)}) %all-to-all-start.4) | async-done | bytes 98336 | tf_op jit(solution)/shard_map/all_to_all | solution.py:28
  120.2 1.4 %attend.1 = f32[256,640]{1,0:T(8,128)} custom-call(bf16[256,384]{1,0:T(8,128)(2,1)S(1)} %get-tuple-element.17.mine_ref, bf16[256,384]{1,0:T(8,128)(2,1)S(1)} %collective-permute-done.1.theirs_ref, f32[24,8,128]{2,1,0:T(8,128)S(1)} %bitcast.8, f32[256,640]{1,0:T(8,128)S(1)} %convolve.1.local_ref), custom_call_target="tpu_custom_call" | custom-call | flops 167772160 | bytes 3145728 | tf_op jit(solution)/shard_map/attend/pallas_call | solution.py:188
  (11 shorter events, 0.1 us)
Async XLA Ops:
  0.0 0.8 copy-start.2
  0.8 0.8 copy-start.3
  1.5 0.8 copy-start.4
  3.0 30.8 %all-to-all-start = ((bf16[16,36,128]{2,1,0:T(8,128)(2,1)}), bf16[16,36,128]{2,1,0:T(8,128)(2,1)S(1)}, u32[]{:S(2)}, u32[]{:S(2)}) async-start(bf16[16,36,128]{2,1,0:T(8,128)(2,1)} %pick.1), calls=%async_computation | async-start | bytes 327680 | tf_op jit(solution)/shard_map/all_to_all | solution.py:28
  18.9 1.1 copy-start
  20.2 13.8 %collective-permute-start = (bf16[256,1152]{1,0:T(8,128)(2,1)S(1)}, bf16[256,1152]{1,0:T(8,128)(2,1)S(1)}, u32[]{:S(2)}, u32[]{:S(2)}) collective-permute-start(bf16[256,1152]{1,0:T(8,128)(2,1)S(1)} %norm.1.mine_ref), channel_id=1, source_target_pairs={{0,64},{64,0},{1,65},{65,1},{2,66},{66,2},{3,67},{67,3},{4,68},{68... | collective-permute-start | bytes 1769480 | tf_op jit(solution)/shard_map/ppermute | solution.py:198
  67.8 41.6 %copy-start.1 = (bf16[27,640]{1,0:T(8,128)(2,1)S(1)}, bf16[27,640]{1,0:T(8,128)(2,1)}, u32[]{:S(2)}) copy-start(bf16[27,640]{1,0:T(8,128)(2,1)} %weight_ref.1) | copy-start | bytes 103684
  69.5 3.5 %collective-permute-start.2 = (bf16[256,640]{1,0:T(8,128)(2,1)S(1)}, bf16[256,640]{1,0:T(8,128)(2,1)S(1)}, u32[]{:S(2)}, u32[]{:S(2)}) collective-permute-start(bf16[256,640]{1,0:T(8,128)(2,1)S(1)} %get-tuple-element.20), channel_id=1, source_target_pairs={{0,64},{64,0},{1,65},{65,1},{2,66},{66,2},{3,67},{67,3},{4,68},{68... | collective-permute-start | bytes 983048 | tf_op jit(solution)/shard_map/ppermute | solution.py:198
  82.3 28.8 %all-to-all-start.3 = ((bf16[16,48,128]{2,1,0:T(8,128)(2,1)}), bf16[16,48,128]{2,1,0:T(8,128)(2,1)S(1)}, u32[]{:S(2)}, u32[]{:S(2)}) async-start(bf16[16,48,128]{2,1,0:T(8,128)(2,1)} %broadcast_in_dim.9), calls=%async_computation.3 | async-start | bytes 393216 | tf_op jit(solution)/shard_map/all_to_all | solution.py:28
  90.1 17.0 %collective-permute-start.4 = (bf16[256,640]{1,0:T(8,128)(2,1)S(1)}, bf16[256,640]{1,0:T(8,128)(2,1)S(1)}, u32[]{:S(2)}, u32[]{:S(2)}) collective-permute-start(bf16[256,640]{1,0:T(8,128)(2,1)S(1)} %get-tuple-element.22.values_ref), channel_id=1, source_target_pairs={{1,0},{2,1},{3,2},{4,3},{5,4},{6,5},{7,6},{8,7},{9,8},{10,9},{11,1... | collective-permute-start | bytes 983048 | tf_op jit(solution)/shard_map/ppermute | solution.py:243
  96.0 13.3 %collective-permute-start.3 = (bf16[256,640]{1,0:T(8,128)(2,1)S(1)}, bf16[256,640]{1,0:T(8,128)(2,1)S(1)}, u32[]{:S(2)}, u32[]{:S(2)}) collective-permute-start(bf16[256,640]{1,0:T(8,128)(2,1)S(1)} %get-tuple-element.22.values_ref), channel_id=1, source_target_pairs={{0,1},{1,2},{2,3},{3,4},{4,5},{5,6},{6,7},{7,8},{8,9},{9,10},{10,1... | collective-permute-start | bytes 983048 | tf_op jit(solution)/shard_map/ppermute | solution.py:242
  98.0 17.9 %collective-permute-start.1 = (bf16[256,384]{1,0:T(8,128)(2,1)S(1)}, bf16[256,384]{1,0:T(8,128)(2,1)S(1)}, u32[]{:S(2)}, u32[]{:S(2)}) collective-permute-start(bf16[256,384]{1,0:T(8,128)(2,1)S(1)} %get-tuple-element.18), channel_id=1, source_target_pairs={{0,64},{64,0},{1,65},{65,1},{2,66},{66,2},{3,67},{67,3},{4,68},{68... | collective-permute-start | bytes 589832 | tf_op jit(solution)/shard_map/ppermute | solution.py:198
  111.8 8.4 %all-to-all-start.4 = ((f32[4,6,8,128]{3,2,1,0:T(8,128)}), f32[4,6,8,128]{3,2,1,0:T(8,128)S(1)}, u32[]{:S(2)}, u32[]{:S(2)}) async-start(f32[4,6,8,128]{3,2,1,0:T(8,128)} %broadcast_in_dim.21), calls=%async_computation.4 | async-start | bytes 196608 | tf_op jit(solution)/shard_map/all_to_all | solution.py:28

commit v5 on v4

--- a/solution.py
+++ b/solution.py
@@ -49,49 +49,45 @@
     )(tokens, gain.reshape(1, -1))
 
 
-def project_kernel(mine_ref, theirs_ref, weight_ref, *out_refs):
+def project_kernel(mine_ref, theirs_ref, weight_ref, own_ref, other_ref):
     first = lax.axis_index("core") == 0
-    split = GROUPS * LANES
     for step in range(weight_ref.shape[0]):
         weight = weight_ref[step]
-        for tokens_ref, main_ref, rest_ref in (
-            (mine_ref, out_refs[0], out_refs[1]),
-            (theirs_ref, out_refs[2], out_refs[3]),
-        ):
+        for tokens_ref, out_ref in ((mine_ref, own_ref), (theirs_ref, other_ref)):
             both = jnp.dot(tokens_ref[...], weight, preferred_element_type=jnp.float32)
             for half in range(2):
-                at = step * BLOCK + half * LANES
+                unit = 2 * step + half
                 proj = both[:, half * LANES : (half + 1) * LANES]
                 feat = jnp.where(proj > 0, proj, jnp.exp(jnp.minimum(proj, 0.0)) - 1.0) + 1.0
-                if at < split:
-                    feat = jnp.where(first, proj, feat).astype(jnp.bfloat16)
-                    main_ref[:, at : at + LANES] = feat
-                else:
-                    rest_ref[:, at - split : at - split + LANES] = feat.astype(jnp.bfloat16)
+                if unit < GROUPS:
+                    feat = jnp.where(first, proj, feat)
+                out_ref[:, unit * LANES : (unit + 1) * LANES] = feat.astype(jnp.bfloat16)
 
 
 def project(mine, theirs, weights):
     steps, depth, _ = weights.shape
     rows = mine.shape[0]
-    widths = (GROUPS * LANES, steps * BLOCK - GROUPS * LANES) * 2
     return pl.pallas_call(
         project_kernel,
-        out_shape=[jax.ShapeDtypeStruct((rows, width), jnp.bfloat16) for width in widths],
+        out_shape=[jax.ShapeDtypeStruct((rows, steps * BLOCK), jnp.bfloat16)] * 2,
         compiler_params=PARAMS,
         cost_estimate=cost(4 * rows * depth * steps * BLOCK, 5 * 1024 * 1024),
         name="project",
     )(mine, theirs, weights)
 
 
+def unit_of(core, mine_ref, theirs_ref, unit):
+    at = slice(unit * LANES, (unit + 1) * LANES)
+    return jnp.where(lax.axis_index("core") == core, mine_ref[:, at], theirs_ref[:, at])
+
+
 def state_kernel(mine_ref, theirs_ref, values_ref, tiles_ref):
-    first = lax.axis_index("core") == 0
     lane = lax.broadcasted_iota(jnp.int32, (HEAD_WIDTH, LANES), 1) // HEAD_WIDTH
     tiles_ref[...] = jnp.zeros_like(tiles_ref)
     for g in range(GROUPS):
-        cols = slice(g * LANES, (g + 1) * LANES)
-        values = jnp.where(first, mine_ref[:, cols], theirs_ref[:, cols])
-        kfeat = jnp.where(first, theirs_ref[:, cols], mine_ref[:, cols])
-        values_ref[:, cols] = values
+        values = unit_of(0, mine_ref, theirs_ref, g)
+        kfeat = unit_of(1, mine_ref, theirs_ref, 2 + g)
+        values_ref[:, g * LANES : (g + 1) * LANES] = values
         square = lax.dot_general(
             kfeat, values, (((0,), (0,)), ((), ())), preferred_element_type=jnp.float32
         )
@@ -166,14 +162,12 @@
 
 
 def attend_kernel(mine_ref, theirs_ref, tiles_ref, local_ref, out_ref):
-    first = lax.axis_index("core") == 0
     row = lax.broadcasted_iota(jnp.int32, (LANES, LANES), 0) // HEAD_WIDTH
     lane = lax.broadcasted_iota(jnp.int32, (LANES, LANES), 1) // HEAD_WIDTH
     same = row == lane
     for g in range(GROUPS):
-        early, late = (mine_ref, theirs_ref) if g < 3 else (theirs_ref, mine_ref)
-        at = slice(g % 3 * LANES, (g % 3 + 1) * LANES)
-        qfeat = jnp.where(first, early[:, at], late[:, at])
+        core, unit = (0, GROUPS + g) if g < 3 else (1, g - 3)
+        qfeat = unit_of(core, mine_ref, theirs_ref, unit)
         packed = tiles_ref[4 * g : 4 * g + 4].reshape(HEAD_WIDTH, LANES)
         state = jnp.where(same, jnp.concatenate([packed] * 4, axis=0), 0.0)
         ksum = jnp.broadcast_to(tiles_ref[4 * GROUPS, g : g + 1, :], (LANES, LANES)).T
@@ -198,58 +192,39 @@
     return lax.ppermute(block, "core", [(0, 1), (1, 0)])
 
 
-def pick_kernel(value_ref, key_ref, query_ref, out_ref, held):
-    width = GROUPS * LANES
-    cut = 3 * LANES
-    query = query_ref[...].astype(jnp.float32)
-    held[:, :width] = value_ref[...].astype(jnp.float32)
-    held[:, width : width + cut] = query[:, :cut]
-    held[:, width + cut : 2 * width + cut] = key_ref[...].astype(jnp.float32)
-    held[:, 2 * width + cut : 3 * width] = query[:, cut:]
-    held[:, 3 * width :] = jnp.zeros((held.shape[0], LANES), jnp.float32)
+def pick(w_query, w_key, w_value):
+    pad = jnp.zeros((w_query.shape[0], LANES), w_query.dtype)
+    cat = jnp.concatenate([w_value, w_query, w_key, pad], axis=1)
     place = 4 * lax.axis_index("core") + lax.axis_index("y")
-    mine = held[:, pl.ds(pl.multiple_of(place * BLOCK, BLOCK), BLOCK)]
-    mine = jnp.concatenate([mine[:, :LANES], mine[:, LANES:]], axis=0).astype(jnp.bfloat16)
-    for i in range(out_ref.shape[0]):
-        out_ref[i] = mine
-
-
-def pick(w_value, w_key, w_query, copies):
-    rows, width = w_query.shape
-    return pl.pallas_call(
-        pick_kernel,
-        out_shape=jax.ShapeDtypeStruct((copies, 2 * rows, LANES), jnp.bfloat16),
-        scratch_shapes=[pltpu.VMEM((rows, 3 * width + LANES), jnp.float32)],
-        compiler_params=PARAMS,
-        cost_estimate=cost(0, 4 * 1024 * rows),
-        name="pick",
-    )(w_value, w_key, w_query)
+    mine = lax.dynamic_slice_in_dim(cat, place * BLOCK, BLOCK, axis=1)
+    return jnp.concatenate([mine[:, :LANES], mine[:, LANES:]], axis=0)
 
 
 def body(tokens, gain, w_query, w_key, w_value, conv_weight):
     rows = w_query.shape[0]
     normed = norm(tokens, gain)
     other = swap(normed)
-    column = exchange(pick(w_value, w_key, w_query, lax.axis_size(ZAX)), ZAX)
+    column = spread(pick(w_query, w_key, w_value), ZAX)
     column = jnp.concatenate([column[:, :rows], column[:, rows:]], axis=2).reshape(-1, BLOCK)
     column, other = lax.optimization_barrier((column, other))
     weights = spread(column, ("y", "x")).reshape(lax.axis_size("y"), -1, BLOCK)
 
-    main, rest, their_main, their_rest = project(normed, other, weights)
-    values, tiles = states(main, swap(their_main))
-    their_rest = swap(their_rest)
+    mine, theirs = project(normed, other, weights)
+    theirs = swap(theirs)
+    values, tiles = states(mine, theirs)
     count = lax.axis_size(TM)
     before = lax.ppermute(values, TM, [(i, i + 1) for i in range(count - 1)])
     after = lax.ppermute(values, TM, [(i + 1, i) for i in range(count - 1)])
-    local = convolve(before, values, after, conv_weight)
 
     share = TILES // lax.axis_size("x")
     part = jnp.sum(exchange(tiles, "x").reshape((-1, share) + tiles.shape[1:]), axis=0)
-    part = spread(part.astype(jnp.bfloat16).reshape(-1, LANES), ZAX)
-    part = jnp.sum(part.astype(jnp.float32), axis=0)
+    part = part.astype(jnp.bfloat16).reshape(-1, LANES)
+    part, before, after = lax.optimization_barrier((part, before, after))
+    local = convolve(before, values, after, conv_weight)
+    part = jnp.sum(spread(part, ZAX).astype(jnp.float32), axis=0)
     part, local = lax.optimization_barrier((part, local))
     tiles = spread(part.reshape((share,) + tiles.shape[1:]), "x").reshape(tiles.shape)
-    return attend(rest, their_rest, tiles, local)
+    return attend(mine, theirs, tiles, local)
 
 
 def solution(mesh):

time: 122 us -> 125 us (1.025)
  the two profiles are of different devices: /device:TPU:2 before, /device:TPU:32 now
where the time goes in v5:
time: 125 us; the launch traced here: 124 us
  blocking collectives  52.9 us (42%)
  starting transfers between devices  34.6 us (28%)
  waiting for transfers between devices  26.9 us (22%)
  Pallas kernels  5.43 us (4%)
  local copies, waits for them, and re-layouts  3.55 us (3%)
    all_to_all x3, blocking collectives, exchange(): return lax.all_to_all(blocks, axes, 0, 0, tiled=True)  52.9 us
    all_to_all x2, waiting for transfers between devices, exchange(): return lax.all_to_all(blocks, axes, 0, 0, tiled=True)  25 us
    all_to_all x2, starting transfers between devices, exchange(): return lax.all_to_all(blocks, axes, 0, 0, tiled=True)  24.9 us
    ppermute x1, starting transfers between devices, body(): before = lax.ppermute(values, TM, [(i, i + 1) for i in range(count - 1)])  3.92 us
    ppermute x2, starting transfers between devices, swap(): return lax.ppermute(block, 'core', [(0, 1), (1, 0)])  3.84 us
  transfers between devices with their start and end apart: 6, of which 3 were waited for; matrix products, arithmetic and copies ran while one was open for 1% of the time, Pallas kernels for 2%

profile of v5, /device:TPU:32, one launch (start us, length us, event | category | flops | bytes accessed | tf_op | source)
XLA Modules:
  0.0 124.2 jit_solution(12163607422148322080)
XLA Ops:
  0.0 0.1 pad_dynamic-slice_fusion.3
  0.1 0.7 fusion.2
  0.8 0.7 broadcast_in_dim.13
  1.5 15.2 %all-to-all-start = ((bf16[16,36,128]{2,1,0:T(8,128)(2,1)}), bf16[16,36,128]{2,1,0:T(8,128)(2,1)S(1)}, u32[]{:S(2)}, u32[]{:S(2)}) async-start(bf16[16,36,128]{2,1,0:T(8,128)(2,1)} %broadcast_in_dim.13), calls=%async_computation | async-start | bytes 327680 | tf_op jit(solution)/shard_map/all_to_all | solution.py:28
  16.7 0.7 reshape.22.gain_ref
  17.4 0.0 copy-start
  17.4 1.1 copy-done
  18.5 0.2 norm.1.mine_ref
  18.7 1.9 %collective-permute-start = (bf16[256,1152]{1,0:T(8,128)(2,1)S(1)}, bf16[256,1152]{1,0:T(8,128)(2,1)S(1)}, u32[]{:S(2)}, u32[]{:S(2)}) collective-permute-start(bf16[256,1152]{1,0:T(8,128)(2,1)S(1)} %norm.1.mine_ref), channel_id=1, source_target_pairs={{0,64},{64,0},{1,65},{65,1},{2,66},{66,2},{3,67},{67,3},{4,68},{68... | collective-permute-start | bytes 1769480 | tf_op jit(solution)/shard_map/ppermute | solution.py:192
  20.7 11.0 %all-to-all-done = bf16[16,36,128]{2,1,0:T(8,128)(2,1)S(1)} async-done(((bf16[16,36,128]{2,1,0:T(8,128)(2,1)}), bf16[16,36,128]{2,1,0:T(8,128)(2,1)S(1)}, u32[]{:S(2)}, u32[]{:S(2)}) %all-to-all-start) | async-done | bytes 147488 | tf_op jit(solution)/shard_map/all_to_all | solution.py:28
  31.7 0.1 reshape.23
  31.7 0.0 collective-permute-done.theirs_ref
  31.8 0.2 broadcast_in_dim.14
  32.0 36.5 %all_to_all.25 = bf16[16,288,256]{2,1,0:T(8,128)(2,1)S(1)} all-to-all(bf16[16,288,256]{2,1,0:T(8,128)(2,1)S(1)} %broadcast_in_dim.14), channel_id=1, replica_groups=mesh['y'=4,'core'=2,'x'=4,'zh'=4,'zl'=4] {'y','x'}, dimensions={0} | all-to-all | bytes 4718592 | tf_op jit(solution)/shard_map/all_to_all | solution.py:28
  68.5 0.0 copy-start.1
  68.5 1.7 %project.1 = (bf16[256,1024]{1,0:T(8,128)(2,1)S(1)}, bf16[256,1024]{1,0:T(8,128)(2,1)S(1)}) custom-call(bf16[256,1152]{1,0:T(8,128)(2,1)S(1)} %norm.1.mine_ref, bf16[256,1152]{1,0:T(8,128)(2,1)S(1)} %collective-permute-done.theirs_ref, bf16[4,1152,256]{2,1,0:T(8,128)(2,1)S(1)} %bitcast.7), custom_call_target="tpu_custom_call" | custom-call | flops 1207959552 | bytes 5242880 | tf_op jit(solution)/shard_map/project/pallas_call | solution.py:70
  70.2 1.9 %collective-permute-start.1 = (bf16[256,1024]{1,0:T(8,128)(2,1)S(1)}, bf16[256,1024]{1,0:T(8,128)(2,1)S(1)}, u32[]{:S(2)}, u32[]{:S(2)}) collective-permute-start(bf16[256,1024]{1,0:T(8,128)(2,1)S(1)} %get-tuple-element.19), channel_id=1, source_target_pairs={{0,64},{64,0},{1,65},{65,1},{2,66},{66,2},{3,67},{67,3},{4,68},{68... | collective-permute-start | bytes 1572872 | tf_op jit(solution)/shard_map/ppermute | solution.py:192
  72.1 1.9 %collective-permute-done.1.theirs_ref = bf16[256,1024]{1,0:T(8,128)(2,1)S(1)} collective-permute-done((bf16[256,1024]{1,0:T(8,128)(2,1)S(1)}, bf16[256,1024]{1,0:T(8,128)(2,1)S(1)}, u32[]{:S(2)}, u32[]{:S(2)}) %collective-permute-start.1) | collective-permute-done | bytes 524320 | tf_op jit(solution)/shard_map/ppermute | solution.py:192
  74.0 0.4 states.1
  74.4 1.9 %collective-permute-start.3 = (bf16[256,640]{1,0:T(8,128)(2,1)S(1)}, bf16[256,640]{1,0:T(8,128)(2,1)S(1)}, u32[]{:S(2)}, u32[]{:S(2)}) collective-permute-start(bf16[256,640]{1,0:T(8,128)(2,1)S(1)} %get-tuple-element.21.values_ref), channel_id=1, source_target_pairs={{1,0},{2,1},{3,2},{4,3},{5,4},{6,5},{7,6},{8,7},{9,8},{10,9},{11,1... | collective-permute-start | bytes 983048 | tf_op jit(solution)/shard_map/ppermute | solution.py:217
  76.3 3.9 %collective-permute-start.2 = (bf16[256,640]{1,0:T(8,128)(2,1)S(1)}, bf16[256,640]{1,0:T(8,128)(2,1)S(1)}, u32[]{:S(2)}, u32[]{:S(2)}) collective-permute-start(bf16[256,640]{1,0:T(8,128)(2,1)S(1)} %get-tuple-element.21.values_ref), channel_id=1, source_target_pairs={{0,1},{1,2},{2,3},{3,4},{4,5},{5,6},{6,7},{7,8},{8,9},{9,10},{10,1... | collective-permute-start | bytes 983048 | tf_op jit(solution)/shard_map/ppermute | solution.py:216
  80.2 8.2 %all_to_all.26 = f32[24,8,128]{2,1,0:T(8,128)S(1)} all-to-all(f32[24,8,128]{2,1,0:T(8,128)S(1)} %get-tuple-element.20), channel_id=1, replica_groups=mesh['y'=4,'core'=2,'x'=4,'zh'=4,'zl'=4] {'x'}, dimensions={0} | all-to-all | bytes 196608 | tf_op jit(solution)/shard_map/all_to_all | solution.py:28
  88.4 0.0 collective-permute-done.3.after_ref
  88.4 0.0 collective-permute-done.2.before_ref
  88.4 0.7 broadcast_in_dim.15
  89.1 9.7 %all-to-all-start.3 = ((bf16[16,48,128]{2,1,0:T(8,128)(2,1)}), bf16[16,48,128]{2,1,0:T(8,128)(2,1)S(1)}, u32[]{:S(2)}, u32[]{:S(2)}) async-start(bf16[16,48,128]{2,1,0:T(8,128)(2,1)} %broadcast_in_dim.15), calls=%async_computation.3 | async-start | bytes 393216 | tf_op jit(solution)/shard_map/all_to_all | solution.py:28
  98.8 0.0 copy-done.1
  98.8 1.7 %convolve.1.local_ref = f32[256,640]{1,0:T(8,128)S(1)} custom-call(bf16[256,640]{1,0:T(8,128)(2,1)S(1)} %collective-permute-done.2.before_ref, bf16[256,640]{1,0:T(8,128)(2,1)S(1)} %get-tuple-element.21.values_ref, bf16[256,640]{1,0:T(8,128)(2,1)S(1)} %collective-permute-done.3.after_ref, bf16[27,640]{1,0:T(8,128)(2,1)S(1)} %copy-done.1), custom_call_target="tpu_custom_call" | custom-call | flops 8847360 | bytes 2097152 | tf_op jit(solution)/shard_map/convolve/pallas_call | solution.py:144
  100.5 14.0 %all-to-all-done.3 = bf16[16,48,128]{2,1,0:T(8,128)(2,1)S(1)} async-done(((bf16[16,48,128]{2,1,0:T(8,128)(2,1)}), bf16[16,48,128]{2,1,0:T(8,128)(2,1)S(1)}, u32[]{:S(2)}, u32[]{:S(2)}) %all-to-all-start.3) | async-done | bytes 196640 | tf_op jit(solution)/shard_map/all_to_all | solution.py:28
  114.6 8.2 %all_to_all.27 = f32[4,6,8,128]{3,2,1,0:T(8,128)S(1)} all-to-all(f32[4,6,8,128]{3,2,1,0:T(8,128)S(1)} %broadcast_in_dim.33), channel_id=1, replica_groups=mesh['y'=4,'core'=2,'x'=4,'zh'=4,'zl'=4] {'x'}, dimensions={0} | all-to-all | bytes 196608 | tf_op jit(solution)/shard_map/all_to_all | solution.py:28
  122.8 1.4 %attend.1 = f32[256,640]{1,0:T(8,128)} custom-call(bf16[256,1024]{1,0:T(8,128)(2,1)S(1)} %get-tuple-element.18.mine_ref, bf16[256,1024]{1,0:T(8,128)(2,1)S(1)} %collective-permute-done.1.theirs_ref, f32[24,8,128]{2,1,0:T(8,128)S(1)} %bitcast.8, f32[256,640]{1,0:T(8,128)S(1)} %convolve.1.local_ref), custom_call_target="tpu_custom_call" | custom-call | flops 167772160 | bytes 3145728 | tf_op jit(solution)/shard_map/attend/pallas_call | solution.py:182
  (8 shorter events, 0.1 us)
Async XLA Ops:
  1.5 30.1 %all-to-all-start = ((bf16[16,36,128]{2,1,0:T(8,128)(2,1)}), bf16[16,36,128]{2,1,0:T(8,128)(2,1)S(1)}, u32[]{:S(2)}, u32[]{:S(2)}) async-start(bf16[16,36,128]{2,1,0:T(8,128)(2,1)} %broadcast_in_dim.13), calls=%async_computation | async-start | bytes 327680 | tf_op jit(solution)/shard_map/all_to_all | solution.py:28
  17.4 1.1 copy-start
  18.7 13.0 %collective-permute-start = (bf16[256,1152]{1,0:T(8,128)(2,1)S(1)}, bf16[256,1152]{1,0:T(8,128)(2,1)S(1)}, u32[]{:S(2)}, u32[]{:S(2)}) collective-permute-start(bf16[256,1152]{1,0:T(8,128)(2,1)S(1)} %norm.1.mine_ref), channel_id=1, source_target_pairs={{0,64},{64,0},{1,65},{65,1},{2,66},{66,2},{3,67},{67,3},{4,68},{68... | collective-permute-start | bytes 1769480 | tf_op jit(solution)/shard_map/ppermute | solution.py:192
  68.5 30.3 %copy-start.1 = (bf16[27,640]{1,0:T(8,128)(2,1)S(1)}, bf16[27,640]{1,0:T(8,128)(2,1)}, u32[]{:S(2)}) copy-start(bf16[27,640]{1,0:T(8,128)(2,1)} %weight_ref.1) | copy-start | bytes 103684
  70.2 3.8 %collective-permute-start.1 = (bf16[256,1024]{1,0:T(8,128)(2,1)S(1)}, bf16[256,1024]{1,0:T(8,128)(2,1)S(1)}, u32[]{:S(2)}, u32[]{:S(2)}) collective-permute-start(bf16[256,1024]{1,0:T(8,128)(2,1)S(1)} %get-tuple-element.19), channel_id=1, source_target_pairs={{0,64},{64,0},{1,65},{65,1},{2,66},{66,2},{3,67},{67,3},{4,68},{68... | collective-permute-start | bytes 1572872 | tf_op jit(solution)/shard_map/ppermute | solution.py:192
  74.4 14.1 %collective-permute-start.3 = (bf16[256,640]{1,0:T(8,128)(2,1)S(1)}, bf16[256,640]{1,0:T(8,128)(2,1)S(1)}, u32[]{:S(2)}, u32[]{:S(2)}) collective-permute-start(bf16[256,640]{1,0:T(8,128)(2,1)S(1)} %get-tuple-element.21.values_ref), channel_id=1, source_target_pairs={{1,0},{2,1},{3,2},{4,3},{5,4},{6,5},{7,6},{8,7},{9,8},{10,9},{11,1... | collective-permute-start | bytes 983048 | tf_op jit(solution)/shard_map/ppermute | solution.py:217
  76.3 12.1 %collective-permute-start.2 = (bf16[256,640]{1,0:T(8,128)(2,1)S(1)}, bf16[256,640]{1,0:T(8,128)(2,1)S(1)}, u32[]{:S(2)}, u32[]{:S(2)}) collective-permute-start(bf16[256,640]{1,0:T(8,128)(2,1)S(1)} %get-tuple-element.21.values_ref), channel_id=1, source_target_pairs={{0,1},{1,2},{2,3},{3,4},{4,5},{5,6},{6,7},{7,8},{8,9},{9,10},{10,1... | collective-permute-start | bytes 983048 | tf_op jit(solution)/shard_map/ppermute | solution.py:216
  89.1 25.4 %all-to-all-start.3 = ((bf16[16,48,128]{2,1,0:T(8,128)(2,1)}), bf16[16,48,128]{2,1,0:T(8,128)(2,1)S(1)}, u32[]{:S(2)}, u32[]{:S(2)}) async-start(bf16[16,48,128]{2,1,0:T(8,128)(2,1)} %broadcast_in_dim.15), calls=%async_computation.3 | async-start | bytes 393216 | tf_op jit(solution)/shard_map/all_to_all | solution.py:28

commit v6 on v5

--- a/solution.py
+++ b/solution.py
@@ -219,7 +219,6 @@
     share = TILES // lax.axis_size("x")
     part = jnp.sum(exchange(tiles, "x").reshape((-1, share) + tiles.shape[1:]), axis=0)
     part = part.astype(jnp.bfloat16).reshape(-1, LANES)
-    part, before, after = lax.optimization_barrier((part, before, after))
     local = convolve(before, values, after, conv_weight)
     part = jnp.sum(spread(part, ZAX).astype(jnp.float32), axis=0)
     part, local = lax.optimization_barrier((part, local))

time: 125 us -> 120 us (0.960)
  the two profiles are of different devices: /device:TPU:32 before, /device:TPU:2 now
where the time goes in v6:
time: 120 us
  blocking collectives  49.9 us (42%)
  starting transfers between devices  34.7 us (29%)
  waiting for transfers between devices  25 us (21%)
  Pallas kernels  5.42 us (5%)
  local copies, waits for them, and re-layouts  3.55 us (3%)
    all_to_all x3, blocking collectives, exchange(): return lax.all_to_all(blocks, axes, 0, 0, tiled=True)  49.9 us
    all_to_all x2, starting transfers between devices, exchange(): return lax.all_to_all(blocks, axes, 0, 0, tiled=True)  23 us
    all_to_all x2, waiting for transfers between devices, exchange(): return lax.all_to_all(blocks, axes, 0, 0, tiled=True)  11.7 us
    ppermute x1, waiting for transfers between devices, body(): after = lax.ppermute(values, TM, [(i + 1, i) for i in range(count - 1)])  9.09 us
    ppermute x1, starting transfers between devices, body(): after = lax.ppermute(values, TM, [(i + 1, i) for i in range(count - 1)])  5.94 us
    ppermute x2, starting transfers between devices, swap(): return lax.ppermute(block, 'core', [(0, 1), (1, 0)])  3.84 us
  transfers between devices with their start and end apart: 6, of which 4 were waited for; matrix products, arithmetic and copies ran while one was open for 1% of the time, Pallas kernels for 2%

profile of v6, /device:TPU:2, one launch (start us, length us, event | category | flops | bytes accessed | tf_op | source)
XLA Modules:
  0.0 119.6 jit_solution(2485370567320320199)
XLA Ops:
  0.0 0.1 pad_dynamic-slice_fusion.3
  0.1 0.7 fusion.2
  0.8 0.7 broadcast_in_dim.13
  1.5 15.2 %all-to-all-start = ((bf16[16,36,128]{2,1,0:T(8,128)(2,1)}), bf16[16,36,128]{2,1,0:T(8,128)(2,1)S(1)}, u32[]{:S(2)}, u32[]{:S(2)}) async-start(bf16[16,36,128]{2,1,0:T(8,128)(2,1)} %broadcast_in_dim.13), calls=%async_computation | async-start | bytes 327680 | tf_op jit(solution)/shard_map/all_to_all | solution.py:28
  16.7 0.7 reshape.24.gain_ref
  17.4 0.0 copy-start
  17.4 1.1 copy-done
  18.5 0.2 norm.1.mine_ref
  18.7 1.9 %collective-permute-start = (bf16[256,1152]{1,0:T(8,128)(2,1)S(1)}, bf16[256,1152]{1,0:T(8,128)(2,1)S(1)}, u32[]{:S(2)}, u32[]{:S(2)}) collective-permute-start(bf16[256,1152]{1,0:T(8,128)(2,1)S(1)} %norm.1.mine_ref), channel_id=1, source_target_pairs={{0,64},{64,0},{1,65},{65,1},{2,66},{66,2},{3,67},{67,3},{4,68},{68... | collective-permute-start | bytes 1769480 | tf_op jit(solution)/shard_map/ppermute | solution.py:192
  20.7 11.7 %all-to-all-done = bf16[16,36,128]{2,1,0:T(8,128)(2,1)S(1)} async-done(((bf16[16,36,128]{2,1,0:T(8,128)(2,1)}), bf16[16,36,128]{2,1,0:T(8,128)(2,1)S(1)}, u32[]{:S(2)}, u32[]{:S(2)}) %all-to-all-start) | async-done | bytes 147488 | tf_op jit(solution)/shard_map/all_to_all | solution.py:28
  32.4 0.1 reshape.25
  32.5 0.0 collective-permute-done.theirs_ref
  32.5 0.2 broadcast_in_dim.14
  32.7 33.6 %all_to_all.25 = bf16[16,288,256]{2,1,0:T(8,128)(2,1)S(1)} all-to-all(bf16[16,288,256]{2,1,0:T(8,128)(2,1)S(1)} %broadcast_in_dim.14), channel_id=1, replica_groups=mesh['y'=4,'core'=2,'x'=4,'zh'=4,'zl'=4] {'y','x'}, dimensions={0} | all-to-all | bytes 4718592 | tf_op jit(solution)/shard_map/all_to_all | solution.py:28
  66.4 0.0 copy-start.1
  66.4 1.7 %project.1 = (bf16[256,1024]{1,0:T(8,128)(2,1)S(1)}, bf16[256,1024]{1,0:T(8,128)(2,1)S(1)}) custom-call(bf16[256,1152]{1,0:T(8,128)(2,1)S(1)} %norm.1.mine_ref, bf16[256,1152]{1,0:T(8,128)(2,1)S(1)} %collective-permute-done.theirs_ref, bf16[4,1152,256]{2,1,0:T(8,128)(2,1)S(1)} %bitcast.7), custom_call_target="tpu_custom_call" | custom-call | flops 1207959552 | bytes 5242880 | tf_op jit(solution)/shard_map/project/pallas_call | solution.py:70
  68.0 1.9 %collective-permute-start.1 = (bf16[256,1024]{1,0:T(8,128)(2,1)S(1)}, bf16[256,1024]{1,0:T(8,128)(2,1)S(1)}, u32[]{:S(2)}, u32[]{:S(2)}) collective-permute-start(bf16[256,1024]{1,0:T(8,128)(2,1)S(1)} %get-tuple-element.16), channel_id=1, source_target_pairs={{0,64},{64,0},{1,65},{65,1},{2,66},{66,2},{3,67},{67,3},{4,68},{68... | collective-permute-start | bytes 1572872 | tf_op jit(solution)/shard_map/ppermute | solution.py:192
  70.0 1.9 %collective-permute-done.1.theirs_ref = bf16[256,1024]{1,0:T(8,128)(2,1)S(1)} collective-permute-done((bf16[256,1024]{1,0:T(8,128)(2,1)S(1)}, bf16[256,1024]{1,0:T(8,128)(2,1)S(1)}, u32[]{:S(2)}, u32[]{:S(2)}) %collective-permute-start.1) | collective-permute-done | bytes 524320 | tf_op jit(solution)/shard_map/ppermute | solution.py:192
  71.8 0.4 states.1
  72.2 8.2 %all_to_all.26 = f32[24,8,128]{2,1,0:T(8,128)S(1)} all-to-all(f32[24,8,128]{2,1,0:T(8,128)S(1)} %get-tuple-element.17), channel_id=1, replica_groups=mesh['y'=4,'core'=2,'x'=4,'zh'=4,'zl'=4] {'x'}, dimensions={0} | all-to-all | bytes 196608 | tf_op jit(solution)/shard_map/all_to_all | solution.py:28
  80.4 0.7 broadcast_in_dim.30
  81.1 7.8 %all-to-all-start.3 = ((bf16[16,48,128]{2,1,0:T(8,128)(2,1)}), bf16[16,48,128]{2,1,0:T(8,128)(2,1)S(1)}, u32[]{:S(2)}, u32[]{:S(2)}) async-start(bf16[16,48,128]{2,1,0:T(8,128)(2,1)} %broadcast_in_dim.30), calls=%async_computation.3 | async-start | bytes 393216 | tf_op jit(solution)/shard_map/all_to_all | solution.py:28
  88.9 5.9 %collective-permute-start.3 = (bf16[256,640]{1,0:T(8,128)(2,1)S(1)}, bf16[256,640]{1,0:T(8,128)(2,1)S(1)}, u32[]{:S(2)}, u32[]{:S(2)}) collective-permute-start(bf16[256,640]{1,0:T(8,128)(2,1)S(1)} %get-tuple-element.18.values_ref), channel_id=1, source_target_pairs={{1,0},{2,1},{3,2},{4,3},{5,4},{6,5},{7,6},{8,7},{9,8},{10,9},{11,1... | collective-permute-start | bytes 983048 | tf_op jit(solution)/shard_map/ppermute | solution.py:217
  94.8 1.9 %collective-permute-start.2 = (bf16[256,640]{1,0:T(8,128)(2,1)S(1)}, bf16[256,640]{1,0:T(8,128)(2,1)S(1)}, u32[]{:S(2)}, u32[]{:S(2)}) collective-permute-start(bf16[256,640]{1,0:T(8,128)(2,1)S(1)} %get-tuple-element.18.values_ref), channel_id=1, source_target_pairs={{0,1},{1,2},{2,3},{3,4},{4,5},{5,6},{6,7},{7,8},{8,9},{9,10},{10,1... | collective-permute-start | bytes 983048 | tf_op jit(solution)/shard_map/ppermute | solution.py:216
  96.8 9.1 %collective-permute-done.3.after_ref = bf16[256,640]{1,0:T(8,128)(2,1)S(1)} collective-permute-done((bf16[256,640]{1,0:T(8,128)(2,1)S(1)}, bf16[256,640]{1,0:T(8,128)(2,1)S(1)}, u32[]{:S(2)}, u32[]{:S(2)}) %collective-permute-start.3) | collective-permute-done | bytes 327712 | tf_op jit(solution)/shard_map/ppermute | solution.py:217
  105.9 2.3 %collective-permute-done.2.before_ref = bf16[256,640]{1,0:T(8,128)(2,1)S(1)} collective-permute-done((bf16[256,640]{1,0:T(8,128)(2,1)S(1)}, bf16[256,640]{1,0:T(8,128)(2,1)S(1)}, u32[]{:S(2)}, u32[]{:S(2)}) %collective-permute-start.2) | collective-permute-done | bytes 327712 | tf_op jit(solution)/shard_map/ppermute | solution.py:216
  108.2 0.0 copy-done.1
  108.2 1.7 %convolve.1.local_ref = f32[256,640]{1,0:T(8,128)S(1)} custom-call(bf16[256,640]{1,0:T(8,128)(2,1)S(1)} %collective-permute-done.2.before_ref, bf16[256,640]{1,0:T(8,128)(2,1)S(1)} %get-tuple-element.18.values_ref, bf16[256,640]{1,0:T(8,128)(2,1)S(1)} %collective-permute-done.3.after_ref, bf16[27,640]{1,0:T(8,128)(2,1)S(1)} %copy-done.1), custom_call_target="tpu_custom_call" | custom-call | flops 8847360 | bytes 2097152 | tf_op jit(solution)/shard_map/convolve/pallas_call | solution.py:144
  109.9 0.0 all-to-all-done.3
  110.0 8.1 %all_to_all.27 = f32[4,6,8,128]{3,2,1,0:T(8,128)S(1)} all-to-all(f32[4,6,8,128]{3,2,1,0:T(8,128)S(1)} %broadcast_in_dim.32), channel_id=1, replica_groups=mesh['y'=4,'core'=2,'x'=4,'zh'=4,'zl'=4] {'x'}, dimensions={0} | all-to-all | bytes 196608 | tf_op jit(solution)/shard_map/all_to_all | solution.py:28
  118.1 1.4 %attend.1 = f32[256,640]{1,0:T(8,128)} custom-call(bf16[256,1024]{1,0:T(8,128)(2,1)S(1)} %get-tuple-element.15.mine_ref, bf16[256,1024]{1,0:T(8,128)(2,1)S(1)} %collective-permute-done.1.theirs_ref, f32[24,8,128]{2,1,0:T(8,128)S(1)} %bitcast.8, f32[256,640]{1,0:T(8,128)S(1)} %convolve.1.local_ref), custom_call_target="tpu_custom_call" | custom-call | flops 167772160 | bytes 3145728 | tf_op jit(solution)/shard_map/attend/pallas_call | solution.py:182
  (8 shorter events, 0.1 us)
Async XLA Ops:
  1.5 30.9 %all-to-all-start = ((bf16[16,36,128]{2,1,0:T(8,128)(2,1)}), bf16[16,36,128]{2,1,0:T(8,128)(2,1)S(1)}, u32[]{:S(2)}, u32[]{:S(2)}) async-start(bf16[16,36,128]{2,1,0:T(8,128)(2,1)} %broadcast_in_dim.13), calls=%async_computation | async-start | bytes 327680 | tf_op jit(solution)/shard_map/all_to_all | solution.py:28
  17.4 1.1 copy-start
  18.7 13.8 %collective-permute-start = (bf16[256,1152]{1,0:T(8,128)(2,1)S(1)}, bf16[256,1152]{1,0:T(8,128)(2,1)S(1)}, u32[]{:S(2)}, u32[]{:S(2)}) collective-permute-start(bf16[256,1152]{1,0:T(8,128)(2,1)S(1)} %norm.1.mine_ref), channel_id=1, source_target_pairs={{0,64},{64,0},{1,65},{65,1},{2,66},{66,2},{3,67},{67,3},{4,68},{68... | collective-permute-start | bytes 1769480 | tf_op jit(solution)/shard_map/ppermute | solution.py:192
  66.4 41.8 %copy-start.1 = (bf16[27,640]{1,0:T(8,128)(2,1)S(1)}, bf16[27,640]{1,0:T(8,128)(2,1)}, u32[]{:S(2)}) copy-start(bf16[27,640]{1,0:T(8,128)(2,1)} %weight_ref.1) | copy-start | bytes 103684
  68.0 3.8 %collective-permute-start.1 = (bf16[256,1024]{1,0:T(8,128)(2,1)S(1)}, bf16[256,1024]{1,0:T(8,128)(2,1)S(1)}, u32[]{:S(2)}, u32[]{:S(2)}) collective-permute-start(bf16[256,1024]{1,0:T(8,128)(2,1)S(1)} %get-tuple-element.16), channel_id=1, source_target_pairs={{0,64},{64,0},{1,65},{65,1},{2,66},{66,2},{3,67},{67,3},{4,68},{68... | collective-permute-start | bytes 1572872 | tf_op jit(solution)/shard_map/ppermute | solution.py:192
  81.1 28.8 %all-to-all-start.3 = ((bf16[16,48,128]{2,1,0:T(8,128)(2,1)}), bf16[16,48,128]{2,1,0:T(8,128)(2,1)S(1)}, u32[]{:S(2)}, u32[]{:S(2)}) async-start(bf16[16,48,128]{2,1,0:T(8,128)(2,1)} %broadcast_in_dim.30), calls=%async_computation.3 | async-start | bytes 393216 | tf_op jit(solution)/shard_map/all_to_all | solution.py:28
  88.9 17.0 %collective-permute-start.3 = (bf16[256,640]{1,0:T(8,128)(2,1)S(1)}, bf16[256,640]{1,0:T(8,128)(2,1)S(1)}, u32[]{:S(2)}, u32[]{:S(2)}) collective-permute-start(bf16[256,640]{1,0:T(8,128)(2,1)S(1)} %get-tuple-element.18.values_ref), channel_id=1, source_target_pairs={{1,0},{2,1},{3,2},{4,3},{5,4},{6,5},{7,6},{8,7},{9,8},{10,9},{11,1... | collective-permute-start | bytes 983048 | tf_op jit(solution)/shard_map/ppermute | solution.py:217
  94.8 13.3 %collective-permute-start.2 = (bf16[256,640]{1,0:T(8,128)(2,1)S(1)}, bf16[256,640]{1,0:T(8,128)(2,1)S(1)}, u32[]{:S(2)}, u32[]{:S(2)}) collective-permute-start(bf16[256,640]{1,0:T(8,128)(2,1)S(1)} %get-tuple-element.18.values_ref), channel_id=1, source_target_pairs={{0,1},{1,2},{2,3},{3,4},{4,5},{5,6},{6,7},{7,8},{8,9},{9,10},{10,1... | collective-permute-start | bytes 983048 | tf_op jit(solution)/shard_map/ppermute | solution.py:216

commit v7 on v5

v7 whole, which is shorter than its diff:
```python
import jax
import jax.numpy as jnp
from jax import lax
from jax.experimental import pallas as pl
from jax.experimental.pallas import tpu as pltpu
from jax.sharding import Mesh
from jax.sharding import PartitionSpec as P

HEAD_WIDTH = 32
FH = 8
FW = 32
LANES = 128
BLOCK = 2 * LANES
GROUPS = 5
QUARTERS = 4
TILES = 7

AXES = ("y", "core", "xh", "xl", "zh", "zl")
ZAX = ("zh", "zl")
PLANE = ("y", "xh", "xl")
TM = ("xh", "xl", "zh", "zl")
HOME = ("core", "xh", "xl")
PARAMS = pltpu.CompilerParams(vmem_limit_bytes=16 * 1024 * 1024)


def cost(flops, nbytes):
    return pl.CostEstimate(flops=flops, bytes_accessed=nbytes, transcendentals=0)


def exchange(blocks, axes):
    return lax.all_to_all(blocks, axes, 0, 0, tiled=True)


def spread(block, axes):
    count = lax.axis_size(axes)
    return exchange(jnp.broadcast_to(block[None], (count,) + block.shape), axes)


def norm_kernel(tokens_ref, gain_ref, out_ref):
    x = tokens_ref[...].astype(jnp.float32)
    scale = lax.rsqrt(jnp.mean(x * x, axis=1, keepdims=True) + 1e-06)
    out_ref[...] = (x * scale * gain_ref[...].astype(jnp.float32)).astype(jnp.bfloat16)


def norm(tokens, gain):
    return pl.pallas_call(
        norm_kernel,
        out_shape=jax.ShapeDtypeStruct(tokens.shape, jnp.bfloat16),
        compiler_params=PARAMS,
        cost_estimate=cost(10 * tokens.size, 4 * tokens.size),
        name="norm",
    )(tokens, gain.reshape(1, -1))


def project_kernel(own_ref, across_ref, other_ref, far_ref, weight_ref, *out_refs):
    lane = lax.broadcasted_iota(jnp.int32, (own_ref.shape[0], LANES), 1)
    home_ref, away_ref, keys_ref = out_refs
    for pair in range(2):
        weight = jnp.concatenate([weight_ref[2 * pair], weight_ref[2 * pair + 1]], axis=1)
        for i, tokens_ref in enumerate((own_ref, across_ref, other_ref, far_ref)):
            both = jnp.dot(tokens_ref[...], weight, preferred_element_type=jnp.float32)
            for half in range(2):
                unit = 2 * pair + half
                proj = both[:, half * LANES : (half + 1) * LANES]
                feat = jnp.where(proj > 0, proj, jnp.exp(jnp.minimum(proj, 0.0)) - 1.0) + 1.0
                if unit == 0:
                    feat = proj
                if unit == 2:
                    feat = jnp.where(lane < HEAD_WIDTH, proj, feat)
                feat = feat.astype(jnp.bfloat16)
                if unit == 3:
                    keys_ref[i] = feat
                else:
                    out = (home_ref, away_ref)[i // 2]
                    out[i % 2, :, unit * LANES : (unit + 1) * LANES] = feat


def project(own, across, other, far, weights):
    rows, depth = own.shape
    units = weights.shape[0]
    bf16 = jnp.bfloat16
    return pl.pallas_call(
        project_kernel,
        out_shape=[
            jax.ShapeDtypeStruct((2, rows, 3 * LANES), bf16),
            jax.ShapeDtypeStruct((2, rows, 3 * LANES), bf16),
            jax.ShapeDtypeStruct((4, rows, LANES), bf16),
        ],
        compiler_params=PARAMS,
        cost_estimate=cost(8 * rows * depth * units * LANES, 5 * 1024 * 1024),
        name="project",
    )(own, across, other, far, weights)


def gram(a, b):
    return lax.dot_general(a, b, (((0,), (0,)), ((), ())), preferred_element_type=jnp.float32)


def state_kernel(home_ref, away_ref, keys_ref, tiles_ref):
    first = lax.axis_index("core") == 0
    lane = lax.broadcasted_iota(jnp.int32, (HEAD_WIDTH, LANES), 1) // HEAD_WIDTH
    main, extra, sums, extra_sums = [], [], [], []
    for video, ref in enumerate((home_ref, away_ref)):
        square, corner = 0.0, 0.0
        ksum, xsum = 0.0, 0.0
        for frame in range(2):
            keys = keys_ref[2 * video + frame]
            mixed = ref[frame, :, 2 * LANES :]
            square += gram(keys, ref[frame, :, :LANES])
            corner += gram(mixed, mixed)
            ksum += jnp.sum(keys.astype(jnp.float32), axis=0, keepdims=True)
            xsum += jnp.sum(mixed.astype(jnp.float32), axis=0, keepdims=True)
        packed = jnp.zeros((HEAD_WIDTH, LANES), jnp.float32)
        for h in range(LANES // HEAD_WIDTH):
            packed = jnp.where(lane == h, square[h * HEAD_WIDTH : (h + 1) * HEAD_WIDTH], packed)
        main.append(packed)
        extra.append(corner[HEAD_WIDTH : 2 * HEAD_WIDTH])
        sums.append(ksum)
        extra_sums.append(xsum)
    zero = jnp.where(first, main[0], main[1])
    one = jnp.where(first, main[1], main[0])
    early = jnp.where(first, extra[0], extra[1])
    late = pltpu.roll(jnp.where(first, extra[1], extra[0]), HEAD_WIDTH, 1)
    corner = jnp.where(lane == 0, early, jnp.where(lane == 1, late, 0.0))
    for half in range(2):
        for i, block in enumerate((zero, one, corner)):
            for t in range(2):
                at = 8 * (2 * half + t)
                tiles_ref[half, 2 * i + t] = block[at : at + 8]
        tiles_ref[half, 6] = jnp.zeros((8, LANES), jnp.float32)
        tiles_ref[half, 6, 0:1, :] = jnp.where(first, sums[0], sums[1])
        tiles_ref[half, 6, 1:2, :] = jnp.where(first, sums[1], sums[0])
        tiles_ref[half, 6, 2:3, :] = jnp.where(first, extra_sums[0], extra_sums[1])
        tiles_ref[half, 6, 3:4, :] = jnp.where(first, extra_sums[1], extra_sums[0])


def states(home, away, keys):
    return pl.pallas_call(
        state_kernel,
        out_shape=jax.ShapeDtypeStruct((2, TILES, 8, LANES), jnp.float32),
        compiler_params=PARAMS,
        cost_estimate=cost(16 * home.shape[1] * LANES * LANES, 2 * 1024 * 1024),
        name="states",
    )(home, away, keys)


def quarter_of(q, refs):
    core = lax.axis_index("core") != q // 2
    side = lax.axis_index("xl") != q % 2

    def pick_one(unit):
        at = slice(unit * LANES, (unit + 1) * LANES)
        own, across, other, far = (ref[0, :, at] for ref in refs)
        return jnp.where(core, jnp.where(side, far, other), jnp.where(side, across, own))

    return pick_one


def assemble_kernel(own_ref, across_ref, other_ref, far_ref, values_ref, query_ref):
    refs = (own_ref, across_ref, other_ref, far_ref)
    lane = lax.broadcasted_iota(jnp.int32, (own_ref.shape[1], LANES), 1) // HEAD_WIDTH
    value, query = 0.0, 0.0
    for q in range(QUARTERS):
        take = quarter_of(q, refs)
        values_ref[:, q * LANES : (q + 1) * LANES] = take(0)
        query_ref[:, q * LANES : (q + 1) * LANES] = take(1)
        mixed = take(2).astype(jnp.float32)
        moved = pltpu.roll(mixed, q * HEAD_WIDTH, 1) if q else mixed
        value = jnp.where(lane == q, moved, value)
        shift = (q - 2) % 4 * HEAD_WIDTH
        moved = pltpu.roll(mixed, shift, 1) if shift else mixed
        query = jnp.where(lane == q, moved, query)
    values_ref[:, QUARTERS * LANES :] = value.astype(jnp.bfloat16)
    query_ref[:, QUARTERS * LANES :] = query.astype(jnp.bfloat16)


def assemble(own, across, other, far):
    rows = own.shape[1]
    return pl.pallas_call(
        assemble_kernel,
        out_shape=[jax.ShapeDtypeStruct((rows, GROUPS * LANES), jnp.bfloat16)] * 2,
        compiler_params=PARAMS,
        cost_estimate=cost(rows * 4 * LANES, 2 * 1024 * 1024),
        name="assemble",
    )(own, across, other, far)


def conv_kernel(before_ref, values_ref, after_ref, weight_ref, out_ref):
    zeros = jnp.zeros((FW, LANES), jnp.float32)
    rows = FH * FW
    x = lax.broadcasted_iota(jnp.int32, (rows, LANES), 0) % FW
    weight = weight_ref[...].astype(jnp.float32)
    frames = [
        jnp.concatenate([zeros, ref[...].astype(jnp.float32), zeros], axis=0)
        for ref in (before_ref, values_ref, after_ref)
    ]
    sums = []
    for c in range(3):
        total = None
        for a in range(3):
            for b in range(3):
                tap = 9 * a + 3 * b + c
                term = frames[a][b * FW : b * FW + rows] * weight[tap : tap + 1]
                total = term if total is None else total + term
        sums.append(total)
    left = jnp.where(x == 0, 0.0, pltpu.roll(sums[0], 1, 0))
    right = jnp.where(x == FW - 1, 0.0, pltpu.roll(sums[2], rows - 1, 0))
    out_ref[...] = left + sums[1] + right


def convolve(before, values, after, weight):
    rows, width = values.shape
    block = pl.BlockSpec((rows, LANES), lambda i: (0, i))
    return pl.pallas_call(
        conv_kernel,
        grid=(width // LANES,),
        in_specs=[block, block, block, pl.BlockSpec((27, LANES), lambda i: (0, i))],
        out_specs=block,
        out_shape=jax.ShapeDtypeStruct((rows, width), jnp.float32),
        compiler_params=PARAMS,
        cost_estimate=cost(54 * rows * width, 2 * 1024 * 1024),
        name="convolve",
    )(before, values, after, weight)


def split_dot(a, b):
    high = b.astype(jnp.bfloat16)
    low = (b - high.astype(jnp.float32)).astype(jnp.bfloat16)
    return jnp.dot(a, high, preferred_element_type=jnp.float32) + jnp.dot(
        a, low, preferred_element_type=jnp.float32
    )


def attend_kernel(query_ref, tiles_ref, local_ref, out_ref):
    first = lax.axis_index("core") == 0
    row = lax.broadcasted_iota(jnp.int32, (LANES, LANES), 0) // HEAD_WIDTH
    lane = lax.broadcasted_iota(jnp.int32, (LANES, LANES), 1) // HEAD_WIDTH
    same = row == lane
    packs, sums = [], []
    extra, extra_sum = 0.0, 0.0
    for q in range(QUARTERS):
        low, high = (q // 2 * 4 + half * 2 + q % 2 for half in range(2))
        parts = [
            jnp.where(first, tiles_ref[at, t], tiles_ref[at, 2 + t])
            for at in (low, high)
            for t in range(2)
        ]
        packs.append(jnp.concatenate(parts, axis=0))
        ksum = tiles_ref[low, 6]
        sums.append(jnp.where(first, ksum[0:1], ksum[1:2]))
        corner = jnp.concatenate([tiles_ref[at, 4 + t] for at in (low, high) for t in range(2)], 0)
        corner = jnp.where(first, corner, pltpu.roll(corner, LANES - HEAD_WIDTH, 1))
        corner = pltpu.roll(corner, q * HEAD_WIDTH, 1) if q else corner
        extra = jnp.where(lane[:HEAD_WIDTH] == q, corner, extra)
        shift = (q - 1) % 4 * HEAD_WIDTH
        xsum = pltpu.roll(ksum, shift, 1) if shift else ksum
        xsum = jnp.where(first, xsum[2:3], xsum[3:4])
        extra_sum = jnp.where(lane[:1] == q, xsum, extra_sum)
    packs.append(extra)
    sums.append(extra_sum)
    for g in range(GROUPS):
        cols = slice(g * LANES, (g + 1) * LANES)
        state = jnp.where(same, jnp.concatenate([packs[g]] * 4, axis=0), 0.0)
        ksum = jnp.where(same, jnp.broadcast_to(sums[g], (LANES, LANES)).T, 0.0)
        both = split_dot(query_ref[:, cols], jnp.concatenate([state, ksum], axis=1))
        out_ref[:, cols] = both[:, :LANES] / both[:, LANES:] + local_ref[:, cols]


def attend(query, tiles, local):
    rows, width = local.shape
    return pl.pallas_call(
        attend_kernel,
        out_shape=jax.ShapeDtypeStruct((rows, width), jnp.float32),
        compiler_params=PARAMS,
        cost_estimate=cost(8 * rows * width * LANES, 3 * 1024 * 1024),
        name="attend",
    )(query, tiles, local)


def pick_kernel(cat_ref, out_ref):
    y, core = lax.axis_index("y"), lax.axis_index("core")
    width = GROUPS * LANES
    row = lax.broadcasted_iota(jnp.int32, (LANES, LANES), 0)
    lane = lax.broadcasted_iota(jnp.int32, (LANES, LANES), 1)
    blocks = []
    for t in range(2):
        quarter = 2 * core + t
        whole, mixed = [], 0.0
        for i in range(3):
            at = i * width + t * LANES
            left, right = cat_ref[:, at : at + LANES], cat_ref[:, at + BLOCK : at + BLOCK + LANES]
            whole.append(jnp.where(core == 0, left, right).astype(jnp.float32))
            place = (0, 2, 1)[i] * HEAD_WIDTH
            take = jnp.logical_and(lane >= place, lane < place + HEAD_WIDTH)
            take = jnp.logical_and(take, row == quarter * HEAD_WIDTH + lane - place)
            take = jnp.where(take, 1.0, 0.0).astype(jnp.bfloat16)
            tail = cat_ref[:, i * width + 2 * BLOCK : (i + 1) * width]
            mixed += jnp.dot(tail, take, preferred_element_type=jnp.float32)
        value, query, key = whole
        block = jnp.where(y == 1, query, jnp.where(y == 2, mixed, key))
        blocks.append(jnp.where(y == 0, value, block))
    block = jnp.concatenate(blocks, axis=0).astype(jnp.bfloat16)
    for i in range(out_ref.shape[0]):
        out_ref[i] = block


def pick(w_query, w_key, w_value, copies):
    rows = w_query.shape[0]
    return pl.pallas_call(
        pick_kernel,
        out_shape=jax.ShapeDtypeStruct((copies, 2 * rows, LANES), jnp.bfloat16),
        compiler_params=PARAMS,
        cost_estimate=cost(0, 4 * 1024 * rows),
        name="pick",
    )(jnp.concatenate([w_value, w_query, w_key], axis=1))


def flip(block, axis):
    return lax.ppermute(block, axis, [(0, 1), (1, 0)])


def body(tokens, gain, w_query, w_key, w_value, conv_weight):
    rows = w_query.shape[0]
    own = norm(tokens, gain)
    across, other = flip(own, "xl"), flip(own, "core")
    column = exchange(pick(w_query, w_key, w_value, lax.axis_size(ZAX)), ZAX)
    column = column.reshape(-1, 2, rows, LANES).transpose(1, 0, 2, 3).reshape(2, -1, LANES)
    column, across, other = lax.optimization_barrier((column, across, other))
    far = flip(across, "core")
    weights = exchange(
        jnp.broadcast_to(column[None], (8,) + column.shape).reshape((-1,) + column.shape[1:]), PLANE
    )
    weights = weights.reshape(lax.axis_size("y"), -1, LANES)

    home, away, keys = project(own, across, other, far, weights)
    tiles = states(home, away, keys)
    back = flip(away, "core")
    values, query = assemble(home, flip(home[1:], "xl"), back, flip(back[1:], "xl"))
    count = lax.axis_size(TM)
    before = lax.ppermute(values, TM, [(i, i + 1) for i in range(count - 1)])
    after = lax.ppermute(values, TM, [(i + 1, i) for i in range(count - 1)])

    part = jnp.sum(exchange(tiles, "xh"), axis=0)
    part = part.astype(jnp.bfloat16).reshape(-1, LANES)
    part = jnp.sum(spread(part, ZAX).astype(jnp.float32), axis=0)
    part, before, after = lax.optimization_barrier((part, before, after))
    local = convolve(before, values, after, conv_weight)
    tiles = spread(part.reshape(tiles.shape[1:]), HOME)
    return attend(query, tiles, local)


def solution(mesh):
    fine = Mesh(mesh.devices.reshape(4, 2, 2, 2, 4, 4), AXES)
    rows = P(AXES, None)
    split = P(TM, None)
    return jax.shard_map(
        body, mesh=fine, in_specs=(rows, P(), split, split, split, P()), out_specs=rows, check_vma=False
    )
```

time: 125 us -> 131 us (1.048)
  the two profiles are of different devices: /device:TPU:32 before, /device:TPU:1 now
where the time goes in v7:
time: 131 us; the launch traced here: 130 us
  starting transfers between devices  60.3 us (46%)
  blocking collectives  29.7 us (23%)
  waiting for transfers between devices  26.4 us (20%)
  local copies, waits for them, and re-layouts  7.57 us (6%)
  Pallas kernels  6.09 us (5%)
    all_to_all x2, blocking collectives, exchange(): return lax.all_to_all(blocks, axes, 0, 0, tiled=True)  29.7 us
    all_to_all x3, starting transfers between devices, exchange(): return lax.all_to_all(blocks, axes, 0, 0, tiled=True)  27.9 us
    ppermute x6, starting transfers between devices, flip(): return lax.ppermute(block, axis, [(0, 1), (1, 0)])  26.9 us
    all_to_all x3, waiting for transfers between devices, exchange(): return lax.all_to_all(blocks, axes, 0, 0, tiled=True)  11.5 us
    ppermute x6, waiting for transfers between devices, flip(): return lax.ppermute(block, axis, [(0, 1), (1, 0)])  8.91 us
    ppermute x1, waiting for transfers between devices, body(): after = lax.ppermute(values, TM, [(i + 1, i) for i in range(count - 1)])  5.16 us
    ppermute x1, starting transfers between devices, body(): before = lax.ppermute(values, TM, [(i, i + 1) for i in range(count - 1)])  4.19 us
    unnamed x18, local copies, waits for them, and re-layouts  4.05 us
  transfers between devices with their start and end apart: 11, of which 7 were waited for; matrix products, arithmetic and copies ran while one was open for 0% of the time, Pallas kernels for 2%

profile of v7, /device:TPU:1, one launch (start us, length us, event | category | flops | bytes accessed | tf_op | source)
XLA Modules:
  0.0 130.3 jit_solution(400602510059994479)
XLA Ops:
  0.0 0.7 reshape.23.gain_ref
  0.7 1.1 copy-done
  2.0 8.8 %collective-permute-start.1 = (bf16[256,1152]{1,0:T(8,128)(2,1)S(1)}, bf16[256,1152]{1,0:T(8,128)(2,1)S(1)}, u32[]{:S(2)}, u32[]{:S(2)}) collective-permute-start(bf16[256,1152]{1,0:T(8,128)(2,1)S(1)} %norm.1.own_ref), channel_id=1, source_target_pairs={{0,64},{64,0},{1,65},{65,1},{2,66},{66,2},{3,67},{67,3},{4,68},{68... | collective-permute-start | bytes 1769480 | tf_op jit(solution)/shard_map/ppermute | solution.py:319
  10.8 1.9 %collective-permute-start = (bf16[256,1152]{1,0:T(8,128)(2,1)S(1)}, bf16[256,1152]{1,0:T(8,128)(2,1)S(1)}, u32[]{:S(2)}, u32[]{:S(2)}) collective-permute-start(bf16[256,1152]{1,0:T(8,128)(2,1)S(1)} %norm.1.own_ref), channel_id=1, source_target_pairs={{0,16},{16,0},{1,17},{17,1},{2,18},{18,2},{3,19},{19,3},{4,20},{20... | collective-permute-start | bytes 1769480 | tf_op jit(solution)/shard_map/ppermute | solution.py:319
  13.0 22.9 %all_to_all.25 = bf16[16,36,128]{2,1,0:T(8,128)(2,1)S(1)} all-to-all(bf16[16,36,128]{2,1,0:T(8,128)(2,1)S(1)} %pick.1), channel_id=1, replica_groups=mesh['y'=4,'core'=2,'xh'=2,'xl'=2,'zh'=4,'zl'=4] {'zh','zl'}, dimensions={0} | all-to-all | bytes 294912 | tf_op jit(solution)/shard_map/all_to_all | solution.py:31
  36.1 1.2 broadcast_in_dim.8
  37.3 6.5 %all-to-all-start.1 = ((bf16[16,288,128]{2,1,0:T(8,128)(2,1)}), bf16[16,288,128]{2,1,0:T(8,128)(2,1)S(1)}, u32[]{:S(2)}, u32[]{:S(2)}) async-start(bf16[16,288,128]{2,1,0:T(8,128)(2,1)} %bitcast.11), calls=%async_computation.1 | async-start | bytes 2359296 | tf_op jit(solution)/shard_map/all_to_all | solution.py:31
  43.7 5.6 %collective-permute-start.2 = (bf16[256,1152]{1,0:T(8,128)(2,1)S(1)}, bf16[256,1152]{1,0:T(8,128)(2,1)S(1)}, u32[]{:S(2)}, u32[]{:S(2)}) collective-permute-start(bf16[256,1152]{1,0:T(8,128)(2,1)S(1)} %collective-permute-done.across_ref), channel_id=1, source_target_pairs={{0,64},{64,0},{1,65},{65,1},{2,66},{66,2},{3,67},{67,3},{4,68},{68... | collective-permute-start | bytes 1769480 | tf_op jit(solution)/shard_map/ppermute | solution.py:319
  49.3 1.6 %collective-permute-done.2.far_ref = bf16[256,1152]{1,0:T(8,128)(2,1)S(1)} collective-permute-done((bf16[256,1152]{1,0:T(8,128)(2,1)S(1)}, bf16[256,1152]{1,0:T(8,128)(2,1)S(1)}, u32[]{:S(2)}, u32[]{:S(2)}) %collective-permute-start.2) | collective-permute-done | bytes 589856 | tf_op jit(solution)/shard_map/ppermute | solution.py:319
  50.9 0.8 copy-done.4
  51.8 7.0 %all-to-all-done.1 = bf16[16,288,128]{2,1,0:T(8,128)(2,1)S(1)} async-done(((bf16[16,288,128]{2,1,0:T(8,128)(2,1)}), bf16[16,288,128]{2,1,0:T(8,128)(2,1)S(1)}, u32[]{:S(2)}, u32[]{:S(2)}) %all-to-all-start.1) | async-done | bytes 1179680 | tf_op jit(solution)/shard_map/all_to_all | solution.py:31
  58.7 1.1 copy-done.3
  59.8 1.1 copy-done.5
  60.9 1.6 %project.1 = (bf16[2,256,384]{2,1,0:T(8,128)(2,1)S(1)}, bf16[2,256,384]{2,1,0:T(8,128)(2,1)S(1)}, bf16[4,256,128]{2,1,0:T(8,128)(2,1)S(1)}) custom-call(bf16[256,1152]{1,0:T(8,128)(2,1)S(1)} %norm.1.own_ref, bf16[256,1152]{1,0:T(8,128)(2,1)S(1)} %copy-done.3, bf16[256,1152]{1,0:T(8,128)(2,1)S(1)} %collective-permute-done.1.other_ref, ...), custom_call_target="tpu_custom_call" | custom-call | flops 1207959552 | bytes 5242880 | tf_op jit(solution)/shard_map/project/pallas_call | solution.py:82
  62.9 6.8 %all_to_all.26 = f32[2,7,8,128]{3,2,1,0:T(8,128)S(1)} all-to-all(f32[2,7,8,128]{3,2,1,0:T(8,128)S(1)} %states.1), channel_id=1, replica_groups=mesh['y'=4,'core'=2,'xh'=2,'xl'=2,'zh'=4,'zl'=4] {'xh'}, dimensions={0} | all-to-all | bytes 114688 | tf_op jit(solution)/shard_map/all_to_all | solution.py:31
  69.7 0.7 broadcast_in_dim.9
  70.4 10.9 %all-to-all-start.3 = ((bf16[16,56,128]{2,1,0:T(8,128)(2,1)}), bf16[16,56,128]{2,1,0:T(8,128)(2,1)S(1)}, u32[]{:S(2)}, u32[]{:S(2)}) async-start(bf16[16,56,128]{2,1,0:T(8,128)(2,1)} %broadcast_in_dim.9), calls=%async_computation.3 | async-start | bytes 458752 | tf_op jit(solution)/shard_map/all_to_all | solution.py:31
  81.3 5.3 %collective-permute-start.4 = (bf16[2,256,384]{2,1,0:T(8,128)(2,1)S(1)}, bf16[2,256,384]{2,1,0:T(8,128)(2,1)S(1)}, u32[]{:S(2)}, u32[]{:S(2)}) collective-permute-start(bf16[2,256,384]{2,1,0:T(8,128)(2,1)S(1)} %get-tuple-element.20.away_ref), channel_id=1, source_target_pairs={{0,64},{64,0},{1,65},{65,1},{2,66},{66,2},{3,67},{67,3},{4,68},{68... | collective-permute-start | bytes 1179656 | tf_op jit(solution)/shard_map/ppermute | solution.py:319
  86.6 1.9 %collective-permute-start.3 = (bf16[1,256,384]{2,1,0:T(8,128)(2,1)S(1)}, bf16[1,256,384]{2,1,0:T(8,128)(2,1)S(1)}, u32[]{:S(2)}, u32[]{:S(2)}) collective-permute-start(bf16[1,256,384]{2,1,0:T(8,128)(2,1)S(1)} %slice.6), channel_id=1, source_target_pairs={{0,16},{16,0},{1,17},{17,1},{2,18},{18,2},{3,19},{19,3},{4,20},{20... | collective-permute-start | bytes 589832 | tf_op jit(solution)/shard_map/ppermute | solution.py:319
  88.6 3.4 %collective-permute-start.5 = (bf16[1,256,384]{2,1,0:T(8,128)(2,1)S(1)}, bf16[1,256,384]{2,1,0:T(8,128)(2,1)S(1)}, u32[]{:S(2)}, u32[]{:S(2)}) collective-permute-start(bf16[1,256,384]{2,1,0:T(8,128)(2,1)S(1)} %slice.8), channel_id=1, source_target_pairs={{0,16},{16,0},{1,17},{17,1},{2,18},{18,2},{3,19},{19,3},{4,20},{20... | collective-permute-start | bytes 589832 | tf_op jit(solution)/shard_map/ppermute | solution.py:319
  92.0 3.1 %collective-permute-done.3.across_ref = bf16[1,256,384]{2,1,0:T(8,128)(2,1)S(1)} collective-permute-done((bf16[1,256,384]{2,1,0:T(8,128)(2,1)S(1)}, bf16[1,256,384]{2,1,0:T(8,128)(2,1)S(1)}, u32[]{:S(2)}, u32[]{:S(2)}) %collective-permute-start.3) | collective-permute-done | bytes 196640 | tf_op jit(solution)/shard_map/ppermute | solution.py:319
  95.1 4.2 %collective-permute-done.5.far_ref = bf16[1,256,384]{2,1,0:T(8,128)(2,1)S(1)} collective-permute-done((bf16[1,256,384]{2,1,0:T(8,128)(2,1)S(1)}, bf16[1,256,384]{2,1,0:T(8,128)(2,1)S(1)}, u32[]{:S(2)}, u32[]{:S(2)}) %collective-permute-start.5) | collective-permute-done | bytes 196640 | tf_op jit(solution)/shard_map/ppermute | solution.py:319
  99.3 0.5 assemble.1
  99.8 1.3 collective-permute-start.7
  101.1 4.2 %collective-permute-start.6 = (bf16[256,640]{1,0:T(8,128)(2,1)S(1)}, bf16[256,640]{1,0:T(8,128)(2,1)S(1)}, u32[]{:S(2)}, u32[]{:S(2)}) collective-permute-start(bf16[256,640]{1,0:T(8,128)(2,1)S(1)} %get-tuple-element.23.values_ref), channel_id=1, source_target_pairs={{0,1},{1,2},{2,3},{3,4},{4,5},{5,6},{6,7},{7,8},{8,9},{9,10},{10,1... | collective-permute-start | bytes 983048 | tf_op jit(solution)/shard_map/ppermute | solution.py:340
  105.3 5.2 %collective-permute-done.7.after_ref = bf16[256,640]{1,0:T(8,128)(2,1)S(1)} collective-permute-done((bf16[256,640]{1,0:T(8,128)(2,1)S(1)}, bf16[256,640]{1,0:T(8,128)(2,1)S(1)}, u32[]{:S(2)}, u32[]{:S(2)}) %collective-permute-start.7) | collective-permute-done | bytes 327712 | tf_op jit(solution)/shard_map/ppermute | solution.py:341
  110.5 0.9 collective-permute-done.6.before_ref
  111.4 0.7 broadcast_in_dim.21
  112.1 10.6 %all-to-all-start.4 = ((f32[8,7,8,128]{3,2,1,0:T(8,128)}), f32[8,7,8,128]{3,2,1,0:T(8,128)S(1)}, u32[]{:S(2)}, u32[]{:S(2)}) async-start(f32[8,7,8,128]{3,2,1,0:T(8,128)} %broadcast_in_dim.21), calls=%async_computation.4 | async-start | bytes 458752 | tf_op jit(solution)/shard_map/all_to_all | solution.py:31
  122.7 1.7 %convolve.1.local_ref = f32[256,640]{1,0:T(8,128)S(1)} custom-call(bf16[256,640]{1,0:T(8,128)(2,1)S(1)} %collective-permute-done.6.before_ref, bf16[256,640]{1,0:T(8,128)(2,1)S(1)} %get-tuple-element.23.values_ref, bf16[256,640]{1,0:T(8,128)(2,1)S(1)} %collective-permute-done.7.after_ref, bf16[27,640]{1,0:T(8,128)(2,1)S(1)} %copy-done.1), custom_call_target="tpu_custom_call" | custom-call | flops 8847360 | bytes 2097152 | tf_op jit(solution)/shard_map/convolve/pallas_call | solution.py:214
  124.4 4.5 %all-to-all-done.4.tiles_ref = f32[8,7,8,128]{3,2,1,0:T(8,128)S(1)} async-done(((f32[8,7,8,128]{3,2,1,0:T(8,128)}), f32[8,7,8,128]{3,2,1,0:T(8,128)S(1)}, u32[]{:S(2)}, u32[]{:S(2)}) %all-to-all-start.4) | async-done | bytes 229408 | tf_op jit(solution)/shard_map/all_to_all | solution.py:31
  128.9 1.4 %attend.1 = f32[256,640]{1,0:T(8,128)} custom-call(bf16[256,640]{1,0:T(8,128)(2,1)S(1)} %get-tuple-element.21.query_ref, f32[8,7,8,128]{3,2,1,0:T(8,128)S(1)} %all-to-all-done.4.tiles_ref, f32[256,640]{1,0:T(8,128)S(1)} %convolve.1.local_ref), custom_call_target="tpu_custom_call" | custom-call | flops 167772160 | bytes 3145728 | tf_op jit(solution)/shard_map/attend/pallas_call | solution.py:271
  (29 shorter events, 1.1 us)
Async XLA Ops:
  0.7 1.1 copy-start
  1.8 11.0 %copy-start.6 = (bf16[18,640]{1,0:T(8,128)(2,1)S(1)}, bf16[18,640]{1,0:T(8,128)(2,1)}, u32[]{:S(2)}) copy-start(bf16[18,640]{1,0:T(8,128)(2,1)} %param.9) | copy-start | bytes 69124
  1.8 11.0 %copy-start.7 = (bf16[18,640]{1,0:T(8,128)(2,1)S(1)}, bf16[18,640]{1,0:T(8,128)(2,1)}, u32[]{:S(2)}) copy-start(bf16[18,640]{1,0:T(8,128)(2,1)} %param.8) | copy-start | bytes 69124
  1.8 11.0 %copy-start.8 = (bf16[18,640]{1,0:T(8,128)(2,1)S(1)}, bf16[18,640]{1,0:T(8,128)(2,1)}, u32[]{:S(2)}) copy-start(bf16[18,640]{1,0:T(8,128)(2,1)} %param.10) | copy-start | bytes 69124
  2.0 34.0 %collective-permute-start.1 = (bf16[256,1152]{1,0:T(8,128)(2,1)S(1)}, bf16[256,1152]{1,0:T(8,128)(2,1)S(1)}, u32[]{:S(2)}, u32[]{:S(2)}) collective-permute-start(bf16[256,1152]{1,0:T(8,128)(2,1)S(1)} %norm.1.own_ref), channel_id=1, source_target_pairs={{0,64},{64,0},{1,65},{65,1},{2,66},{66,2},{3,67},{67,3},{4,68},{68... | collective-permute-start | bytes 1769480 | tf_op jit(solution)/shard_map/ppermute | solution.py:319
  10.8 25.2 %collective-permute-start = (bf16[256,1152]{1,0:T(8,128)(2,1)S(1)}, bf16[256,1152]{1,0:T(8,128)(2,1)S(1)}, u32[]{:S(2)}, u32[]{:S(2)}) collective-permute-start(bf16[256,1152]{1,0:T(8,128)(2,1)S(1)} %norm.1.own_ref), channel_id=1, source_target_pairs={{0,16},{16,0},{1,17},{17,1},{2,18},{18,2},{3,19},{19,3},{4,20},{20... | collective-permute-start | bytes 1769480 | tf_op jit(solution)/shard_map/ppermute | solution.py:319
  36.0 22.7 %copy-start.2 = (bf16[256,1152]{1,0:T(8,128)(2,1)}, bf16[256,1152]{1,0:T(8,128)(2,1)S(1)}, u32[]{:S(2)}) copy-start(bf16[256,1152]{1,0:T(8,128)(2,1)S(1)} %collective-permute-done.across_ref) | copy-start | bytes 1769476
  37.3 21.5 %all-to-all-start.1 = ((bf16[16,288,128]{2,1,0:T(8,128)(2,1)}), bf16[16,288,128]{2,1,0:T(8,128)(2,1)S(1)}, u32[]{:S(2)}, u32[]{:S(2)}) async-start(bf16[16,288,128]{2,1,0:T(8,128)(2,1)} %bitcast.11), calls=%async_computation.1 | async-start | bytes 2359296 | tf_op jit(solution)/shard_map/all_to_all | solution.py:31
  43.7 7.2 %collective-permute-start.2 = (bf16[256,1152]{1,0:T(8,128)(2,1)S(1)}, bf16[256,1152]{1,0:T(8,128)(2,1)S(1)}, u32[]{:S(2)}, u32[]{:S(2)}) collective-permute-start(bf16[256,1152]{1,0:T(8,128)(2,1)S(1)} %collective-permute-done.across_ref), channel_id=1, source_target_pairs={{0,64},{64,0},{1,65},{65,1},{2,66},{66,2},{3,67},{67,3},{4,68},{68... | collective-permute-start | bytes 1769480 | tf_op jit(solution)/shard_map/ppermute | solution.py:319
  50.9 0.8 copy-start.4
  58.7 1.1 copy-start.3
  59.8 1.1 copy-start.5
  70.4 34.9 %all-to-all-start.3 = ((bf16[16,56,128]{2,1,0:T(8,128)(2,1)}), bf16[16,56,128]{2,1,0:T(8,128)(2,1)S(1)}, u32[]{:S(2)}, u32[]{:S(2)}) async-start(bf16[16,56,128]{2,1,0:T(8,128)(2,1)} %broadcast_in_dim.9), calls=%async_computation.3 | async-start | bytes 458752 | tf_op jit(solution)/shard_map/all_to_all | solution.py:31
  81.3 7.3 %collective-permute-start.4 = (bf16[2,256,384]{2,1,0:T(8,128)(2,1)S(1)}, bf16[2,256,384]{2,1,0:T(8,128)(2,1)S(1)}, u32[]{:S(2)}, u32[]{:S(2)}) collective-permute-start(bf16[2,256,384]{2,1,0:T(8,128)(2,1)S(1)} %get-tuple-element.20.away_ref), channel_id=1, source_target_pairs={{0,64},{64,0},{1,65},{65,1},{2,66},{66,2},{3,67},{67,3},{4,68},{68... | collective-permute-start | bytes 1179656 | tf_op jit(solution)/shard_map/ppermute | solution.py:319
  86.6 36.0 %copy-start.1 = (bf16[27,640]{1,0:T(8,128)(2,1)S(1)}, bf16[27,640]{1,0:T(8,128)(2,1)}, u32[]{:S(2)}) copy-start(bf16[27,640]{1,0:T(8,128)(2,1)} %weight_ref.1) | copy-start | bytes 103684
  86.6 8.4 %collective-permute-start.3 = (bf16[1,256,384]{2,1,0:T(8,128)(2,1)S(1)}, bf16[1,256,384]{2,1,0:T(8,128)(2,1)S(1)}, u32[]{:S(2)}, u32[]{:S(2)}) collective-permute-start(bf16[1,256,384]{2,1,0:T(8,128)(2,1)S(1)} %slice.6), channel_id=1, source_target_pairs={{0,16},{16,0},{1,17},{17,1},{2,18},{18,2},{3,19},{19,3},{4,20},{20... | collective-permute-start | bytes 589832 | tf_op jit(solution)/shard_map/ppermute | solution.py:319
  88.6 10.7 %collective-permute-start.5 = (bf16[1,256,384]{2,1,0:T(8,128)(2,1)S(1)}, bf16[1,256,384]{2,1,0:T(8,128)(2,1)S(1)}, u32[]{:S(2)}, u32[]{:S(2)}) collective-permute-start(bf16[1,256,384]{2,1,0:T(8,128)(2,1)S(1)} %slice.8), channel_id=1, source_target_pairs={{0,16},{16,0},{1,17},{17,1},{2,18},{18,2},{3,19},{19,3},{4,20},{20... | collective-permute-start | bytes 589832 | tf_op jit(solution)/shard_map/ppermute | solution.py:319
  99.8 10.7 %collective-permute-start.7 = (bf16[256,640]{1,0:T(8,128)(2,1)S(1)}, bf16[256,640]{1,0:T(8,128)(2,1)S(1)}, u32[]{:S(2)}, u32[]{:S(2)}) collective-permute-start(bf16[256,640]{1,0:T(8,128)(2,1)S(1)} %get-tuple-element.23.values_ref), channel_id=1, source_target_pairs={{1,0},{2,1},{3,2},{4,3},{5,4},{6,5},{7,6},{8,7},{9,8},{10,9},{11,1... | collective-permute-start | bytes 983048 | tf_op jit(solution)/shard_map/ppermute | solution.py:341
  101.1 10.3 %collective-permute-start.6 = (bf16[256,640]{1,0:T(8,128)(2,1)S(1)}, bf16[256,640]{1,0:T(8,128)(2,1)S(1)}, u32[]{:S(2)}, u32[]{:S(2)}) collective-permute-start(bf16[256,640]{1,0:T(8,128)(2,1)S(1)} %get-tuple-element.23.values_ref), channel_id=1, source_target_pairs={{0,1},{1,2},{2,3},{3,4},{4,5},{5,6},{6,7},{7,8},{8,9},{9,10},{10,1... | collective-permute-start | bytes 983048 | tf_op jit(solution)/shard_map/ppermute | solution.py:340
  112.1 16.8 %all-to-all-start.4 = ((f32[8,7,8,128]{3,2,1,0:T(8,128)}), f32[8,7,8,128]{3,2,1,0:T(8,128)S(1)}, u32[]{:S(2)}, u32[]{:S(2)}) async-start(f32[8,7,8,128]{3,2,1,0:T(8,128)} %broadcast_in_dim.21), calls=%async_computation.4 | async-start | bytes 458752 | tf_op jit(solution)/shard_map/all_to_all | solution.py:31

commit v8 on v6

--- a/solution.py
+++ b/solution.py
@@ -17,6 +17,7 @@
 AXES = ("y", "core", "x", "zh", "zl")
 ZAX = ("zh", "zl")
 TM = ("x", "zh", "zl")
+NEAR = ("x", "zl")
 PARAMS = pltpu.CompilerParams(vmem_limit_bytes=16 * 1024 * 1024)
 
 
@@ -36,7 +37,7 @@
 def norm_kernel(tokens_ref, gain_ref, out_ref):
     x = tokens_ref[...].astype(jnp.float32)
     scale = lax.rsqrt(jnp.mean(x * x, axis=1, keepdims=True) + 1e-06)
-    out_ref[...] = (x * scale * gain_ref[...].astype(jnp.float32)).astype(jnp.bfloat16)
+    out_ref[...] = (x * scale * gain_ref[...].astype(jnp.float32)[None]).astype(jnp.bfloat16)
 
 
 def norm(tokens, gain):
@@ -46,34 +47,34 @@
         compiler_params=PARAMS,
         cost_estimate=cost(10 * tokens.size, 4 * tokens.size),
         name="norm",
-    )(tokens, gain.reshape(1, -1))
-
-
-def project_kernel(mine_ref, theirs_ref, weight_ref, own_ref, other_ref):
+    )(tokens, gain)
+
+
+def project_kernel(tokens_ref, weight_ref, out_ref):
     first = lax.axis_index("core") == 0
-    for step in range(weight_ref.shape[0]):
-        weight = weight_ref[step]
-        for tokens_ref, out_ref in ((mine_ref, own_ref), (theirs_ref, other_ref)):
-            both = jnp.dot(tokens_ref[...], weight, preferred_element_type=jnp.float32)
-            for half in range(2):
-                unit = 2 * step + half
-                proj = both[:, half * LANES : (half + 1) * LANES]
-                feat = jnp.where(proj > 0, proj, jnp.exp(jnp.minimum(proj, 0.0)) - 1.0) + 1.0
-                if unit < GROUPS:
-                    feat = jnp.where(first, proj, feat)
-                out_ref[:, unit * LANES : (unit + 1) * LANES] = feat.astype(jnp.bfloat16)
-
-
-def project(mine, theirs, weights):
-    steps, depth, _ = weights.shape
-    rows = mine.shape[0]
+    for step in range(4):
+        places = [jnp.where(first, 4 * step + x, 4 * x + step) for x in range(4)]
+        weight = jnp.concatenate([weight_ref[place] for place in places], axis=0)
+        both = jnp.dot(tokens_ref[...], weight, preferred_element_type=jnp.float32)
+        for half in range(2):
+            unit = 2 * step + half
+            proj = both[:, half * LANES : (half + 1) * LANES]
+            feat = jnp.where(proj > 0, proj, jnp.exp(jnp.minimum(proj, 0.0)) - 1.0) + 1.0
+            if unit < GROUPS:
+                feat = jnp.where(first, proj, feat)
+            out_ref[:, unit * LANES : (unit + 1) * LANES] = feat.astype(jnp.bfloat16)
+
+
+def project(tokens, weights):
+    rows, depth = tokens.shape
+    steps = 4
     return pl.pallas_call(
         project_kernel,
-        out_shape=[jax.ShapeDtypeStruct((rows, steps * BLOCK), jnp.bfloat16)] * 2,
-        compiler_params=PARAMS,
-        cost_estimate=cost(4 * rows * depth * steps * BLOCK, 5 * 1024 * 1024),
+        out_shape=jax.ShapeDtypeStruct((rows, steps * BLOCK), jnp.bfloat16),
+        compiler_params=PARAMS,
+        cost_estimate=cost(2 * rows * depth * steps * BLOCK, 4 * 1024 * 1024),
         name="project",
-    )(mine, theirs, weights)
+    )(tokens, weights)
 
 
 def unit_of(core, mine_ref, theirs_ref, unit):
@@ -156,8 +157,10 @@
 def split_dot(a, b):
     high = b.astype(jnp.bfloat16)
     low = (b - high.astype(jnp.float32)).astype(jnp.bfloat16)
-    return jnp.dot(a, high, preferred_element_type=jnp.float32) + jnp.dot(
-        a, low, preferred_element_type=jnp.float32
+    return jnp.dot(
+        jnp.concatenate([a, a], axis=1),
+        jnp.concatenate([high, low], axis=0),
+        preferred_element_type=jnp.float32,
     )
 
 
@@ -188,6 +191,17 @@
     )(mine, theirs, tiles, local)
 
 
+def spread_crossed(block, turn):
+    ys, xs = lax.axis_size("y"), lax.axis_size("x")
+    place = lambda core, y, x: (core * ys + y) * xs + x
+    along_x = [[place(turn, y, x) for x in range(xs)] for y in range(ys)]
+    along_y = [[place(1 - turn, y, x) for y in range(ys)] for x in range(xs)]
+    blocks = jnp.broadcast_to(block[None], (xs,) + block.shape)
+    return lax.all_to_all(
+        blocks, ("core", "y", "x"), 0, 0, tiled=True, axis_index_groups=along_x + along_y
+    )
+
+
 def swap(block):
     return lax.ppermute(block, "core", [(0, 1), (1, 0)])
 
@@ -207,27 +221,28 @@
     column = spread(pick(w_query, w_key, w_value), ZAX)
     column = jnp.concatenate([column[:, :rows], column[:, rows:]], axis=2).reshape(-1, BLOCK)
     column, other = lax.optimization_barrier((column, other))
-    weights = spread(column, ("y", "x")).reshape(lax.axis_size("y"), -1, BLOCK)
-
-    mine, theirs = project(normed, other, weights)
-    theirs = swap(theirs)
+    weights = spread_crossed(spread_crossed(column, 0).reshape(-1, BLOCK), 1)
+    weights = weights.reshape((-1,) + column.shape)
+
+    theirs = swap(project(other, weights))
+    mine = project(normed, weights)
     values, tiles = states(mine, theirs)
     count = lax.axis_size(TM)
     before = lax.ppermute(values, TM, [(i, i + 1) for i in range(count - 1)])
     after = lax.ppermute(values, TM, [(i + 1, i) for i in range(count - 1)])
 
-    share = TILES // lax.axis_size("x")
-    part = jnp.sum(exchange(tiles, "x").reshape((-1, share) + tiles.shape[1:]), axis=0)
+    share = TILES // lax.axis_size(NEAR)
+    part = jnp.sum(exchange(tiles, NEAR).reshape((-1, share) + tiles.shape[1:]), axis=0)
     part = part.astype(jnp.bfloat16).reshape(-1, LANES)
+    part = jnp.sum(spread(part, "zh").astype(jnp.float32), axis=0)
     local = convolve(before, values, after, conv_weight)
-    part = jnp.sum(spread(part, ZAX).astype(jnp.float32), axis=0)
     part, local = lax.optimization_barrier((part, local))
-    tiles = spread(part.reshape((share,) + tiles.shape[1:]), "x").reshape(tiles.shape)
+    tiles = spread(part.reshape((share,) + tiles.shape[1:]), NEAR).reshape(tiles.shape)
     return attend(mine, theirs, tiles, local)
 
 
 def solution(mesh):
-    fine = Mesh(mesh.devices.reshape(4, 2, 4, 4, 4), AXES)
+    fine = Mesh(mesh.devices.reshape(4, 2, 4, 8, 2), AXES)
     rows = P(AXES, None)
     split = P(TM, None)
     return jax.shard_map(

time: 120 us -> 115 us (0.958)
  blocking collectives: 49.9 us -> 45 us
    all_to_all x3 -> x1, blocking collectives: 49.9 us -> 11.3 us  [exchange(): return lax.all_to_all(blocks, axes, 0, 0, tiled=True)]
    all_to_all x0 -> x2, blocking collectives: none -> 33.8 us  [spread_crossed(): lax.all_to_all(blocks, ('core', 'y', 'x'), 0, 0, tiled=True, axis_index_g...]
    ppermute x1, waiting for transfers between devices: 9.09 us -> 0.01 us  [body(): after = lax.ppermute(values, TM, [(i + 1, i) for i in range(count - 1)])]
    all_to_all x2 -> x3, waiting for transfers between devices: 11.7 us -> 16.4 us  [exchange(): return lax.all_to_all(blocks, axes, 0, 0, tiled=True)]
    ppermute x1, waiting for transfers between devices: 2.33 us -> 6.63 us  [body(): before = lax.ppermute(values, TM, [(i, i + 1) for i in range(count - 1)])]
    all_to_all x2 -> x3, starting transfers between devices: 23 us -> 24.8 us  [exchange(): return lax.all_to_all(blocks, axes, 0, 0, tiled=True)]
    ppermute x1, starting transfers between devices: 5.94 us -> 4.59 us  [body(): after = lax.ppermute(values, TM, [(i + 1, i) for i in range(count - 1)])]
  transfers between devices with their start and end apart: 6 -> 7, of which waited for: 4 -> 4; matrix products, arithmetic and copies ran while one was open for 1% -> 1% of each run, Pallas kernels for 2% -> 3%
where the time goes in v8:
time: 115 us
  blocking collectives  45 us (39%)
  starting transfers between devices  35.2 us (31%)
  waiting for transfers between devices  23.9 us (21%)
  Pallas kernels  6.12 us (5%)
  local copies, waits for them, and re-layouts  3.44 us (3%)
    all_to_all x2, blocking collectives, spread_crossed(): lax.all_to_all(blocks, ('core', 'y', 'x'), 0, 0, tiled=True, axis_index_g...  33.8 us
    all_to_all x3, starting transfers between devices, exchange(): return lax.all_to_all(blocks, axes, 0, 0, tiled=True)  24.8 us
    all_to_all x3, waiting for transfers between devices, exchange(): return lax.all_to_all(blocks, axes, 0, 0, tiled=True)  16.4 us
    all_to_all x1, blocking collectives, exchange(): return lax.all_to_all(blocks, axes, 0, 0, tiled=True)  11.3 us
    ppermute x1, waiting for transfers between devices, body(): before = lax.ppermute(values, TM, [(i, i + 1) for i in range(count - 1)])  6.63 us
    ppermute x1, starting transfers between devices, body(): after = lax.ppermute(values, TM, [(i + 1, i) for i in range(count - 1)])  4.59 us
    ppermute x2, starting transfers between devices, swap(): return lax.ppermute(block, 'core', [(0, 1), (1, 0)])  3.84 us
  transfers between devices with their start and end apart: 7, of which 4 were waited for; matrix products, arithmetic and copies ran while one was open for 1% of the time, Pallas kernels for 3%

profile of v8, /device:TPU:2, one launch (start us, length us, event | category | flops | bytes accessed | tf_op | source)
XLA Modules:
  0.0 114.7 jit_solution(6939275382356944175)
XLA Ops:
  0.0 0.1 pad_dynamic-slice_fusion.3
  0.1 0.7 fusion.2
  0.8 0.7 broadcast_in_dim.17
  1.5 15.2 %all-to-all-start = ((bf16[16,36,128]{2,1,0:T(8,128)(2,1)}), bf16[16,36,128]{2,1,0:T(8,128)(2,1)S(1)}, u32[]{:S(2)}, u32[]{:S(2)}) async-start(bf16[16,36,128]{2,1,0:T(8,128)(2,1)} %broadcast_in_dim.17), calls=%async_computation | async-start | bytes 327680 | tf_op jit(solution)/shard_map/all_to_all | solution.py:29
  16.7 0.0 copy-start
  16.7 1.1 copy-done
  17.8 0.7 copy-done.2
  18.5 0.2 norm.1.tokens_ref
  18.7 1.9 %collective-permute-start = (bf16[256,1152]{1,0:T(8,128)(2,1)S(1)}, bf16[256,1152]{1,0:T(8,128)(2,1)S(1)}, u32[]{:S(2)}, u32[]{:S(2)}) collective-permute-start(bf16[256,1152]{1,0:T(8,128)(2,1)S(1)} %norm.1.tokens_ref), channel_id=1, source_target_pairs={{0,64},{64,0},{1,65},{65,1},{2,66},{66,2},{3,67},{67,3},{4,68},{68... | collective-permute-start | bytes 1769480 | tf_op jit(solution)/shard_map/ppermute | solution.py:206
  20.7 11.7 %all-to-all-done = bf16[16,36,128]{2,1,0:T(8,128)(2,1)S(1)} async-done(((bf16[16,36,128]{2,1,0:T(8,128)(2,1)}), bf16[16,36,128]{2,1,0:T(8,128)(2,1)S(1)}, u32[]{:S(2)}, u32[]{:S(2)}) %all-to-all-start) | async-done | bytes 147488 | tf_op jit(solution)/shard_map/all_to_all | solution.py:29
  32.4 0.1 reshape.22
  32.5 0.0 collective-permute-done.tokens_ref
  32.6 11.6 %all_to_all.30 = bf16[4,288,256]{2,1,0:T(8,128)(2,1)S(1)} all-to-all(bf16[4,288,256]{2,1,0:T(8,128)(2,1)S(1)} %broadcast_in_dim.36), channel_id=1, replica_groups={{0,16,32,48},{128,144,160,176},{256,272,288,304},{384,400,416,432},{64,..., dimensions={0} | all-to-all | bytes 1179648 | tf_op jit(solution)/shard_map/all_to_all | solution.py:200
  44.2 0.2 broadcast_in_dim.38
  44.3 22.2 %all_to_all.31 = bf16[4,1152,256]{2,1,0:T(8,128)(2,1)S(1)} all-to-all(bf16[4,1152,256]{2,1,0:T(8,128)(2,1)S(1)} %broadcast_in_dim.38), channel_id=1, replica_groups={{64,80,96,112},{192,208,224,240},{320,336,352,368},{448,464,480,496},{0..., dimensions={0} | all-to-all | bytes 4718592 | tf_op jit(solution)/shard_map/all_to_all | solution.py:200
  66.5 0.9 project.3
  67.4 0.0 copy-start.1
  67.4 1.9 %collective-permute-start.1 = (bf16[256,1024]{1,0:T(8,128)(2,1)S(1)}, bf16[256,1024]{1,0:T(8,128)(2,1)S(1)}, u32[]{:S(2)}, u32[]{:S(2)}) collective-permute-start(bf16[256,1024]{1,0:T(8,128)(2,1)S(1)} %project.3), channel_id=1, source_target_pairs={{0,64},{64,0},{1,65},{65,1},{2,66},{66,2},{3,67},{67,3},{4,68},{68... | collective-permute-start | bytes 1572872 | tf_op jit(solution)/shard_map/ppermute | solution.py:206
  69.4 0.9 project.2.mine_ref
  70.3 0.9 collective-permute-done.1.theirs_ref
  71.3 1.0 states.1
  72.3 4.9 %all-to-all-start.3 = ((f32[24,8,128]{2,1,0:T(8,128)}), f32[24,8,128]{2,1,0:T(8,128)S(1)}, u32[]{:S(2)}, u32[]{:S(2)}) async-start(f32[24,8,128]{2,1,0:T(8,128)} %get-tuple-element.13), calls=%async_computation.3 | async-start | bytes 196608 | tf_op jit(solution)/shard_map/all_to_all | solution.py:29
  77.2 4.6 %collective-permute-start.3 = (bf16[256,640]{1,0:T(8,128)(2,1)S(1)}, bf16[256,640]{1,0:T(8,128)(2,1)S(1)}, u32[]{:S(2)}, u32[]{:S(2)}) collective-permute-start(bf16[256,640]{1,0:T(8,128)(2,1)S(1)} %get-tuple-element.14.values_ref), channel_id=1, source_target_pairs={{1,0},{2,1},{3,2},{4,3},{5,4},{6,5},{7,6},{8,7},{9,8},{10,9},{11,1... | collective-permute-start | bytes 983048 | tf_op jit(solution)/shard_map/ppermute | solution.py:232
  81.8 1.9 %collective-permute-start.2 = (bf16[256,640]{1,0:T(8,128)(2,1)S(1)}, bf16[256,640]{1,0:T(8,128)(2,1)S(1)}, u32[]{:S(2)}, u32[]{:S(2)}) collective-permute-start(bf16[256,640]{1,0:T(8,128)(2,1)S(1)} %get-tuple-element.14.values_ref), channel_id=1, source_target_pairs={{0,1},{1,2},{2,3},{3,4},{4,5},{5,6},{6,7},{7,8},{8,9},{9,10},{10,1... | collective-permute-start | bytes 983048 | tf_op jit(solution)/shard_map/ppermute | solution.py:231
  83.7 0.0 all-to-all-done.3
  83.7 0.6 broadcast_in_dim.39
  84.4 4.7 %all-to-all-start.4 = ((bf16[8,24,128]{2,1,0:T(8,128)(2,1)}), bf16[8,24,128]{2,1,0:T(8,128)(2,1)S(1)}, u32[]{:S(2)}, u32[]{:S(2)}) async-start(bf16[8,24,128]{2,1,0:T(8,128)(2,1)} %broadcast_in_dim.39), calls=%async_computation.4 | async-start | bytes 98304 | tf_op jit(solution)/shard_map/all_to_all | solution.py:29
  89.1 6.6 %collective-permute-done.2.before_ref = bf16[256,640]{1,0:T(8,128)(2,1)S(1)} collective-permute-done((bf16[256,640]{1,0:T(8,128)(2,1)S(1)}, bf16[256,640]{1,0:T(8,128)(2,1)S(1)}, u32[]{:S(2)}, u32[]{:S(2)}) %collective-permute-start.2) | collective-permute-done | bytes 327712 | tf_op jit(solution)/shard_map/ppermute | solution.py:231
  95.8 1.7 %convolve.1.local_ref = f32[256,640]{1,0:T(8,128)S(1)} custom-call(bf16[256,640]{1,0:T(8,128)(2,1)S(1)} %collective-permute-done.2.before_ref, bf16[256,640]{1,0:T(8,128)(2,1)S(1)} %get-tuple-element.14.values_ref, bf16[256,640]{1,0:T(8,128)(2,1)S(1)} %collective-permute-done.3.after_ref, bf16[27,640]{1,0:T(8,128)(2,1)S(1)} %copy-done.1), custom_call_target="tpu_custom_call" | custom-call | flops 8847360 | bytes 2097152 | tf_op jit(solution)/shard_map/convolve/pallas_call | solution.py:145
  97.5 4.6 %all-to-all-done.4 = bf16[8,24,128]{2,1,0:T(8,128)(2,1)S(1)} async-done(((bf16[8,24,128]{2,1,0:T(8,128)(2,1)}), bf16[8,24,128]{2,1,0:T(8,128)(2,1)S(1)}, u32[]{:S(2)}, u32[]{:S(2)}) %all-to-all-start.4) | async-done | bytes 49184 | tf_op jit(solution)/shard_map/all_to_all | solution.py:29
  102.1 11.3 %all_to_all.32 = f32[8,3,8,128]{3,2,1,0:T(8,128)S(1)} all-to-all(f32[8,3,8,128]{3,2,1,0:T(8,128)S(1)} %broadcast_in_dim.41), channel_id=1, replica_groups=mesh['y'=4,'core'=2,'x'=4,'zh'=8,'zl'=2] {'x','zl'}, dimensions={0} | all-to-all | bytes 196608 | tf_op jit(solution)/shard_map/all_to_all | solution.py:29
  113.4 1.3 %attend.1 = f32[256,640]{1,0:T(8,128)} custom-call(bf16[256,1024]{1,0:T(8,128)(2,1)S(1)} %project.2.mine_ref, bf16[256,1024]{1,0:T(8,128)(2,1)S(1)} %collective-permute-done.1.theirs_ref, f32[24,8,128]{2,1,0:T(8,128)S(1)} %bitcast.10, f32[256,640]{1,0:T(8,128)S(1)} %convolve.1.local_ref), custom_call_target="tpu_custom_call" | custom-call | flops 167772160 | bytes 3145728 | tf_op jit(solution)/shard_map/attend/pallas_call | solution.py:185
  (12 shorter events, 0.2 us)
Async XLA Ops:
  1.5 30.9 %all-to-all-start = ((bf16[16,36,128]{2,1,0:T(8,128)(2,1)}), bf16[16,36,128]{2,1,0:T(8,128)(2,1)S(1)}, u32[]{:S(2)}, u32[]{:S(2)}) async-start(bf16[16,36,128]{2,1,0:T(8,128)(2,1)} %broadcast_in_dim.17), calls=%async_computation | async-start | bytes 327680 | tf_op jit(solution)/shard_map/all_to_all | solution.py:29
  16.7 1.1 copy-start
  17.8 0.7 copy-start.2
  18.7 13.8 %collective-permute-start = (bf16[256,1152]{1,0:T(8,128)(2,1)S(1)}, bf16[256,1152]{1,0:T(8,128)(2,1)S(1)}, u32[]{:S(2)}, u32[]{:S(2)}) collective-permute-start(bf16[256,1152]{1,0:T(8,128)(2,1)S(1)} %norm.1.tokens_ref), channel_id=1, source_target_pairs={{0,64},{64,0},{1,65},{65,1},{2,66},{66,2},{3,67},{67,3},{4,68},{68... | collective-permute-start | bytes 1769480 | tf_op jit(solution)/shard_map/ppermute | solution.py:206
  67.4 28.3 %copy-start.1 = (bf16[27,640]{1,0:T(8,128)(2,1)S(1)}, bf16[27,640]{1,0:T(8,128)(2,1)}, u32[]{:S(2)}) copy-start(bf16[27,640]{1,0:T(8,128)(2,1)} %weight_ref.1) | copy-start | bytes 103684
  67.4 3.8 %collective-permute-start.1 = (bf16[256,1024]{1,0:T(8,128)(2,1)S(1)}, bf16[256,1024]{1,0:T(8,128)(2,1)S(1)}, u32[]{:S(2)}, u32[]{:S(2)}) collective-permute-start(bf16[256,1024]{1,0:T(8,128)(2,1)S(1)} %project.3), channel_id=1, source_target_pairs={{0,64},{64,0},{1,65},{65,1},{2,66},{66,2},{3,67},{67,3},{4,68},{68... | collective-permute-start | bytes 1572872 | tf_op jit(solution)/shard_map/ppermute | solution.py:206
  72.3 11.4 %all-to-all-start.3 = ((f32[24,8,128]{2,1,0:T(8,128)}), f32[24,8,128]{2,1,0:T(8,128)S(1)}, u32[]{:S(2)}, u32[]{:S(2)}) async-start(f32[24,8,128]{2,1,0:T(8,128)} %get-tuple-element.13), calls=%async_computation.3 | async-start | bytes 196608 | tf_op jit(solution)/shard_map/all_to_all | solution.py:29
  77.2 11.9 %collective-permute-start.3 = (bf16[256,640]{1,0:T(8,128)(2,1)S(1)}, bf16[256,640]{1,0:T(8,128)(2,1)S(1)}, u32[]{:S(2)}, u32[]{:S(2)}) collective-permute-start(bf16[256,640]{1,0:T(8,128)(2,1)S(1)} %get-tuple-element.14.values_ref), channel_id=1, source_target_pairs={{1,0},{2,1},{3,2},{4,3},{5,4},{6,5},{7,6},{8,7},{9,8},{10,9},{11,1... | collective-permute-start | bytes 983048 | tf_op jit(solution)/shard_map/ppermute | solution.py:232
  81.8 14.0 %collective-permute-start.2 = (bf16[256,640]{1,0:T(8,128)(2,1)S(1)}, bf16[256,640]{1,0:T(8,128)(2,1)S(1)}, u32[]{:S(2)}, u32[]{:S(2)}) collective-permute-start(bf16[256,640]{1,0:T(8,128)(2,1)S(1)} %get-tuple-element.14.values_ref), channel_id=1, source_target_pairs={{0,1},{1,2},{2,3},{3,4},{4,5},{5,6},{6,7},{7,8},{8,9},{9,10},{10,1... | collective-permute-start | bytes 983048 | tf_op jit(solution)/shard_map/ppermute | solution.py:231
  84.4 17.7 %all-to-all-start.4 = ((bf16[8,24,128]{2,1,0:T(8,128)(2,1)}), bf16[8,24,128]{2,1,0:T(8,128)(2,1)S(1)}, u32[]{:S(2)}, u32[]{:S(2)}) async-start(bf16[8,24,128]{2,1,0:T(8,128)(2,1)} %broadcast_in_dim.39), calls=%async_computation.4 | async-start | bytes 98304 | tf_op jit(solution)/shard_map/all_to_all | solution.py:29

commit v9 on v8

--- a/solution.py
+++ b/solution.py
@@ -234,10 +234,11 @@
     share = TILES // lax.axis_size(NEAR)
     part = jnp.sum(exchange(tiles, NEAR).reshape((-1, share) + tiles.shape[1:]), axis=0)
     part = part.astype(jnp.bfloat16).reshape(-1, LANES)
-    part = jnp.sum(spread(part, "zh").astype(jnp.float32), axis=0)
+    part = spread(part, ZAX).astype(jnp.float32)
+    part = jnp.sum(part.reshape((lax.axis_size("zh"), -1) + part.shape[1:]), axis=0)
+    part, before, after = lax.optimization_barrier((part, before, after))
     local = convolve(before, values, after, conv_weight)
-    part, local = lax.optimization_barrier((part, local))
-    tiles = spread(part.reshape((share,) + tiles.shape[1:]), NEAR).reshape(tiles.shape)
+    tiles = spread(part.reshape((-1,) + tiles.shape[1:]), "x").reshape(tiles.shape)
     return attend(mine, theirs, tiles, local)
 
 

time: 115 us -> 115 us (level)
  blocking collectives: 45 us -> 43.5 us
  waiting for transfers between devices: 23.9 us -> 25.4 us
    all_to_all x3, waiting for transfers between devices: 16.4 us -> 19.5 us  [exchange(): return lax.all_to_all(blocks, axes, 0, 0, tiled=True)]
    all_to_all x3, starting transfers between devices: 24.8 us -> 23.1 us  [exchange(): return lax.all_to_all(blocks, axes, 0, 0, tiled=True)]
    ppermute x1, waiting for transfers between devices: 6.63 us -> 4.9 us  [body(): before = lax.ppermute(values, TM, [(i, i + 1) for i in range(count - 1)])]
    all_to_all x1, blocking collectives: 11.3 us -> 9.69 us  [exchange(): return lax.all_to_all(blocks, axes, 0, 0, tiled=True)]
    ppermute x1, starting transfers between devices: 4.59 us -> 6.04 us  [body(): after = lax.ppermute(values, TM, [(i + 1, i) for i in range(count - 1)])]
  transfers between devices with their start and end apart: 7 -> 7, of which waited for: 4 -> 6; matrix products, arithmetic and copies ran while one was open for 1% -> 0% of each run, Pallas kernels for 3% -> 3%
where the time goes in v9:
time: 115 us; the launch traced here: 114 us
  blocking collectives  43.5 us (38%)
  starting transfers between devices  34.9 us (30%)
  waiting for transfers between devices  25.4 us (22%)
  Pallas kernels  5.46 us (5%)
  local copies, waits for them, and re-layouts  4.1 us (4%)
    all_to_all x2, blocking collectives, spread_crossed(): lax.all_to_all(blocks, ('core', 'y', 'x'), 0, 0, tiled=True, axis_index_g...  33.8 us
    all_to_all x3, starting transfers between devices, exchange(): return lax.all_to_all(blocks, axes, 0, 0, tiled=True)  23.1 us
    all_to_all x3, waiting for transfers between devices, exchange(): return lax.all_to_all(blocks, axes, 0, 0, tiled=True)  19.5 us
    all_to_all x1, blocking collectives, exchange(): return lax.all_to_all(blocks, axes, 0, 0, tiled=True)  9.69 us
    ppermute x1, starting transfers between devices, body(): after = lax.ppermute(values, TM, [(i + 1, i) for i in range(count - 1)])  6.04 us
    ppermute x1, waiting for transfers between devices, body(): before = lax.ppermute(values, TM, [(i, i + 1) for i in range(count - 1)])  4.9 us
    ppermute x2, starting transfers between devices, swap(): return lax.ppermute(block, 'core', [(0, 1), (1, 0)])  3.84 us
  transfers between devices with their start and end apart: 7, of which 6 were waited for; matrix products, arithmetic and copies ran while one was open for 0% of the time, Pallas kernels for 3%

profile of v9, /device:TPU:2, one launch (start us, length us, event | category | flops | bytes accessed | tf_op | source)
XLA Modules:
  0.0 114.3 jit_solution(1104908254868447356)
XLA Ops:
  0.0 0.1 pad_dynamic-slice_fusion.3
  0.1 0.7 fusion.2
  0.8 0.7 broadcast_in_dim.17
  1.5 15.2 %all-to-all-start = ((bf16[16,36,128]{2,1,0:T(8,128)(2,1)}), bf16[16,36,128]{2,1,0:T(8,128)(2,1)S(1)}, u32[]{:S(2)}, u32[]{:S(2)}) async-start(bf16[16,36,128]{2,1,0:T(8,128)(2,1)} %broadcast_in_dim.17), calls=%async_computation | async-start | bytes 327680 | tf_op jit(solution)/shard_map/all_to_all | solution.py:29
  16.7 0.0 copy-start
  16.7 1.1 copy-done
  17.8 0.7 copy-done.2
  18.5 0.2 norm.1.tokens_ref
  18.7 1.9 %collective-permute-start = (bf16[256,1152]{1,0:T(8,128)(2,1)S(1)}, bf16[256,1152]{1,0:T(8,128)(2,1)S(1)}, u32[]{:S(2)}, u32[]{:S(2)}) collective-permute-start(bf16[256,1152]{1,0:T(8,128)(2,1)S(1)} %norm.1.tokens_ref), channel_id=1, source_target_pairs={{0,64},{64,0},{1,65},{65,1},{2,66},{66,2},{3,67},{67,3},{4,68},{68... | collective-permute-start | bytes 1769480 | tf_op jit(solution)/shard_map/ppermute | solution.py:206
  20.7 11.7 %all-to-all-done = bf16[16,36,128]{2,1,0:T(8,128)(2,1)S(1)} async-done(((bf16[16,36,128]{2,1,0:T(8,128)(2,1)}), bf16[16,36,128]{2,1,0:T(8,128)(2,1)S(1)}, u32[]{:S(2)}, u32[]{:S(2)}) %all-to-all-start) | async-done | bytes 147488 | tf_op jit(solution)/shard_map/all_to_all | solution.py:29
  32.4 0.1 reshape.28
  32.6 11.6 %all_to_all.30 = bf16[4,288,256]{2,1,0:T(8,128)(2,1)S(1)} all-to-all(bf16[4,288,256]{2,1,0:T(8,128)(2,1)S(1)} %broadcast_in_dim.36), channel_id=1, replica_groups={{0,16,32,48},{128,144,160,176},{256,272,288,304},{384,400,416,432},{64,..., dimensions={0} | all-to-all | bytes 1179648 | tf_op jit(solution)/shard_map/all_to_all | solution.py:200
  44.2 0.2 broadcast_in_dim.38
  44.3 22.2 %all_to_all.31 = bf16[4,1152,256]{2,1,0:T(8,128)(2,1)S(1)} all-to-all(bf16[4,1152,256]{2,1,0:T(8,128)(2,1)S(1)} %broadcast_in_dim.38), channel_id=1, replica_groups={{64,80,96,112},{192,208,224,240},{320,336,352,368},{448,464,480,496},{0..., dimensions={0} | all-to-all | bytes 4718592 | tf_op jit(solution)/shard_map/all_to_all | solution.py:200
  66.5 0.9 project.3
  67.4 1.9 %collective-permute-start.1 = (bf16[256,1024]{1,0:T(8,128)(2,1)S(1)}, bf16[256,1024]{1,0:T(8,128)(2,1)S(1)}, u32[]{:S(2)}, u32[]{:S(2)}) collective-permute-start(bf16[256,1024]{1,0:T(8,128)(2,1)S(1)} %project.3), channel_id=1, source_target_pairs={{0,64},{64,0},{1,65},{65,1},{2,66},{66,2},{3,67},{67,3},{4,68},{68... | collective-permute-start | bytes 1572872 | tf_op jit(solution)/shard_map/ppermute | solution.py:206
  69.4 0.9 project.2.mine_ref
  70.3 0.9 collective-permute-done.1.theirs_ref
  71.3 0.4 states.1
  71.6 9.7 %all_to_all.32 = f32[24,8,128]{2,1,0:T(8,128)S(1)} all-to-all(f32[24,8,128]{2,1,0:T(8,128)S(1)} %get-tuple-element.14), channel_id=1, replica_groups=mesh['y'=4,'core'=2,'x'=4,'zh'=8,'zl'=2] {'x','zl'}, dimensions={0} | all-to-all | bytes 196608 | tf_op jit(solution)/shard_map/all_to_all | solution.py:29
  81.3 0.7 broadcast_in_dim.39
  82.0 4.1 %all-to-all-start.4 = ((bf16[16,24,128]{2,1,0:T(8,128)(2,1)}), bf16[16,24,128]{2,1,0:T(8,128)(2,1)S(1)}, u32[]{:S(2)}, u32[]{:S(2)}) async-start(bf16[16,24,128]{2,1,0:T(8,128)(2,1)} %broadcast_in_dim.39), calls=%async_computation.4 | async-start | bytes 196608 | tf_op jit(solution)/shard_map/all_to_all | solution.py:29
  86.1 6.0 %collective-permute-start.3 = (bf16[256,640]{1,0:T(8,128)(2,1)S(1)}, bf16[256,640]{1,0:T(8,128)(2,1)S(1)}, u32[]{:S(2)}, u32[]{:S(2)}) collective-permute-start(bf16[256,640]{1,0:T(8,128)(2,1)S(1)} %get-tuple-element.15.values_ref), channel_id=1, source_target_pairs={{1,0},{2,1},{3,2},{4,3},{5,4},{6,5},{7,6},{8,7},{9,8},{10,9},{11,1... | collective-permute-start | bytes 983048 | tf_op jit(solution)/shard_map/ppermute | solution.py:232
  92.1 1.9 %collective-permute-start.2 = (bf16[256,640]{1,0:T(8,128)(2,1)S(1)}, bf16[256,640]{1,0:T(8,128)(2,1)S(1)}, u32[]{:S(2)}, u32[]{:S(2)}) collective-permute-start(bf16[256,640]{1,0:T(8,128)(2,1)S(1)} %get-tuple-element.15.values_ref), channel_id=1, source_target_pairs={{0,1},{1,2},{2,3},{3,4},{4,5},{5,6},{6,7},{7,8},{8,9},{9,10},{10,1... | collective-permute-start | bytes 983048 | tf_op jit(solution)/shard_map/ppermute | solution.py:231
  94.0 5.2 %all-to-all-done.4 = bf16[16,24,128]{2,1,0:T(8,128)(2,1)S(1)} async-done(((bf16[16,24,128]{2,1,0:T(8,128)(2,1)}), bf16[16,24,128]{2,1,0:T(8,128)(2,1)S(1)}, u32[]{:S(2)}, u32[]{:S(2)}) %all-to-all-start.4) | async-done | bytes 98336 | tf_op jit(solution)/shard_map/all_to_all | solution.py:29
  99.2 0.1 collective-permute-done.3.after_ref
  99.3 4.9 %collective-permute-done.2.before_ref = bf16[256,640]{1,0:T(8,128)(2,1)S(1)} collective-permute-done((bf16[256,640]{1,0:T(8,128)(2,1)S(1)}, bf16[256,640]{1,0:T(8,128)(2,1)S(1)}, u32[]{:S(2)}, u32[]{:S(2)}) %collective-permute-start.2) | collective-permute-done | bytes 327712 | tf_op jit(solution)/shard_map/ppermute | solution.py:231
  104.2 0.6 broadcast_in_dim.41
  104.8 3.8 %all-to-all-start.5 = ((f32[4,6,8,128]{3,2,1,0:T(8,128)}), f32[4,6,8,128]{3,2,1,0:T(8,128)S(1)}, u32[]{:S(2)}, u32[]{:S(2)}) async-start(f32[4,6,8,128]{3,2,1,0:T(8,128)} %broadcast_in_dim.41), calls=%async_computation.5 | async-start | bytes 196608 | tf_op jit(solution)/shard_map/all_to_all | solution.py:29
  108.6 1.7 %convolve.1.local_ref = f32[256,640]{1,0:T(8,128)S(1)} custom-call(bf16[256,640]{1,0:T(8,128)(2,1)S(1)} %collective-permute-done.2.before_ref, bf16[256,640]{1,0:T(8,128)(2,1)S(1)} %get-tuple-element.15.values_ref, bf16[256,640]{1,0:T(8,128)(2,1)S(1)} %collective-permute-done.3.after_ref, bf16[27,640]{1,0:T(8,128)(2,1)S(1)} %copy-done.1), custom_call_target="tpu_custom_call" | custom-call | flops 8847360 | bytes 2097152 | tf_op jit(solution)/shard_map/convolve/pallas_call | solution.py:145
  110.4 2.6 %all-to-all-done.5 = f32[4,6,8,128]{3,2,1,0:T(8,128)S(1)} async-done(((f32[4,6,8,128]{3,2,1,0:T(8,128)}), f32[4,6,8,128]{3,2,1,0:T(8,128)S(1)}, u32[]{:S(2)}, u32[]{:S(2)}) %all-to-all-start.5) | async-done | bytes 98336 | tf_op jit(solution)/shard_map/all_to_all | solution.py:29
  113.0 1.3 %attend.1 = f32[256,640]{1,0:T(8,128)} custom-call(bf16[256,1024]{1,0:T(8,128)(2,1)S(1)} %project.2.mine_ref, bf16[256,1024]{1,0:T(8,128)(2,1)S(1)} %collective-permute-done.1.theirs_ref, f32[24,8,128]{2,1,0:T(8,128)S(1)} %bitcast.12, f32[256,640]{1,0:T(8,128)S(1)} %convolve.1.local_ref), custom_call_target="tpu_custom_call" | custom-call | flops 167772160 | bytes 3145728 | tf_op jit(solution)/shard_map/attend/pallas_call | solution.py:185
  (12 shorter events, 0.2 us)
Async XLA Ops:
  1.5 30.9 %all-to-all-start = ((bf16[16,36,128]{2,1,0:T(8,128)(2,1)}), bf16[16,36,128]{2,1,0:T(8,128)(2,1)S(1)}, u32[]{:S(2)}, u32[]{:S(2)}) async-start(bf16[16,36,128]{2,1,0:T(8,128)(2,1)} %broadcast_in_dim.17), calls=%async_computation | async-start | bytes 327680 | tf_op jit(solution)/shard_map/all_to_all | solution.py:29
  16.7 1.1 copy-start
  17.8 0.7 copy-start.2
  18.7 13.8 %collective-permute-start = (bf16[256,1152]{1,0:T(8,128)(2,1)S(1)}, bf16[256,1152]{1,0:T(8,128)(2,1)S(1)}, u32[]{:S(2)}, u32[]{:S(2)}) collective-permute-start(bf16[256,1152]{1,0:T(8,128)(2,1)S(1)} %norm.1.tokens_ref), channel_id=1, source_target_pairs={{0,64},{64,0},{1,65},{65,1},{2,66},{66,2},{3,67},{67,3},{4,68},{68... | collective-permute-start | bytes 1769480 | tf_op jit(solution)/shard_map/ppermute | solution.py:206
  67.4 41.2 %copy-start.1 = (bf16[27,640]{1,0:T(8,128)(2,1)S(1)}, bf16[27,640]{1,0:T(8,128)(2,1)}, u32[]{:S(2)}) copy-start(bf16[27,640]{1,0:T(8,128)(2,1)} %weight_ref.1) | copy-start | bytes 103684
  67.4 3.8 %collective-permute-start.1 = (bf16[256,1024]{1,0:T(8,128)(2,1)S(1)}, bf16[256,1024]{1,0:T(8,128)(2,1)S(1)}, u32[]{:S(2)}, u32[]{:S(2)}) collective-permute-start(bf16[256,1024]{1,0:T(8,128)(2,1)S(1)} %project.3), channel_id=1, source_target_pairs={{0,64},{64,0},{1,65},{65,1},{2,66},{66,2},{3,67},{67,3},{4,68},{68... | collective-permute-start | bytes 1572872 | tf_op jit(solution)/shard_map/ppermute | solution.py:206
  82.0 17.2 %all-to-all-start.4 = ((bf16[16,24,128]{2,1,0:T(8,128)(2,1)}), bf16[16,24,128]{2,1,0:T(8,128)(2,1)S(1)}, u32[]{:S(2)}, u32[]{:S(2)}) async-start(bf16[16,24,128]{2,1,0:T(8,128)(2,1)} %broadcast_in_dim.39), calls=%async_computation.4 | async-start | bytes 196608 | tf_op jit(solution)/shard_map/all_to_all | solution.py:29
  86.1 13.2 %collective-permute-start.3 = (bf16[256,640]{1,0:T(8,128)(2,1)S(1)}, bf16[256,640]{1,0:T(8,128)(2,1)S(1)}, u32[]{:S(2)}, u32[]{:S(2)}) collective-permute-start(bf16[256,640]{1,0:T(8,128)(2,1)S(1)} %get-tuple-element.15.values_ref), channel_id=1, source_target_pairs={{1,0},{2,1},{3,2},{4,3},{5,4},{6,5},{7,6},{8,7},{9,8},{10,9},{11,1... | collective-permute-start | bytes 983048 | tf_op jit(solution)/shard_map/ppermute | solution.py:232
  92.1 12.1 %collective-permute-start.2 = (bf16[256,640]{1,0:T(8,128)(2,1)S(1)}, bf16[256,640]{1,0:T(8,128)(2,1)S(1)}, u32[]{:S(2)}, u32[]{:S(2)}) collective-permute-start(bf16[256,640]{1,0:T(8,128)(2,1)S(1)} %get-tuple-element.15.values_ref), channel_id=1, source_target_pairs={{0,1},{1,2},{2,3},{3,4},{4,5},{5,6},{6,7},{7,8},{8,9},{9,10},{10,1... | collective-permute-start | bytes 983048 | tf_op jit(solution)/shard_map/ppermute | solution.py:231
  104.8 8.1 %all-to-all-start.5 = ((f32[4,6,8,128]{3,2,1,0:T(8,128)}), f32[4,6,8,128]{3,2,1,0:T(8,128)S(1)}, u32[]{:S(2)}, u32[]{:S(2)}) async-start(f32[4,6,8,128]{3,2,1,0:T(8,128)} %broadcast_in_dim.41), calls=%async_computation.5 | async-start | bytes 196608 | tf_op jit(solution)/shard_map/all_to_all | solution.py:29

commit v10 on v9

--- a/solution.py
+++ b/solution.py
@@ -236,7 +236,6 @@
     part = part.astype(jnp.bfloat16).reshape(-1, LANES)
     part = spread(part, ZAX).astype(jnp.float32)
     part = jnp.sum(part.reshape((lax.axis_size("zh"), -1) + part.shape[1:]), axis=0)
-    part, before, after = lax.optimization_barrier((part, before, after))
     local = convolve(before, values, after, conv_weight)
     tiles = spread(part.reshape((-1,) + tiles.shape[1:]), "x").reshape(tiles.shape)
     return attend(mine, theirs, tiles, local)

time: 115 us -> 112 us (0.974)
  the two profiles are of different devices: /device:TPU:2 before, /device:TPU:32 now
where the time goes in v10:
time: 112 us; the launch traced here: 111 us
  blocking collectives  44.1 us (39%)
  starting transfers between devices  33.5 us (30%)
  waiting for transfers between devices  23 us (21%)
  Pallas kernels  5.48 us (5%)
  local copies, waits for them, and re-layouts  4.1 us (4%)
    all_to_all x2, blocking collectives, spread_crossed(): lax.all_to_all(blocks, ('core', 'y', 'x'), 0, 0, tiled=True, axis_index_g...  35.1 us
    all_to_all x3, starting transfers between devices, exchange(): return lax.all_to_all(blocks, axes, 0, 0, tiled=True)  23.8 us
    all_to_all x3, waiting for transfers between devices, exchange(): return lax.all_to_all(blocks, axes, 0, 0, tiled=True)  22.1 us
    all_to_all x1, blocking collectives, exchange(): return lax.all_to_all(blocks, axes, 0, 0, tiled=True)  8.94 us
    ppermute x2, starting transfers between devices, swap(): return lax.ppermute(block, 'core', [(0, 1), (1, 0)])  3.84 us
    ppermute x1, starting transfers between devices, body(): before = lax.ppermute(values, TM, [(i, i + 1) for i in range(count - 1)])  3.82 us
  transfers between devices with their start and end apart: 7, of which 4 were waited for; matrix products, arithmetic and copies ran while one was open for 1% of the time, Pallas kernels for 3%

profile of v10, /device:TPU:32, one launch (start us, length us, event | category | flops | bytes accessed | tf_op | source)
XLA Modules:
  0.0 111.1 jit_solution(10709683210203563554)
XLA Ops:
  0.0 0.1 pad_dynamic-slice_fusion.3
  0.1 0.7 fusion.2
  0.8 0.7 broadcast_in_dim.17
  1.5 15.2 %all-to-all-start = ((bf16[16,36,128]{2,1,0:T(8,128)(2,1)}), bf16[16,36,128]{2,1,0:T(8,128)(2,1)S(1)}, u32[]{:S(2)}, u32[]{:S(2)}) async-start(bf16[16,36,128]{2,1,0:T(8,128)(2,1)} %broadcast_in_dim.17), calls=%async_computation | async-start | bytes 327680 | tf_op jit(solution)/shard_map/all_to_all | solution.py:29
  16.7 1.1 copy-done
  17.8 0.7 copy-done.2
  18.5 0.2 norm.1.tokens_ref
  18.7 1.9 %collective-permute-start = (bf16[256,1152]{1,0:T(8,128)(2,1)S(1)}, bf16[256,1152]{1,0:T(8,128)(2,1)S(1)}, u32[]{:S(2)}, u32[]{:S(2)}) collective-permute-start(bf16[256,1152]{1,0:T(8,128)(2,1)S(1)} %norm.1.tokens_ref), channel_id=1, source_target_pairs={{0,64},{64,0},{1,65},{65,1},{2,66},{66,2},{3,67},{67,3},{4,68},{68... | collective-permute-start | bytes 1769480 | tf_op jit(solution)/shard_map/ppermute | solution.py:206
  20.7 11.0 %all-to-all-done = bf16[16,36,128]{2,1,0:T(8,128)(2,1)S(1)} async-done(((bf16[16,36,128]{2,1,0:T(8,128)(2,1)}), bf16[16,36,128]{2,1,0:T(8,128)(2,1)S(1)}, u32[]{:S(2)}, u32[]{:S(2)}) %all-to-all-start) | async-done | bytes 147488 | tf_op jit(solution)/shard_map/all_to_all | solution.py:29
  31.7 0.1 reshape.28
  31.7 0.0 collective-permute-done.tokens_ref
  31.8 12.5 %all_to_all.30 = bf16[4,288,256]{2,1,0:T(8,128)(2,1)S(1)} all-to-all(bf16[4,288,256]{2,1,0:T(8,128)(2,1)S(1)} %broadcast_in_dim.36), channel_id=1, replica_groups={{0,16,32,48},{128,144,160,176},{256,272,288,304},{384,400,416,432},{64,..., dimensions={0} | all-to-all | bytes 1179648 | tf_op jit(solution)/shard_map/all_to_all | solution.py:200
  44.3 0.2 broadcast_in_dim.38
  44.5 22.6 %all_to_all.31 = bf16[4,1152,256]{2,1,0:T(8,128)(2,1)S(1)} all-to-all(bf16[4,1152,256]{2,1,0:T(8,128)(2,1)S(1)} %broadcast_in_dim.38), channel_id=1, replica_groups={{64,80,96,112},{192,208,224,240},{320,336,352,368},{448,464,480,496},{0..., dimensions={0} | all-to-all | bytes 4718592 | tf_op jit(solution)/shard_map/all_to_all | solution.py:200
  67.1 0.9 project.3
  68.0 0.0 copy-start.1
  68.0 1.9 %collective-permute-start.1 = (bf16[256,1024]{1,0:T(8,128)(2,1)S(1)}, bf16[256,1024]{1,0:T(8,128)(2,1)S(1)}, u32[]{:S(2)}, u32[]{:S(2)}) collective-permute-start(bf16[256,1024]{1,0:T(8,128)(2,1)S(1)} %project.3), channel_id=1, source_target_pairs={{0,64},{64,0},{1,65},{65,1},{2,66},{66,2},{3,67},{67,3},{4,68},{68... | collective-permute-start | bytes 1572872 | tf_op jit(solution)/shard_map/ppermute | solution.py:206
  70.0 0.9 project.2.mine_ref
  70.9 0.9 collective-permute-done.1.theirs_ref
  71.8 0.4 states.1
  72.2 8.9 %all_to_all.32 = f32[24,8,128]{2,1,0:T(8,128)S(1)} all-to-all(f32[24,8,128]{2,1,0:T(8,128)S(1)} %get-tuple-element.11), channel_id=1, replica_groups=mesh['y'=4,'core'=2,'x'=4,'zh'=8,'zl'=2] {'x','zl'}, dimensions={0} | all-to-all | bytes 196608 | tf_op jit(solution)/shard_map/all_to_all | solution.py:29
  81.2 0.7 broadcast_in_dim.39
  81.8 5.3 %all-to-all-start.4 = ((bf16[16,24,128]{2,1,0:T(8,128)(2,1)}), bf16[16,24,128]{2,1,0:T(8,128)(2,1)S(1)}, u32[]{:S(2)}, u32[]{:S(2)}) async-start(bf16[16,24,128]{2,1,0:T(8,128)(2,1)} %broadcast_in_dim.39), calls=%async_computation.4 | async-start | bytes 196608 | tf_op jit(solution)/shard_map/all_to_all | solution.py:29
  87.1 2.0 %collective-permute-start.3 = (bf16[256,640]{1,0:T(8,128)(2,1)S(1)}, bf16[256,640]{1,0:T(8,128)(2,1)S(1)}, u32[]{:S(2)}, u32[]{:S(2)}) collective-permute-start(bf16[256,640]{1,0:T(8,128)(2,1)S(1)} %get-tuple-element.12.values_ref), channel_id=1, source_target_pairs={{1,0},{2,1},{3,2},{4,3},{5,4},{6,5},{7,6},{8,7},{9,8},{10,9},{11,1... | collective-permute-start | bytes 983048 | tf_op jit(solution)/shard_map/ppermute | solution.py:232
  89.1 3.8 %collective-permute-start.2 = (bf16[256,640]{1,0:T(8,128)(2,1)S(1)}, bf16[256,640]{1,0:T(8,128)(2,1)S(1)}, u32[]{:S(2)}, u32[]{:S(2)}) collective-permute-start(bf16[256,640]{1,0:T(8,128)(2,1)S(1)} %get-tuple-element.12.values_ref), channel_id=1, source_target_pairs={{0,1},{1,2},{2,3},{3,4},{4,5},{5,6},{6,7},{7,8},{8,9},{9,10},{10,1... | collective-permute-start | bytes 983048 | tf_op jit(solution)/shard_map/ppermute | solution.py:231
  92.9 7.1 %all-to-all-done.4 = bf16[16,24,128]{2,1,0:T(8,128)(2,1)S(1)} async-done(((bf16[16,24,128]{2,1,0:T(8,128)(2,1)}), bf16[16,24,128]{2,1,0:T(8,128)(2,1)S(1)}, u32[]{:S(2)}, u32[]{:S(2)}) %all-to-all-start.4) | async-done | bytes 98336 | tf_op jit(solution)/shard_map/all_to_all | solution.py:29
  100.1 0.6 broadcast_in_dim.41
  100.7 3.3 %all-to-all-start.5 = ((f32[4,6,8,128]{3,2,1,0:T(8,128)}), f32[4,6,8,128]{3,2,1,0:T(8,128)S(1)}, u32[]{:S(2)}, u32[]{:S(2)}) async-start(f32[4,6,8,128]{3,2,1,0:T(8,128)} %broadcast_in_dim.41), calls=%async_computation.5 | async-start | bytes 196608 | tf_op jit(solution)/shard_map/all_to_all | solution.py:29
  104.0 0.0 collective-permute-done.3.after_ref
  104.0 1.7 %convolve.1.local_ref = f32[256,640]{1,0:T(8,128)S(1)} custom-call(bf16[256,640]{1,0:T(8,128)(2,1)S(1)} %collective-permute-done.2.before_ref, bf16[256,640]{1,0:T(8,128)(2,1)S(1)} %get-tuple-element.12.values_ref, bf16[256,640]{1,0:T(8,128)(2,1)S(1)} %collective-permute-done.3.after_ref, bf16[27,640]{1,0:T(8,128)(2,1)S(1)} %copy-done.1), custom_call_target="tpu_custom_call" | custom-call | flops 8847360 | bytes 2097152 | tf_op jit(solution)/shard_map/convolve/pallas_call | solution.py:145
  105.8 4.0 %all-to-all-done.5 = f32[4,6,8,128]{3,2,1,0:T(8,128)S(1)} async-done(((f32[4,6,8,128]{3,2,1,0:T(8,128)}), f32[4,6,8,128]{3,2,1,0:T(8,128)S(1)}, u32[]{:S(2)}, u32[]{:S(2)}) %all-to-all-start.5) | async-done | bytes 98336 | tf_op jit(solution)/shard_map/all_to_all | solution.py:29
  109.8 1.3 %attend.1 = f32[256,640]{1,0:T(8,128)} custom-call(bf16[256,1024]{1,0:T(8,128)(2,1)S(1)} %project.2.mine_ref, bf16[256,1024]{1,0:T(8,128)(2,1)S(1)} %collective-permute-done.1.theirs_ref, f32[24,8,128]{2,1,0:T(8,128)S(1)} %bitcast.12, f32[256,640]{1,0:T(8,128)S(1)} %convolve.1.local_ref), custom_call_target="tpu_custom_call" | custom-call | flops 167772160 | bytes 3145728 | tf_op jit(solution)/shard_map/attend/pallas_call | solution.py:185
  (12 shorter events, 0.2 us)
Async XLA Ops:
  1.5 30.1 %all-to-all-start = ((bf16[16,36,128]{2,1,0:T(8,128)(2,1)}), bf16[16,36,128]{2,1,0:T(8,128)(2,1)S(1)}, u32[]{:S(2)}, u32[]{:S(2)}) async-start(bf16[16,36,128]{2,1,0:T(8,128)(2,1)} %broadcast_in_dim.17), calls=%async_computation | async-start | bytes 327680 | tf_op jit(solution)/shard_map/all_to_all | solution.py:29
  16.7 1.1 copy-start
  17.8 0.7 copy-start.2
  18.7 13.0 %collective-permute-start = (bf16[256,1152]{1,0:T(8,128)(2,1)S(1)}, bf16[256,1152]{1,0:T(8,128)(2,1)S(1)}, u32[]{:S(2)}, u32[]{:S(2)}) collective-permute-start(bf16[256,1152]{1,0:T(8,128)(2,1)S(1)} %norm.1.tokens_ref), channel_id=1, source_target_pairs={{0,64},{64,0},{1,65},{65,1},{2,66},{66,2},{3,67},{67,3},{4,68},{68... | collective-permute-start | bytes 1769480 | tf_op jit(solution)/shard_map/ppermute | solution.py:206
  68.0 36.0 %copy-start.1 = (bf16[27,640]{1,0:T(8,128)(2,1)S(1)}, bf16[27,640]{1,0:T(8,128)(2,1)}, u32[]{:S(2)}) copy-start(bf16[27,640]{1,0:T(8,128)(2,1)} %weight_ref.1) | copy-start | bytes 103684
  68.0 3.8 %collective-permute-start.1 = (bf16[256,1024]{1,0:T(8,128)(2,1)S(1)}, bf16[256,1024]{1,0:T(8,128)(2,1)S(1)}, u32[]{:S(2)}, u32[]{:S(2)}) collective-permute-start(bf16[256,1024]{1,0:T(8,128)(2,1)S(1)} %project.3), channel_id=1, source_target_pairs={{0,64},{64,0},{1,65},{65,1},{2,66},{66,2},{3,67},{67,3},{4,68},{68... | collective-permute-start | bytes 1572872 | tf_op jit(solution)/shard_map/ppermute | solution.py:206
  81.8 18.2 %all-to-all-start.4 = ((bf16[16,24,128]{2,1,0:T(8,128)(2,1)}), bf16[16,24,128]{2,1,0:T(8,128)(2,1)S(1)}, u32[]{:S(2)}, u32[]{:S(2)}) async-start(bf16[16,24,128]{2,1,0:T(8,128)(2,1)} %broadcast_in_dim.39), calls=%async_computation.4 | async-start | bytes 196608 | tf_op jit(solution)/shard_map/all_to_all | solution.py:29
  87.1 16.9 %collective-permute-start.3 = (bf16[256,640]{1,0:T(8,128)(2,1)S(1)}, bf16[256,640]{1,0:T(8,128)(2,1)S(1)}, u32[]{:S(2)}, u32[]{:S(2)}) collective-permute-start(bf16[256,640]{1,0:T(8,128)(2,1)S(1)} %get-tuple-element.12.values_ref), channel_id=1, source_target_pairs={{1,0},{2,1},{3,2},{4,3},{5,4},{6,5},{7,6},{8,7},{9,8},{10,9},{11,1... | collective-permute-start | bytes 983048 | tf_op jit(solution)/shard_map/ppermute | solution.py:232
  89.1 14.9 %collective-permute-start.2 = (bf16[256,640]{1,0:T(8,128)(2,1)S(1)}, bf16[256,640]{1,0:T(8,128)(2,1)S(1)}, u32[]{:S(2)}, u32[]{:S(2)}) collective-permute-start(bf16[256,640]{1,0:T(8,128)(2,1)S(1)} %get-tuple-element.12.values_ref), channel_id=1, source_target_pairs={{0,1},{1,2},{2,3},{3,4},{4,5},{5,6},{6,7},{7,8},{8,9},{9,10},{10,1... | collective-permute-start | bytes 983048 | tf_op jit(solution)/shard_map/ppermute | solution.py:231
  100.7 9.1 %all-to-all-start.5 = ((f32[4,6,8,128]{3,2,1,0:T(8,128)}), f32[4,6,8,128]{3,2,1,0:T(8,128)S(1)}, u32[]{:S(2)}, u32[]{:S(2)}) async-start(f32[4,6,8,128]{3,2,1,0:T(8,128)} %broadcast_in_dim.41), calls=%async_computation.5 | async-start | bytes 196608 | tf_op jit(solution)/shard_map/all_to_all | solution.py:29

commit v11 on v10

--- a/solution.py
+++ b/solution.py
@@ -18,7 +18,7 @@
 ZAX = ("zh", "zl")
 TM = ("x", "zh", "zl")
 NEAR = ("x", "zl")
-PARAMS = pltpu.CompilerParams(vmem_limit_bytes=16 * 1024 * 1024)
+PARAMS = pltpu.CompilerParams(vmem_limit_bytes=12 * 1024 * 1024)
 
 
 def cost(flops, nbytes):
@@ -113,6 +113,23 @@
         compiler_params=PARAMS,
         cost_estimate=cost(2 * rows * GROUPS * LANES * LANES, 2 * 1024 * 1024),
         name="states",
+    )(mine, theirs)
+
+
+def query_kernel(mine_ref, theirs_ref, out_ref):
+    for g in range(GROUPS):
+        core, unit = (0, GROUPS + g) if g < 3 else (1, g - 3)
+        out_ref[:, g * LANES : (g + 1) * LANES] = unit_of(core, mine_ref, theirs_ref, unit)
+
+
+def queries(mine, theirs):
+    rows = mine.shape[0]
+    return pl.pallas_call(
+        query_kernel,
+        out_shape=jax.ShapeDtypeStruct((rows, GROUPS * LANES), jnp.bfloat16),
+        compiler_params=PARAMS,
+        cost_estimate=cost(rows * GROUPS * LANES, 2 * 1024 * 1024),
+        name="queries",
     )(mine, theirs)
 
 
@@ -164,13 +181,12 @@
     )
 
 
-def attend_kernel(mine_ref, theirs_ref, tiles_ref, local_ref, out_ref):
+def attend_kernel(query_ref, tiles_ref, local_ref, out_ref):
     row = lax.broadcasted_iota(jnp.int32, (LANES, LANES), 0) // HEAD_WIDTH
     lane = lax.broadcasted_iota(jnp.int32, (LANES, LANES), 1) // HEAD_WIDTH
     same = row == lane
     for g in range(GROUPS):
-        core, unit = (0, GROUPS + g) if g < 3 else (1, g - 3)
-        qfeat = unit_of(core, mine_ref, theirs_ref, unit)
+        qfeat = query_ref[:, g * LANES : (g + 1) * LANES]
         packed = tiles_ref[4 * g : 4 * g + 4].reshape(HEAD_WIDTH, LANES)
         state = jnp.where(same, jnp.concatenate([packed] * 4, axis=0), 0.0)
         ksum = jnp.broadcast_to(tiles_ref[4 * GROUPS, g : g + 1, :], (LANES, LANES)).T
@@ -180,7 +196,7 @@
         out_ref[:, cols] = both[:, :LANES] / both[:, LANES:] + local_ref[:, cols]
 
 
-def attend(mine, theirs, tiles, local):
+def attend(query, tiles, local):
     rows, width = local.shape
     return pl.pallas_call(
         attend_kernel,
@@ -188,7 +204,7 @@
         compiler_params=PARAMS,
         cost_estimate=cost(8 * rows * width * LANES, 3 * 1024 * 1024),
         name="attend",
-    )(mine, theirs, tiles, local)
+    )(query, tiles, local)
 
 
 def spread_crossed(block, turn):
@@ -238,7 +254,7 @@
     part = jnp.sum(part.reshape((lax.axis_size("zh"), -1) + part.shape[1:]), axis=0)
     local = convolve(before, values, after, conv_weight)
     tiles = spread(part.reshape((-1,) + tiles.shape[1:]), "x").reshape(tiles.shape)
-    return attend(mine, theirs, tiles, local)
+    return attend(queries(mine, theirs), tiles, local)
 
 
 def solution(mesh):

time: 112 us -> 112 us (level)
  no operation moved by 1% of the time
where the time goes in v11:
time: 112 us; the launch traced here: 111 us
  blocking collectives  44.1 us (39%)
  starting transfers between devices  33.5 us (30%)
  waiting for transfers between devices  22.9 us (20%)
  Pallas kernels  5.57 us (5%)
  local copies, waits for them, and re-layouts  4.1 us (4%)
    all_to_all x2, blocking collectives, spread_crossed(): lax.all_to_all(blocks, ('core', 'y', 'x'), 0, 0, tiled=True, axis_index_g...  35.1 us
    all_to_all x3, starting transfers between devices, exchange(): return lax.all_to_all(blocks, axes, 0, 0, tiled=True)  23.8 us
    all_to_all x3, waiting for transfers between devices, exchange(): return lax.all_to_all(blocks, axes, 0, 0, tiled=True)  21.9 us
    all_to_all x1, blocking collectives, exchange(): return lax.all_to_all(blocks, axes, 0, 0, tiled=True)  8.94 us
    ppermute x2, starting transfers between devices, swap(): return lax.ppermute(block, 'core', [(0, 1), (1, 0)])  3.84 us
    ppermute x1, starting transfers between devices, body(): before = lax.ppermute(values, TM, [(i, i + 1) for i in range(count - 1)])  3.82 us
  transfers between devices with their start and end apart: 7, of which 4 were waited for; matrix products, arithmetic and copies ran while one was open for 1% of the time, Pallas kernels for 3%

profile of v11, /device:TPU:32, one launch (start us, length us, event | category | flops | bytes accessed | tf_op | source)
XLA Modules:
  0.0 111.0 jit_solution(5147999699594495402)
XLA Ops:
  0.0 0.1 pad_dynamic-slice_fusion.3
  0.1 0.7 fusion.2
  0.8 0.7 broadcast_in_dim.17
  1.5 15.2 %all-to-all-start = ((bf16[16,36,128]{2,1,0:T(8,128)(2,1)}), bf16[16,36,128]{2,1,0:T(8,128)(2,1)S(1)}, u32[]{:S(2)}, u32[]{:S(2)}) async-start(bf16[16,36,128]{2,1,0:T(8,128)(2,1)} %broadcast_in_dim.17), calls=%async_computation | async-start | bytes 327680 | tf_op jit(solution)/shard_map/all_to_all | solution.py:29
  16.7 1.1 copy-done
  17.8 0.7 copy-done.2
  18.5 0.2 norm.1.tokens_ref
  18.7 1.9 %collective-permute-start = (bf16[256,1152]{1,0:T(8,128)(2,1)S(1)}, bf16[256,1152]{1,0:T(8,128)(2,1)S(1)}, u32[]{:S(2)}, u32[]{:S(2)}) collective-permute-start(bf16[256,1152]{1,0:T(8,128)(2,1)S(1)} %norm.1.tokens_ref), channel_id=1, source_target_pairs={{0,64},{64,0},{1,65},{65,1},{2,66},{66,2},{3,67},{67,3},{4,68},{68... | collective-permute-start | bytes 1769480 | tf_op jit(solution)/shard_map/ppermute | solution.py:222
  20.7 11.0 %all-to-all-done = bf16[16,36,128]{2,1,0:T(8,128)(2,1)S(1)} async-done(((bf16[16,36,128]{2,1,0:T(8,128)(2,1)}), bf16[16,36,128]{2,1,0:T(8,128)(2,1)S(1)}, u32[]{:S(2)}, u32[]{:S(2)}) %all-to-all-start) | async-done | bytes 147488 | tf_op jit(solution)/shard_map/all_to_all | solution.py:29
  31.7 0.1 reshape.28
  31.7 0.0 collective-permute-done.tokens_ref
  31.8 12.5 %all_to_all.30 = bf16[4,288,256]{2,1,0:T(8,128)(2,1)S(1)} all-to-all(bf16[4,288,256]{2,1,0:T(8,128)(2,1)S(1)} %broadcast_in_dim.36), channel_id=1, replica_groups={{0,16,32,48},{128,144,160,176},{256,272,288,304},{384,400,416,432},{64,..., dimensions={0} | all-to-all | bytes 1179648 | tf_op jit(solution)/shard_map/all_to_all | solution.py:216
  44.3 0.2 broadcast_in_dim.38
  44.5 22.6 %all_to_all.31 = bf16[4,1152,256]{2,1,0:T(8,128)(2,1)S(1)} all-to-all(bf16[4,1152,256]{2,1,0:T(8,128)(2,1)S(1)} %broadcast_in_dim.38), channel_id=1, replica_groups={{64,80,96,112},{192,208,224,240},{320,336,352,368},{448,464,480,496},{0..., dimensions={0} | all-to-all | bytes 4718592 | tf_op jit(solution)/shard_map/all_to_all | solution.py:216
  67.1 0.9 project.3
  68.0 1.9 %collective-permute-start.1 = (bf16[256,1024]{1,0:T(8,128)(2,1)S(1)}, bf16[256,1024]{1,0:T(8,128)(2,1)S(1)}, u32[]{:S(2)}, u32[]{:S(2)}) collective-permute-start(bf16[256,1024]{1,0:T(8,128)(2,1)S(1)} %project.3), channel_id=1, source_target_pairs={{0,64},{64,0},{1,65},{65,1},{2,66},{66,2},{3,67},{67,3},{4,68},{68... | collective-permute-start | bytes 1572872 | tf_op jit(solution)/shard_map/ppermute | solution.py:222
  69.9 0.9 project.2.mine_ref
  70.9 0.0 copy-start.1
  70.9 0.9 collective-permute-done.1.theirs_ref
  71.8 0.4 states.1
  72.2 8.9 %all_to_all.32 = f32[24,8,128]{2,1,0:T(8,128)S(1)} all-to-all(f32[24,8,128]{2,1,0:T(8,128)S(1)} %get-tuple-element.11), channel_id=1, replica_groups=mesh['y'=4,'core'=2,'x'=4,'zh'=8,'zl'=2] {'x','zl'}, dimensions={0} | all-to-all | bytes 196608 | tf_op jit(solution)/shard_map/all_to_all | solution.py:29
  81.2 0.7 broadcast_in_dim.39
  81.8 5.3 %all-to-all-start.4 = ((bf16[16,24,128]{2,1,0:T(8,128)(2,1)}), bf16[16,24,128]{2,1,0:T(8,128)(2,1)S(1)}, u32[]{:S(2)}, u32[]{:S(2)}) async-start(bf16[16,24,128]{2,1,0:T(8,128)(2,1)} %broadcast_in_dim.39), calls=%async_computation.4 | async-start | bytes 196608 | tf_op jit(solution)/shard_map/all_to_all | solution.py:29
  87.1 2.0 %collective-permute-start.3 = (bf16[256,640]{1,0:T(8,128)(2,1)S(1)}, bf16[256,640]{1,0:T(8,128)(2,1)S(1)}, u32[]{:S(2)}, u32[]{:S(2)}) collective-permute-start(bf16[256,640]{1,0:T(8,128)(2,1)S(1)} %get-tuple-element.12.values_ref), channel_id=1, source_target_pairs={{1,0},{2,1},{3,2},{4,3},{5,4},{6,5},{7,6},{8,7},{9,8},{10,9},{11,1... | collective-permute-start | bytes 983048 | tf_op jit(solution)/shard_map/ppermute | solution.py:248
  89.1 3.8 %collective-permute-start.2 = (bf16[256,640]{1,0:T(8,128)(2,1)S(1)}, bf16[256,640]{1,0:T(8,128)(2,1)S(1)}, u32[]{:S(2)}, u32[]{:S(2)}) collective-permute-start(bf16[256,640]{1,0:T(8,128)(2,1)S(1)} %get-tuple-element.12.values_ref), channel_id=1, source_target_pairs={{0,1},{1,2},{2,3},{3,4},{4,5},{5,6},{6,7},{7,8},{8,9},{9,10},{10,1... | collective-permute-start | bytes 983048 | tf_op jit(solution)/shard_map/ppermute | solution.py:247
  92.9 7.1 %all-to-all-done.4 = bf16[16,24,128]{2,1,0:T(8,128)(2,1)S(1)} async-done(((bf16[16,24,128]{2,1,0:T(8,128)(2,1)}), bf16[16,24,128]{2,1,0:T(8,128)(2,1)S(1)}, u32[]{:S(2)}, u32[]{:S(2)}) %all-to-all-start.4) | async-done | bytes 98336 | tf_op jit(solution)/shard_map/all_to_all | solution.py:29
  100.0 0.6 broadcast_in_dim.41
  100.7 3.3 %all-to-all-start.5 = ((f32[4,6,8,128]{3,2,1,0:T(8,128)}), f32[4,6,8,128]{3,2,1,0:T(8,128)S(1)}, u32[]{:S(2)}, u32[]{:S(2)}) async-start(f32[4,6,8,128]{3,2,1,0:T(8,128)} %broadcast_in_dim.41), calls=%async_computation.5 | async-start | bytes 196608 | tf_op jit(solution)/shard_map/all_to_all | solution.py:29
  104.0 0.1 queries.1.query_ref
  104.2 1.7 %convolve.1.local_ref = f32[256,640]{1,0:T(8,128)S(1)} custom-call(bf16[256,640]{1,0:T(8,128)(2,1)S(1)} %collective-permute-done.2.before_ref, bf16[256,640]{1,0:T(8,128)(2,1)S(1)} %get-tuple-element.12.values_ref, bf16[256,640]{1,0:T(8,128)(2,1)S(1)} %collective-permute-done.3.after_ref, bf16[27,640]{1,0:T(8,128)(2,1)S(1)} %copy-done.1), custom_call_target="tpu_custom_call" | custom-call | flops 8847360 | bytes 2097152 | tf_op jit(solution)/shard_map/convolve/pallas_call | solution.py:162
  105.9 3.9 %all-to-all-done.5 = f32[4,6,8,128]{3,2,1,0:T(8,128)S(1)} async-done(((f32[4,6,8,128]{3,2,1,0:T(8,128)}), f32[4,6,8,128]{3,2,1,0:T(8,128)S(1)}, u32[]{:S(2)}, u32[]{:S(2)}) %all-to-all-start.5) | async-done | bytes 98336 | tf_op jit(solution)/shard_map/all_to_all | solution.py:29
  109.8 1.3 %attend.1 = f32[256,640]{1,0:T(8,128)} custom-call(bf16[256,640]{1,0:T(8,128)(2,1)S(1)} %queries.1.query_ref, f32[24,8,128]{2,1,0:T(8,128)S(1)} %bitcast.12, f32[256,640]{1,0:T(8,128)S(1)} %convolve.1.local_ref), custom_call_target="tpu_custom_call" | custom-call | flops 167772160 | bytes 3145728 | tf_op jit(solution)/shard_map/attend/pallas_call | solution.py:201
  (13 shorter events, 0.2 us)
Async XLA Ops:
  1.5 30.1 %all-to-all-start = ((bf16[16,36,128]{2,1,0:T(8,128)(2,1)}), bf16[16,36,128]{2,1,0:T(8,128)(2,1)S(1)}, u32[]{:S(2)}, u32[]{:S(2)}) async-start(bf16[16,36,128]{2,1,0:T(8,128)(2,1)} %broadcast_in_dim.17), calls=%async_computation | async-start | bytes 327680 | tf_op jit(solution)/shard_map/all_to_all | solution.py:29
  16.7 1.1 copy-start
  17.8 0.7 copy-start.2
  18.7 13.0 %collective-permute-start = (bf16[256,1152]{1,0:T(8,128)(2,1)S(1)}, bf16[256,1152]{1,0:T(8,128)(2,1)S(1)}, u32[]{:S(2)}, u32[]{:S(2)}) collective-permute-start(bf16[256,1152]{1,0:T(8,128)(2,1)S(1)} %norm.1.tokens_ref), channel_id=1, source_target_pairs={{0,64},{64,0},{1,65},{65,1},{2,66},{66,2},{3,67},{67,3},{4,68},{68... | collective-permute-start | bytes 1769480 | tf_op jit(solution)/shard_map/ppermute | solution.py:222
  68.0 3.8 %collective-permute-start.1 = (bf16[256,1024]{1,0:T(8,128)(2,1)S(1)}, bf16[256,1024]{1,0:T(8,128)(2,1)S(1)}, u32[]{:S(2)}, u32[]{:S(2)}) collective-permute-start(bf16[256,1024]{1,0:T(8,128)(2,1)S(1)} %project.3), channel_id=1, source_target_pairs={{0,64},{64,0},{1,65},{65,1},{2,66},{66,2},{3,67},{67,3},{4,68},{68... | collective-permute-start | bytes 1572872 | tf_op jit(solution)/shard_map/ppermute | solution.py:222
  70.9 33.3 %copy-start.1 = (bf16[27,640]{1,0:T(8,128)(2,1)S(1)}, bf16[27,640]{1,0:T(8,128)(2,1)}, u32[]{:S(2)}) copy-start(bf16[27,640]{1,0:T(8,128)(2,1)} %weight_ref.1) | copy-start | bytes 103684
  81.8 18.2 %all-to-all-start.4 = ((bf16[16,24,128]{2,1,0:T(8,128)(2,1)}), bf16[16,24,128]{2,1,0:T(8,128)(2,1)S(1)}, u32[]{:S(2)}, u32[]{:S(2)}) async-start(bf16[16,24,128]{2,1,0:T(8,128)(2,1)} %broadcast_in_dim.39), calls=%async_computation.4 | async-start | bytes 196608 | tf_op jit(solution)/shard_map/all_to_all | solution.py:29
  87.1 17.0 %collective-permute-start.3 = (bf16[256,640]{1,0:T(8,128)(2,1)S(1)}, bf16[256,640]{1,0:T(8,128)(2,1)S(1)}, u32[]{:S(2)}, u32[]{:S(2)}) collective-permute-start(bf16[256,640]{1,0:T(8,128)(2,1)S(1)} %get-tuple-element.12.values_ref), channel_id=1, source_target_pairs={{1,0},{2,1},{3,2},{4,3},{5,4},{6,5},{7,6},{8,7},{9,8},{10,9},{11,1... | collective-permute-start | bytes 983048 | tf_op jit(solution)/shard_map/ppermute | solution.py:248
  89.1 15.0 %collective-permute-start.2 = (bf16[256,640]{1,0:T(8,128)(2,1)S(1)}, bf16[256,640]{1,0:T(8,128)(2,1)S(1)}, u32[]{:S(2)}, u32[]{:S(2)}) collective-permute-start(bf16[256,640]{1,0:T(8,128)(2,1)S(1)} %get-tuple-element.12.values_ref), channel_id=1, source_target_pairs={{0,1},{1,2},{2,3},{3,4},{4,5},{5,6},{6,7},{7,8},{8,9},{9,10},{10,1... | collective-permute-start | bytes 983048 | tf_op jit(solution)/shard_map/ppermute | solution.py:247
  100.7 9.1 %all-to-all-start.5 = ((f32[4,6,8,128]{3,2,1,0:T(8,128)}), f32[4,6,8,128]{3,2,1,0:T(8,128)S(1)}, u32[]{:S(2)}, u32[]{:S(2)}) async-start(f32[4,6,8,128]{3,2,1,0:T(8,128)} %broadcast_in_dim.41), calls=%async_computation.5 | async-start | bytes 196608 | tf_op jit(solution)/shard_map/all_to_all | solution.py:29

commit v12 on v11

--- a/solution.py
+++ b/solution.py
@@ -59,7 +59,7 @@
         for half in range(2):
             unit = 2 * step + half
             proj = both[:, half * LANES : (half + 1) * LANES]
-            feat = jnp.where(proj > 0, proj, jnp.exp(jnp.minimum(proj, 0.0)) - 1.0) + 1.0
+            feat = jnp.where(proj > 0, proj + 1.0, jnp.exp(jnp.minimum(proj, 0.0)))
             if unit < GROUPS:
                 feat = jnp.where(first, proj, feat)
             out_ref[:, unit * LANES : (unit + 1) * LANES] = feat.astype(jnp.bfloat16)

time: 112 us -> 112 us (level)
  no operation moved by 1% of the time
where the time goes in v12:
time: 112 us; the launch traced here: 111 us
  blocking collectives  44.1 us (39%)
  starting transfers between devices  33.5 us (30%)
  waiting for transfers between devices  22.9 us (20%)
  Pallas kernels  5.52 us (5%)
  local copies, waits for them, and re-layouts  4.1 us (4%)
    all_to_all x2, blocking collectives, spread_crossed(): lax.all_to_all(blocks, ('core', 'y', 'x'), 0, 0, tiled=True, axis_index_g...  35.1 us
    all_to_all x3, starting transfers between devices, exchange(): return lax.all_to_all(blocks, axes, 0, 0, tiled=True)  23.8 us
    all_to_all x3, waiting for transfers between devices, exchange(): return lax.all_to_all(blocks, axes, 0, 0, tiled=True)  21.9 us
    all_to_all x1, blocking collectives, exchange(): return lax.all_to_all(blocks, axes, 0, 0, tiled=True)  8.94 us
    ppermute x2, starting transfers between devices, swap(): return lax.ppermute(block, 'core', [(0, 1), (1, 0)])  3.84 us
    ppermute x1, starting transfers between devices, body(): before = lax.ppermute(values, TM, [(i, i + 1) for i in range(count - 1)])  3.82 us
  transfers between devices with their start and end apart: 7, of which 4 were waited for; matrix products, arithmetic and copies ran while one was open for 1% of the time, Pallas kernels for 3%

profile of v12, /device:TPU:32, one launch (start us, length us, event | category | flops | bytes accessed | tf_op | source)
XLA Modules:
  0.0 111.0 jit_solution(17019450052538499466)
XLA Ops:
  0.0 0.1 pad_dynamic-slice_fusion.3
  0.1 0.7 fusion.2
  0.8 0.7 broadcast_in_dim.17
  1.5 15.2 %all-to-all-start = ((bf16[16,36,128]{2,1,0:T(8,128)(2,1)}), bf16[16,36,128]{2,1,0:T(8,128)(2,1)S(1)}, u32[]{:S(2)}, u32[]{:S(2)}) async-start(bf16[16,36,128]{2,1,0:T(8,128)(2,1)} %broadcast_in_dim.17), calls=%async_computation | async-start | bytes 327680 | tf_op jit(solution)/shard_map/all_to_all | solution.py:29
  16.7 1.1 copy-done
  17.8 0.7 copy-done.2
  18.5 0.2 norm.1.tokens_ref
  18.7 1.9 %collective-permute-start = (bf16[256,1152]{1,0:T(8,128)(2,1)S(1)}, bf16[256,1152]{1,0:T(8,128)(2,1)S(1)}, u32[]{:S(2)}, u32[]{:S(2)}) collective-permute-start(bf16[256,1152]{1,0:T(8,128)(2,1)S(1)} %norm.1.tokens_ref), channel_id=1, source_target_pairs={{0,64},{64,0},{1,65},{65,1},{2,66},{66,2},{3,67},{67,3},{4,68},{68... | collective-permute-start | bytes 1769480 | tf_op jit(solution)/shard_map/ppermute | solution.py:222
  20.7 11.0 %all-to-all-done = bf16[16,36,128]{2,1,0:T(8,128)(2,1)S(1)} async-done(((bf16[16,36,128]{2,1,0:T(8,128)(2,1)}), bf16[16,36,128]{2,1,0:T(8,128)(2,1)S(1)}, u32[]{:S(2)}, u32[]{:S(2)}) %all-to-all-start) | async-done | bytes 147488 | tf_op jit(solution)/shard_map/all_to_all | solution.py:29
  31.7 0.1 reshape.28
  31.7 0.0 collective-permute-done.tokens_ref
  31.8 12.5 %all_to_all.30 = bf16[4,288,256]{2,1,0:T(8,128)(2,1)S(1)} all-to-all(bf16[4,288,256]{2,1,0:T(8,128)(2,1)S(1)} %broadcast_in_dim.36), channel_id=1, replica_groups={{0,16,32,48},{128,144,160,176},{256,272,288,304},{384,400,416,432},{64,..., dimensions={0} | all-to-all | bytes 1179648 | tf_op jit(solution)/shard_map/all_to_all | solution.py:216
  44.3 0.2 broadcast_in_dim.38
  44.5 22.6 %all_to_all.31 = bf16[4,1152,256]{2,1,0:T(8,128)(2,1)S(1)} all-to-all(bf16[4,1152,256]{2,1,0:T(8,128)(2,1)S(1)} %broadcast_in_dim.38), channel_id=1, replica_groups={{64,80,96,112},{192,208,224,240},{320,336,352,368},{448,464,480,496},{0..., dimensions={0} | all-to-all | bytes 4718592 | tf_op jit(solution)/shard_map/all_to_all | solution.py:216
  67.1 0.9 project.3
  68.0 1.9 %collective-permute-start.1 = (bf16[256,1024]{1,0:T(8,128)(2,1)S(1)}, bf16[256,1024]{1,0:T(8,128)(2,1)S(1)}, u32[]{:S(2)}, u32[]{:S(2)}) collective-permute-start(bf16[256,1024]{1,0:T(8,128)(2,1)S(1)} %project.3), channel_id=1, source_target_pairs={{0,64},{64,0},{1,65},{65,1},{2,66},{66,2},{3,67},{67,3},{4,68},{68... | collective-permute-start | bytes 1572872 | tf_op jit(solution)/shard_map/ppermute | solution.py:222
  69.9 0.9 project.2.mine_ref
  70.8 0.0 copy-start.1
  70.8 0.9 collective-permute-done.1.theirs_ref
  71.8 0.4 states.1
  72.2 8.9 %all_to_all.32 = f32[24,8,128]{2,1,0:T(8,128)S(1)} all-to-all(f32[24,8,128]{2,1,0:T(8,128)S(1)} %get-tuple-element.11), channel_id=1, replica_groups=mesh['y'=4,'core'=2,'x'=4,'zh'=8,'zl'=2] {'x','zl'}, dimensions={0} | all-to-all | bytes 196608 | tf_op jit(solution)/shard_map/all_to_all | solution.py:29
  81.1 0.7 broadcast_in_dim.39
  81.8 5.3 %all-to-all-start.4 = ((bf16[16,24,128]{2,1,0:T(8,128)(2,1)}), bf16[16,24,128]{2,1,0:T(8,128)(2,1)S(1)}, u32[]{:S(2)}, u32[]{:S(2)}) async-start(bf16[16,24,128]{2,1,0:T(8,128)(2,1)} %broadcast_in_dim.39), calls=%async_computation.4 | async-start | bytes 196608 | tf_op jit(solution)/shard_map/all_to_all | solution.py:29
  87.1 2.0 %collective-permute-start.3 = (bf16[256,640]{1,0:T(8,128)(2,1)S(1)}, bf16[256,640]{1,0:T(8,128)(2,1)S(1)}, u32[]{:S(2)}, u32[]{:S(2)}) collective-permute-start(bf16[256,640]{1,0:T(8,128)(2,1)S(1)} %get-tuple-element.12.values_ref), channel_id=1, source_target_pairs={{1,0},{2,1},{3,2},{4,3},{5,4},{6,5},{7,6},{8,7},{9,8},{10,9},{11,1... | collective-permute-start | bytes 983048 | tf_op jit(solution)/shard_map/ppermute | solution.py:248
  89.1 3.8 %collective-permute-start.2 = (bf16[256,640]{1,0:T(8,128)(2,1)S(1)}, bf16[256,640]{1,0:T(8,128)(2,1)S(1)}, u32[]{:S(2)}, u32[]{:S(2)}) collective-permute-start(bf16[256,640]{1,0:T(8,128)(2,1)S(1)} %get-tuple-element.12.values_ref), channel_id=1, source_target_pairs={{0,1},{1,2},{2,3},{3,4},{4,5},{5,6},{6,7},{7,8},{8,9},{9,10},{10,1... | collective-permute-start | bytes 983048 | tf_op jit(solution)/shard_map/ppermute | solution.py:247
  92.9 7.1 %all-to-all-done.4 = bf16[16,24,128]{2,1,0:T(8,128)(2,1)S(1)} async-done(((bf16[16,24,128]{2,1,0:T(8,128)(2,1)}), bf16[16,24,128]{2,1,0:T(8,128)(2,1)S(1)}, u32[]{:S(2)}, u32[]{:S(2)}) %all-to-all-start.4) | async-done | bytes 98336 | tf_op jit(solution)/shard_map/all_to_all | solution.py:29
  100.0 0.6 broadcast_in_dim.41
  100.7 3.3 %all-to-all-start.5 = ((f32[4,6,8,128]{3,2,1,0:T(8,128)}), f32[4,6,8,128]{3,2,1,0:T(8,128)S(1)}, u32[]{:S(2)}, u32[]{:S(2)}) async-start(f32[4,6,8,128]{3,2,1,0:T(8,128)} %broadcast_in_dim.41), calls=%async_computation.5 | async-start | bytes 196608 | tf_op jit(solution)/shard_map/all_to_all | solution.py:29
  104.0 0.1 queries.1.query_ref
  104.1 1.7 %convolve.1.local_ref = f32[256,640]{1,0:T(8,128)S(1)} custom-call(bf16[256,640]{1,0:T(8,128)(2,1)S(1)} %collective-permute-done.2.before_ref, bf16[256,640]{1,0:T(8,128)(2,1)S(1)} %get-tuple-element.12.values_ref, bf16[256,640]{1,0:T(8,128)(2,1)S(1)} %collective-permute-done.3.after_ref, bf16[27,640]{1,0:T(8,128)(2,1)S(1)} %copy-done.1), custom_call_target="tpu_custom_call" | custom-call | flops 8847360 | bytes 2097152 | tf_op jit(solution)/shard_map/convolve/pallas_call | solution.py:162
  105.9 3.9 %all-to-all-done.5 = f32[4,6,8,128]{3,2,1,0:T(8,128)S(1)} async-done(((f32[4,6,8,128]{3,2,1,0:T(8,128)}), f32[4,6,8,128]{3,2,1,0:T(8,128)S(1)}, u32[]{:S(2)}, u32[]{:S(2)}) %all-to-all-start.5) | async-done | bytes 98336 | tf_op jit(solution)/shard_map/all_to_all | solution.py:29
  109.7 1.3 %attend.1 = f32[256,640]{1,0:T(8,128)} custom-call(bf16[256,640]{1,0:T(8,128)(2,1)S(1)} %queries.1.query_ref, f32[24,8,128]{2,1,0:T(8,128)S(1)} %bitcast.12, f32[256,640]{1,0:T(8,128)S(1)} %convolve.1.local_ref), custom_call_target="tpu_custom_call" | custom-call | flops 167772160 | bytes 3145728 | tf_op jit(solution)/shard_map/attend/pallas_call | solution.py:201
  (13 shorter events, 0.2 us)
Async XLA Ops:
  1.5 30.1 %all-to-all-start = ((bf16[16,36,128]{2,1,0:T(8,128)(2,1)}), bf16[16,36,128]{2,1,0:T(8,128)(2,1)S(1)}, u32[]{:S(2)}, u32[]{:S(2)}) async-start(bf16[16,36,128]{2,1,0:T(8,128)(2,1)} %broadcast_in_dim.17), calls=%async_computation | async-start | bytes 327680 | tf_op jit(solution)/shard_map/all_to_all | solution.py:29
  16.7 1.1 copy-start
  17.8 0.7 copy-start.2
  18.7 13.0 %collective-permute-start = (bf16[256,1152]{1,0:T(8,128)(2,1)S(1)}, bf16[256,1152]{1,0:T(8,128)(2,1)S(1)}, u32[]{:S(2)}, u32[]{:S(2)}) collective-permute-start(bf16[256,1152]{1,0:T(8,128)(2,1)S(1)} %norm.1.tokens_ref), channel_id=1, source_target_pairs={{0,64},{64,0},{1,65},{65,1},{2,66},{66,2},{3,67},{67,3},{4,68},{68... | collective-permute-start | bytes 1769480 | tf_op jit(solution)/shard_map/ppermute | solution.py:222
  68.0 3.8 %collective-permute-start.1 = (bf16[256,1024]{1,0:T(8,128)(2,1)S(1)}, bf16[256,1024]{1,0:T(8,128)(2,1)S(1)}, u32[]{:S(2)}, u32[]{:S(2)}) collective-permute-start(bf16[256,1024]{1,0:T(8,128)(2,1)S(1)} %project.3), channel_id=1, source_target_pairs={{0,64},{64,0},{1,65},{65,1},{2,66},{66,2},{3,67},{67,3},{4,68},{68... | collective-permute-start | bytes 1572872 | tf_op jit(solution)/shard_map/ppermute | solution.py:222
  70.8 33.3 %copy-start.1 = (bf16[27,640]{1,0:T(8,128)(2,1)S(1)}, bf16[27,640]{1,0:T(8,128)(2,1)}, u32[]{:S(2)}) copy-start(bf16[27,640]{1,0:T(8,128)(2,1)} %weight_ref.1) | copy-start | bytes 103684
  81.8 18.2 %all-to-all-start.4 = ((bf16[16,24,128]{2,1,0:T(8,128)(2,1)}), bf16[16,24,128]{2,1,0:T(8,128)(2,1)S(1)}, u32[]{:S(2)}, u32[]{:S(2)}) async-start(bf16[16,24,128]{2,1,0:T(8,128)(2,1)} %broadcast_in_dim.39), calls=%async_computation.4 | async-start | bytes 196608 | tf_op jit(solution)/shard_map/all_to_all | solution.py:29
  87.1 17.0 %collective-permute-start.3 = (bf16[256,640]{1,0:T(8,128)(2,1)S(1)}, bf16[256,640]{1,0:T(8,128)(2,1)S(1)}, u32[]{:S(2)}, u32[]{:S(2)}) collective-permute-start(bf16[256,640]{1,0:T(8,128)(2,1)S(1)} %get-tuple-element.12.values_ref), channel_id=1, source_target_pairs={{1,0},{2,1},{3,2},{4,3},{5,4},{6,5},{7,6},{8,7},{9,8},{10,9},{11,1... | collective-permute-start | bytes 983048 | tf_op jit(solution)/shard_map/ppermute | solution.py:248
  89.1 15.0 %collective-permute-start.2 = (bf16[256,640]{1,0:T(8,128)(2,1)S(1)}, bf16[256,640]{1,0:T(8,128)(2,1)S(1)}, u32[]{:S(2)}, u32[]{:S(2)}) collective-permute-start(bf16[256,640]{1,0:T(8,128)(2,1)S(1)} %get-tuple-element.12.values_ref), channel_id=1, source_target_pairs={{0,1},{1,2},{2,3},{3,4},{4,5},{5,6},{6,7},{7,8},{8,9},{9,10},{10,1... | collective-permute-start | bytes 983048 | tf_op jit(solution)/shard_map/ppermute | solution.py:247
  100.7 9.1 %all-to-all-start.5 = ((f32[4,6,8,128]{3,2,1,0:T(8,128)}), f32[4,6,8,128]{3,2,1,0:T(8,128)S(1)}, u32[]{:S(2)}, u32[]{:S(2)}) async-start(f32[4,6,8,128]{3,2,1,0:T(8,128)} %broadcast_in_dim.41), calls=%async_computation.5 | async-start | bytes 196608 | tf_op jit(solution)/shard_map/all_to_all | solution.py:29
